TPU v7x, 32 devices: a whole 2x2x4 slice. The times are simulated.
32 devices in a mesh: seq: 4 (over y, x), head: 4 (over z), batch: 2 (over core).
Axes of the slice: x: 2, y: 2, z: 4, core: 2. Of those that a mesh axis runs over, the one named last changes fastest.
Arguments:
- queries: bfloat16 [16384, 1024], P(('batch', 'seq'), 'head'), parts along dimension 0, may hold values from -6 to 6
- keys: bfloat16 [16384, 1024], P(('batch', 'seq'), 'head'), parts along dimension 0, may hold values from -6 to 6
- values: bfloat16 [16384, 1024], P(('batch', 'seq'), 'head'), parts along dimension 0, may hold values from -6 to 6
- rand_blocks: int32 [256, 16, 3], P(('batch', 'seq'), 'head'), parts along dimension 0, may hold values from 0 to 127, as said below
- global_blocks: int32 [16], P(('batch', 'seq')), parts along dimension 0, may hold values from 0 to 127, as said below
Outputs:
- attended: bfloat16 [16384, 1024], P(('batch', 'seq'), 'head'), parts along dimension 0
There are 2 independent parts, one for each index of `batch`. A program takes and returns all parts, laid end to end along the dimension named above; each array names one. Nothing has to cross between parts.
Inputs may be any that keep to these rules, and one draw needn't show every extreme that they name: `rand_blocks`: over the 32 block rows of one device's range and one head, the random blocks that lie in any one device's range of 32 blocks are exactly 24 distinct blocks. `global_blocks`: entries 2i and 2i+1 are two distinct blocks of device i's range, from i * 32 to (i + 1) * 32 - 1.
All inputs are finite; a program needn't handle non-finite values.
Results may differ from a plain program's by a relative error of at most 0.0041.
Values may be sent and summed in bfloat16 or wider, within the bound.
No kernel may reach another device: no remote copies, remote signals or barrier semaphores. Data moves between devices by JAX's collectives and lax.ppermute only.
A program may use at most 192 MiB of HBM per device.

v0:
```python
import jax
import jax.numpy as jnp
from jax import lax
from jax.sharding import PartitionSpec as P

DH = 64
BLK = 64
RAND = 3


score_scale = 0.125


def with_halo(block, sides, width):
    for axis, dim in sides:
        count = lax.axis_size(axis)
        forward = [(i, i + 1) for i in range(count - 1)]
        forward.append((count - 1, 0))
        backward = [(target, source) for source, target in forward]
        low = lax.ppermute(
            lax.slice_in_dim(block, block.shape[dim] - width, None, axis=dim), axis, forward
        )
        high = lax.ppermute(lax.slice_in_dim(block, 0, width, axis=dim), axis, backward)
        block = jnp.concatenate([low, block, high], axis=dim)
    return block


def merged(array, axis, combine):
    everything = jax.tree.map(lambda part: lax.all_gather(part, axis), array)
    initial = jax.tree.map(lambda part: part[0], everything)

    def lap(k, so_far):
        return combine(so_far, jax.tree.map(lambda part: part[k], everything))

    return lax.fori_loop(1, lax.axis_size(axis), lap, initial)


def attend(query_blk, window_kv, random_kv, global_kv):
    rows = query_blk.shape[0]
    s_win = jnp.einsum(
        "rqd,rjkd->rqjk", query_blk, window_kv[..., :DH], preferred_element_type=jnp.float32
    ).reshape(rows, BLK, -1)
    s_rnd = jnp.einsum(
        "rqd,rjkd->rqjk", query_blk, random_kv[..., :DH], preferred_element_type=jnp.float32
    ).reshape(rows, BLK, -1)
    s_glb = jnp.einsum(
        "rqd,gkd->rqgk", query_blk, global_kv[..., :DH], preferred_element_type=jnp.float32
    ).reshape(rows, BLK, -1)
    scores = jnp.concatenate([s_win, s_rnd, s_glb], axis=-1) * score_scale
    peak = jnp.max(scores, axis=-1, keepdims=True)
    weights = jnp.exp(scores - peak)
    totals = jnp.sum(weights, axis=-1)
    probs = weights.astype(jnp.bfloat16)
    span = 3 * BLK
    p_win = probs[..., :span].reshape(rows, BLK, 3, BLK)
    p_rnd = probs[..., span : 2 * span].reshape(rows, BLK, 3, BLK)
    p_glb = probs[..., 2 * span :].reshape(rows, BLK, -1, BLK)
    summed = jnp.einsum(
        "rqjk,rjkd->rqd", p_win, window_kv[..., DH:], preferred_element_type=jnp.float32
    )
    summed = summed + jnp.einsum(
        "rqjk,rjkd->rqd", p_rnd, random_kv[..., DH:], preferred_element_type=jnp.float32
    )
    summed = summed + jnp.einsum(
        "rqgk,gkd->rqd", p_glb, global_kv[..., DH:], preferred_element_type=jnp.float32
    )
    return (summed / totals[..., None]).astype(jnp.bfloat16)


def take_blocks(source, positions):
    return jnp.take(source, positions.reshape(-1), axis=0).reshape(
        positions.shape + source.shape[1:]
    )


def blend(first, second):
    peak_a, total_a, sums_a = first
    peak_b, total_b, sums_b = second
    top = jnp.maximum(peak_a, peak_b)
    factor_a = jnp.exp(peak_a - top)
    factor_b = jnp.exp(peak_b - top)
    rows_shape = sums_a.shape
    expand_a = jnp.repeat(factor_a, rows_shape[-1] // factor_a.shape[-1], axis=-1)
    expand_b = jnp.repeat(factor_b, rows_shape[-1] // factor_b.shape[-1], axis=-1)
    return (top, total_a * factor_a + total_b * factor_b, sums_a * expand_a + sums_b * expand_b)


def shards(queries, keys, values, rand_blocks, global_blocks):
    tok_count, columns = queries.shape
    heads_here = columns // DH
    blocks_here = tok_count // BLK
    seq_rank = lax.axis_index("seq")
    q_heads = queries.reshape(blocks_here, BLK, heads_here, DH).transpose(2, 0, 1, 3)
    kv_heads = jnp.concatenate(
        [
            keys.reshape(blocks_here, BLK, heads_here, DH),
            values.reshape(blocks_here, BLK, heads_here, DH),
        ],
        axis=-1,
    ).transpose(2, 0, 1, 3)
    rand_heads = rand_blocks.transpose(1, 0, 2)
    widened = with_halo(kv_heads, (("seq", 1),), 1)
    local_glob = global_blocks - seq_rank * blocks_here
    glob_kv, glob_query = (
        lax.all_gather(kv_heads[:, local_glob], "seq", axis=1, tiled=True),
        lax.all_gather(q_heads[:, local_glob], "seq", axis=1, tiled=True),
    )
    start_kv = jnp.zeros((heads_here, blocks_here, RAND, BLK, 2 * DH), jnp.bfloat16)
    shard_rows = lax.all_gather(kv_heads, "seq", axis=1, tiled=True)
    count = shard_rows.shape[1]
    inside = (rand_heads >= 0) & (rand_heads < count)
    clipped = jnp.clip(rand_heads, 0, count - 1)
    picked = jax.vmap(take_blocks)(shard_rows, clipped)
    random_kv = jnp.where(inside[..., None, None], picked, start_kv)
    window_kv = jnp.stack(
        [
            widened[:, 0:blocks_here],
            widened[:, 1 : blocks_here + 1],
            widened[:, 2 : blocks_here + 2],
        ],
        axis=2,
    )
    group_size = min(blocks_here, 16)
    group_count = blocks_here // group_size

    def per_head(items):
        q_head, win_head, rnd_head, glob_head = items
        q_groups = q_head.reshape(group_count, group_size, BLK, DH)
        win_groups = win_head.reshape(group_count, group_size, 3, BLK, 2 * DH)
        rnd_groups = rnd_head.reshape(group_count, group_size, RAND, BLK, 2 * DH)
        result = lax.map(
            lambda group_items: attend(group_items[0], group_items[1], group_items[2], glob_head),
            (q_groups, win_groups, rnd_groups),
        )
        return result.reshape(blocks_here, BLK, DH)

    sparse = lax.map(per_head, (q_heads, window_kv, random_kv, glob_kv))
    glob_count = glob_query.shape[1]
    glob_flat = glob_query.reshape(heads_here, glob_count * BLK, DH)
    keys_local = kv_heads.reshape(heads_here, tok_count, 2 * DH)

    def row_partial(items):
        glob_rows, head_kv = items
        scores = (
            jnp.dot(glob_rows, head_kv[:, :DH].T, preferred_element_type=jnp.float32) * score_scale
        )
        peak = jnp.max(scores, axis=1)
        weights = jnp.exp(scores - peak[:, None])
        return (
            peak,
            jnp.sum(weights, axis=1),
            jnp.dot(
                weights.astype(jnp.bfloat16), head_kv[:, DH:], preferred_element_type=jnp.float32
            ),
        )

    part_peak, part_totals, part_sums = lax.map(row_partial, (glob_flat, keys_local))
    per_dev = global_blocks.shape[0]
    flat_peak = part_peak.reshape(heads_here, glob_count, BLK)
    flat_totals = part_totals.reshape(heads_here, glob_count, BLK)
    flat_sums = part_sums.reshape(heads_here, glob_count, BLK * DH)
    full_peak, full_totals, full_sums = merged((flat_peak, flat_totals, flat_sums), "seq", blend)
    mine_totals = lax.dynamic_slice_in_dim(full_totals, seq_rank * per_dev, per_dev, axis=1)
    mine_sums = lax.dynamic_slice_in_dim(full_sums, seq_rank * per_dev, per_dev, axis=1)
    mine_sums = mine_sums.reshape(heads_here, per_dev, BLK, DH)
    glob_out = (mine_sums / mine_totals[..., None]).astype(jnp.bfloat16)
    combined = sparse.at[:, local_glob].set(glob_out)
    return combined.transpose(1, 2, 0, 3).reshape(tok_count, heads_here * DH)


def solution(mesh):
    in_specs = (
        P(("batch", "seq"), "head"),
        P(("batch", "seq"), "head"),
        P(("batch", "seq"), "head"),
        P(("batch", "seq"), "head", None),
        P(("batch", "seq")),
    )
    out_specs = P(("batch", "seq"), "head")
    return jax.shard_map(shards, mesh=mesh, in_specs=in_specs, out_specs=out_specs, check_vma=False)
```

profile of v0, /device:TPU:0, one launch (start us, length us, event | category | flops | bytes accessed | tf_op | source)
XLA Modules:
  0.0 454.8 jit_solution(1142485364845724968)
XLA Ops:
  14.6 11.5 %all-gather.1 = bf16[4,8,64,64]{3,2,0,1:T(8,128)(2,1)S(1)} all-gather(bf16[4,2,64,64]{3,2,0,1:T(8,128)(2,1)S(1)} %bitcast.207), channel_id=3, replica_groups=mesh['seq'=4,'head'=4,'batch'=2] {'seq'}, dimensions={1}, use_global_device_ids=true | all-gather | bytes 327680 | tf_op jit(solution)/shard_map/all_gather | solution.py:106
  32.4 3.4 pad_maximum_fusion.3
  35.8 17.9 %while.55 = (s32[]{:T(128)}, f32[4,512]{1,0:T(4,128)S(1)}, f32[4,512]{1,0:T(4,128)S(1)}, f32[4,512,64]{1,2,0:T(8,128)}, bf16[4,512,64]{2,1,0:T(8,128)(2,1)}, /*i...) while((s32[]{:T(128)}, f32[4,512]{1,0:T(4,128)S(1)}, f32[4,512]{1,0:T(4,128)S(1)}, ...), condition=%wide.region_9.10_spmd, body=%wide.region_6.9_spmd.sunk | while | flops 276823040 | bytes 14959713 | solution.py:157
  64.2 8.7 %all_gather.22 = f32[4,4,8,64]{3,2,1,0:T(8,128)S(1)} all-gather(f32[1,4,8,64]{3,2,1,0:T(8,128)S(1)} %all_gather_reshape.10), channel_id=1, replica_groups=mesh['seq'=4,'head'=4,'batch'=2] {'seq'}, dimensions={0}, use_global_device_ids=true | all-gather | bytes 40960 | tf_op jit(solution)/shard_map/all_gather | solution.py:29
  72.9 7.2 %all_gather.21 = f32[4,4,8,64]{3,2,1,0:T(8,128)S(1)} all-gather(f32[1,4,8,64]{3,2,1,0:T(8,128)S(1)} %all_gather_reshape.9), channel_id=1, replica_groups=mesh['seq'=4,'head'=4,'batch'=2] {'seq'}, dimensions={0}, use_global_device_ids=true | all-gather | bytes 40960 | tf_op jit(solution)/shard_map/all_gather | solution.py:29
  80.1 14.9 %all-gather = bf16[4,8,64,128]{3,2,0,1:T(8,128)(2,1)} all-gather(bf16[4,2,64,128]{3,2,0,1:T(8,128)(2,1)S(1)} %bitcast.206), channel_id=2, replica_groups=mesh['seq'=4,'head'=4,'batch'=2] {'seq'}, dimensions={1}, use_global_device_ids=true | all-gather | bytes 655360 | tf_op jit(solution)/shard_map/all_gather | solution.py:105
  102.1 8.3 %while.56 = (s32[]{:T(128)}, f32[4,8,64]{2,1,0:T(8,128)S(1)}, f32[4,8,64]{2,1,0:T(8,128)S(1)}, f32[4,8,4096]{2,1,0:T(8,128)S(1)}, f32[4,4,8,64]{3,2,1,0:T(8,128)...) while((s32[]{:T(128)}, f32[4,8,64]{2,1,0:T(8,128)S(1)}, ...), condition=%wide.region_11.12_spmd, body=%wide.region_10.11_spmd.sunk | while | flops 405509 | bytes 5849239 | solution.py:35
  111.6 74.4 %all-gather.5.cloned.1.call-done = bf16[4,128,64,128]{3,2,1,0:T(8,128)(2,1)} async-done(((bf16[4,32,64,128]{3,2,1,0:T(8,128)(2,1)}), bf16[4,128,64,128]{3,2,1,0:T(8,128)(2,1)}) %all-gather.5.cloned.1.call-update) | async-done | bytes 8388624 | tf_op jit(solution)/shard_map/all_gather | solution.py:109
  185.9 7.8 %gather_fusion.2 = bf16[384,64,128]{2,1,0:T(8,128)(2,1)} fusion(bf16[4,128,64,128]{3,2,1,0:T(8,128)(2,1)} %all-gather.5.cloned.1.call-done, s32[384]{0:T(512)S(1)} %reshape.141), kind=kCustom, calls=%fused_computation.2 | custom fusion | bytes 12585984 | tf_op jit(solution)/shard_map/vmap(jit(_take))/gather | solution.py:71
  193.7 6.9 %select_select_fusion = bf16[4,32,3,64,128]{4,3,2,1,0:T(8,128)(2,1)} fusion(bf16[4,32,3,64,128]{4,3,2,1,0:T(8,128)(2,1)} %bitcast.201, pred[4,32,3]{2,1,0:T(8,128)(4,1)S(1)} %copy.109, pred[4,32,3]{2,1,0:T(8,128)(4,1)S(1)} %copy.108), kind=kLoop, calls=%fused_computation.71 | loop fusion | flops 6291456 | bytes 12583680 | tf_op jit(solution)/shard_map/jit(_where)/select_n | solution.py:114
  200.6 239.3 %while.54 = (s32[]{:T(128)}, bf16[4,32,64,64]{3,2,1,0:T(8,128)(2,1)}, bf16[4,32,64,64]{3,2,1,0:T(8,128)(2,1)}, bf16[4,32,3,64,128]{4,3,1,0,2:T(8,128)(2,1)}, bf1...) while((s32[]{:T(128)}, ...), condition=%wide.region_5.6_spmd, body=%wide.region_0.5_spmd.sunk | while | flops 240649088 | bytes 63646092 | solution.py:137
  209.0 49.6 %while.57 = (s32[]{:T(128)}, bf16[2,16,64,64]{3,2,1,0:T(8,128)(2,1)}, bf16[2,16,64,64]{3,2,1,0:T(8,128)(2,1)}, bf16[2,16,3,64,128]{4,3,2,1,0:T(8,128)(2,1)}, bf1...) while((s32[]{:T(128)}, bf16[2,16,64,64]{3,2,1,0:T(8,128)(2,1)}, ...), condition=%wide.region_4.4_spmd, body=%wide.region_1.3_spmd.sunk | while | flops 240649088 | bytes 52373216 | solution.py:131
  217.0 5.8 %fusion.123 = (f32[16,64]{1,0:T(8,128)S(1)}, bf16[16,64,896]{2,1,0:T(8,128)(2,1)S(1)}) fusion(f32[16,64,512]{2,1,0:T(8,128)S(1)} %fusion.120, f32[16,64,192]{2,1,0:T(8,128)S(1)} %copy-done.3, f32[16,64,192]{2,1,0:T(8,128)S(1)} %copy-done.4), kind=kOutput, calls=%fused_computation.95.clone.1 | output fusion | flops 5505919 | bytes 5509120 | tf_op jit(solution)/shard_map/while/body/eval_jaxpr/while/body/eval_jaxpr/sub | solution.py:51
  241.8 5.8 %fusion.123 = (f32[16,64]{1,0:T(8,128)S(1)}, bf16[16,64,896]{2,1,0:T(8,128)(2,1)S(1)}) fusion(f32[16,64,512]{2,1,0:T(8,128)S(1)} %fusion.120, f32[16,64,192]{2,1,0:T(8,128)S(1)} %copy-done.3, f32[16,64,192]{2,1,0:T(8,128)S(1)} %copy-done.4), kind=kOutput, calls=%fused_computation.95.clone.1 | output fusion | flops 5505919 | bytes 5509120 | tf_op jit(solution)/shard_map/while/body/eval_jaxpr/while/body/eval_jaxpr/sub | solution.py:51
  268.8 49.6 %while.57 = (s32[]{:T(128)}, bf16[2,16,64,64]{3,2,1,0:T(8,128)(2,1)}, bf16[2,16,64,64]{3,2,1,0:T(8,128)(2,1)}, bf16[2,16,3,64,128]{4,3,2,1,0:T(8,128)(2,1)}, bf1...) while((s32[]{:T(128)}, bf16[2,16,64,64]{3,2,1,0:T(8,128)(2,1)}, ...), condition=%wide.region_4.4_spmd, body=%wide.region_1.3_spmd.sunk | while | flops 240649088 | bytes 52373216 | solution.py:131
  276.8 5.8 %fusion.123 = (f32[16,64]{1,0:T(8,128)S(1)}, bf16[16,64,896]{2,1,0:T(8,128)(2,1)S(1)}) fusion(f32[16,64,512]{2,1,0:T(8,128)S(1)} %fusion.120, f32[16,64,192]{2,1,0:T(8,128)S(1)} %copy-done.3, f32[16,64,192]{2,1,0:T(8,128)S(1)} %copy-done.4), kind=kOutput, calls=%fused_computation.95.clone.1 | output fusion | flops 5505919 | bytes 5509120 | tf_op jit(solution)/shard_map/while/body/eval_jaxpr/while/body/eval_jaxpr/sub | solution.py:51
  301.6 5.8 %fusion.123 = (f32[16,64]{1,0:T(8,128)S(1)}, bf16[16,64,896]{2,1,0:T(8,128)(2,1)S(1)}) fusion(f32[16,64,512]{2,1,0:T(8,128)S(1)} %fusion.120, f32[16,64,192]{2,1,0:T(8,128)S(1)} %copy-done.3, f32[16,64,192]{2,1,0:T(8,128)S(1)} %copy-done.4), kind=kOutput, calls=%fused_computation.95.clone.1 | output fusion | flops 5505919 | bytes 5509120 | tf_op jit(solution)/shard_map/while/body/eval_jaxpr/while/body/eval_jaxpr/sub | solution.py:51
  328.6 49.6 %while.57 = (s32[]{:T(128)}, bf16[2,16,64,64]{3,2,1,0:T(8,128)(2,1)}, bf16[2,16,64,64]{3,2,1,0:T(8,128)(2,1)}, bf16[2,16,3,64,128]{4,3,2,1,0:T(8,128)(2,1)}, bf1...) while((s32[]{:T(128)}, bf16[2,16,64,64]{3,2,1,0:T(8,128)(2,1)}, ...), condition=%wide.region_4.4_spmd, body=%wide.region_1.3_spmd.sunk | while | flops 240649088 | bytes 52373216 | solution.py:131
  336.6 5.8 %fusion.123 = (f32[16,64]{1,0:T(8,128)S(1)}, bf16[16,64,896]{2,1,0:T(8,128)(2,1)S(1)}) fusion(f32[16,64,512]{2,1,0:T(8,128)S(1)} %fusion.120, f32[16,64,192]{2,1,0:T(8,128)S(1)} %copy-done.3, f32[16,64,192]{2,1,0:T(8,128)S(1)} %copy-done.4), kind=kOutput, calls=%fused_computation.95.clone.1 | output fusion | flops 5505919 | bytes 5509120 | tf_op jit(solution)/shard_map/while/body/eval_jaxpr/while/body/eval_jaxpr/sub | solution.py:51
  361.4 5.8 %fusion.123 = (f32[16,64]{1,0:T(8,128)S(1)}, bf16[16,64,896]{2,1,0:T(8,128)(2,1)S(1)}) fusion(f32[16,64,512]{2,1,0:T(8,128)S(1)} %fusion.120, f32[16,64,192]{2,1,0:T(8,128)S(1)} %copy-done.3, f32[16,64,192]{2,1,0:T(8,128)S(1)} %copy-done.4), kind=kOutput, calls=%fused_computation.95.clone.1 | output fusion | flops 5505919 | bytes 5509120 | tf_op jit(solution)/shard_map/while/body/eval_jaxpr/while/body/eval_jaxpr/sub | solution.py:51
  388.4 49.6 %while.57 = (s32[]{:T(128)}, bf16[2,16,64,64]{3,2,1,0:T(8,128)(2,1)}, bf16[2,16,64,64]{3,2,1,0:T(8,128)(2,1)}, bf16[2,16,3,64,128]{4,3,2,1,0:T(8,128)(2,1)}, bf1...) while((s32[]{:T(128)}, bf16[2,16,64,64]{3,2,1,0:T(8,128)(2,1)}, ...), condition=%wide.region_4.4_spmd, body=%wide.region_1.3_spmd.sunk | while | flops 240649088 | bytes 52373216 | solution.py:131
  396.5 5.8 %fusion.123 = (f32[16,64]{1,0:T(8,128)S(1)}, bf16[16,64,896]{2,1,0:T(8,128)(2,1)S(1)}) fusion(f32[16,64,512]{2,1,0:T(8,128)S(1)} %fusion.120, f32[16,64,192]{2,1,0:T(8,128)S(1)} %copy-done.3, f32[16,64,192]{2,1,0:T(8,128)S(1)} %copy-done.4), kind=kOutput, calls=%fused_computation.95.clone.1 | output fusion | flops 5505919 | bytes 5509120 | tf_op jit(solution)/shard_map/while/body/eval_jaxpr/while/body/eval_jaxpr/sub | solution.py:51
  421.3 5.8 %fusion.123 = (f32[16,64]{1,0:T(8,128)S(1)}, bf16[16,64,896]{2,1,0:T(8,128)(2,1)S(1)}) fusion(f32[16,64,512]{2,1,0:T(8,128)S(1)} %fusion.120, f32[16,64,192]{2,1,0:T(8,128)S(1)} %copy-done.3, f32[16,64,192]{2,1,0:T(8,128)S(1)} %copy-done.4), kind=kOutput, calls=%fused_computation.95.clone.1 | output fusion | flops 5505919 | bytes 5509120 | tf_op jit(solution)/shard_map/while/body/eval_jaxpr/while/body/eval_jaxpr/sub | solution.py:51
  442.2 3.6 copy.135
  (326 shorter events, 255.7 us)
Async XLA Ops:
  6.5 94.5 %all-gather.7.cloned.1.call-start = ((), (), s32[]{:S(2)}) async-start(), calls=%async_computation.1 | async-start | bytes 2621440 | tf_op jit(solution)/shard_map/all_gather | solution.py:29
  7.2 5.3 %copy-start.10 = (s32[2]{0:T(128)}, s32[2]{0:T(128)S(1)}, u32[]{:S(2)}) copy-start(s32[2]{0:T(128)S(1)} %compare_select_fusion.2) | copy-start | bytes 28
  10.5 16.4 %copy-start.7 = (bf16[2048,256]{1,0:T(8,128)(2,1)S(1)}, bf16[2048,256]{1,0:T(8,128)(2,1)}, u32[]{:S(2)}) copy-start(bf16[2048,256]{1,0:T(8,128)(2,1)} %param.14) | copy-start | bytes 3145732
  27.8 1.9 copy-start.8
  53.7 3.0 copy-start.5
  55.5 8.1 %copy-start.9 = (s32[32,4,3]{0,1,2:T(4,128)S(1)}, s32[32,4,3]{0,1,2:T(4,128)}, u32[]{:S(2)}) copy-start(s32[32,4,3]{0,1,2:T(4,128)} %param.16) | copy-start | bytes 4612
  56.7 129.3 %all-gather.5.cloned.1.call-start = ((), (), s32[]{:S(2)}) async-start(), calls=%async_computation | async-start | bytes 10485760 | tf_op jit(solution)/shard_map/all_gather | solution.py:109
  58.3 36.7 %collective-permute-start = (bf16[4,1,64,128]{3,2,1,0:T(8,128)(2,1)S(1)}, bf16[4,1,64,128]{3,2,1,0:T(8,128)(2,1)S(1)}, u32[]{:S(2)}, u32[]{:S(2)}) collective-permute-start(bf16[4,1,64,128]{3,2,1,0:T(8,128)(2,1)S(1)} %get-tuple-element.393), channel_id=1, source_target_pairs={{0,8},{8,16},{16,24},{24,0},{1,9},{9,17},{17,25},{25,1},{2,10},{10... | collective-permute-start | bytes 196616 | tf_op jit(solution)/shard_map/ppermute | solution.py:20
  59.8 35.2 %collective-permute-start.1 = (bf16[4,1,64,128]{3,2,1,0:T(8,128)(2,1)S(1)}, bf16[4,1,64,128]{3,2,1,0:T(8,128)(2,1)S(1)}, u32[]{:S(2)}, u32[]{:S(2)}) collective-permute-start(bf16[4,1,64,128]{3,2,1,0:T(8,128)(2,1)S(1)} %get-tuple-element.394), channel_id=1, source_target_pairs={{8,0},{16,8},{24,16},{0,24},{9,1},{17,9},{25,17},{1,25},{10,2},{18... | collective-permute-start | bytes 196616 | tf_op jit(solution)/shard_map/ppermute | solution.py:23
  95.0 2.8 copy-start.6
  200.6 239.4 %copy-start.11 = (s32[2]{0:T(128)S(1)}, s32[2]{0:T(128)}, u32[]{:S(2)}) copy-start(s32[2]{0:T(128)} %copy-done.10) | copy-start | bytes 28
  215.4 1.6 copy-start.4
  226.1 4.1 copy-start.1
  240.2 1.6 copy-start.4
  250.9 4.1 copy-start.1
  275.2 1.6 copy-start.4
  285.9 4.1 copy-start.1
  300.0 1.6 copy-start.4
  310.7 4.1 copy-start.1
  335.0 1.6 copy-start.4
  345.7 4.1 copy-start.1
  370.5 4.1 copy-start.1
  405.6 4.1 copy-start.1
  430.4 4.1 copy-start.1
  (27 other events, 41.0 us)
Sparse Core Ops, SparseCore 0:
  56.8 39.5 all-gather.6
  98.3 87.6 all-gather.4
where the time goes:
time: 458 us; the launch traced here: 455 us
  local copies, waits for them, and re-layouts  158 us (34%)
  matrix products  90.8 us (20%)
  waiting for transfers between devices  75.1 us (16%)
  other arithmetic  70.6 us (15%)
  blocking collectives  42.2 us (9%)
  between operations  13.6 us (3%)
    all_gather x1, waiting for transfers between devices, shards(): shard_rows = lax.all_gather(kv_heads, 'seq', axis=1, tiled=True)  74.4 us
    sub x8, other arithmetic, attend(): weights = jnp.exp(scores - peak)  46.2 us
    dynamic_slice x16, local copies, waits for them, and re-layouts, shards(): sparse = lax.map(per_head, (q_heads, window_kv, random_kv, glob_kv))  29.6 us
    slice x16, local copies, waits for them, and re-layouts, attend(): p_win = probs[..., :span].reshape(rows, BLK, 3, BLK)  21.8 us
    dot_general x8, matrix products, attend(): jnp.einsum('rqjk,rjkd->rqd', p_win, window_kv[..., DH:], preferred_elemen...  20.3 us
    dot_general x8, matrix products, attend(): jnp.einsum('rqgk,gkd->rqd', p_glb, global_kv[..., DH:], preferred_element...  19 us
    all_gather x2, blocking collectives, merged(): everything = jax.tree.map(lambda part: lax.all_gather(part, axis), array)  15.9 us
    all_gather x1, blocking collectives, shards(): lax.all_gather(kv_heads[:, local_glob], 'seq', axis=1, tiled=True)  14.9 us
  transfers between devices with their start and end apart: 4, of which 1 were waited for; matrix products, arithmetic and copies ran while one was open for 4% of the time, Pallas kernels for 0%

commit v1 on v0

v1 whole, which is shorter than its diff:
```python
import functools

import jax
import jax.numpy as jnp
from jax import lax
from jax.experimental import pallas as pl
from jax.experimental.pallas import tpu as pltpu
from jax.sharding import PartitionSpec as P

DH = 64
BLK = 64
RAND = 3
LANES = 2 * DH
ROWS = 2
CHUNK = 512
EXP2_SCALE = 0.125 * 1.4426950408889634


def qk(q, k):
    return lax.dot_general(q, k, (((1,), (1,)), ((), ())), preferred_element_type=jnp.float32)


def pv(p, v):
    return jnp.dot(p.astype(jnp.bfloat16), v, preferred_element_type=jnp.float32)


def pair_kernel(
    pair, ranges, gpd, tokens, rand_ref, win_ref, glob_ref, own_ref, q_ref, *refs
):
    k_refs, v_refs, refs = refs[:ranges], refs[ranges : 2 * ranges], refs[2 * ranges :]
    if pair > 0:
        refs = refs[1:]
    out_ref, k_all, v_all, k_glob, v_glob, sems = refs
    blocks = tokens // BLK
    globs = gpd * ranges

    def view(ref, j):
        return ref.at[:, pl.ds(pair * LANES, LANES)] if j == 0 else ref

    copies = []
    for j in range(ranges):
        span = pl.ds(j * tokens, tokens)
        copies.append(pltpu.make_async_copy(view(k_refs[j], j), k_all.at[span], sems.at[2 * j]))
        copies.append(pltpu.make_async_copy(view(v_refs[j], j), v_all.at[span], sems.at[2 * j + 1]))
    for copy in copies:
        copy.start()
    for copy in copies:
        copy.wait()

    first = lax.broadcasted_iota(jnp.int32, (BLK, LANES), 1) < DH

    def split_heads(q):
        zero = jnp.zeros_like(q)
        return [jnp.where(first, q, zero), jnp.where(first, zero, q)]

    def block(ref, position):
        return ref[pl.ds(pl.multiple_of(position * BLK, BLK), BLK), :]

    def finish(summed, totals):
        o = summed * (1.0 / totals)
        return jnp.where(first, o[:BLK], o[BLK:]).astype(jnp.bfloat16)

    for g in range(globs):
        k_glob[g * BLK : (g + 1) * BLK, :] = block(k_all, glob_ref[g])
        v_glob[g * BLK : (g + 1) * BLK, :] = block(v_all, glob_ref[g])

    def rows_step(step, carry):
        base = step * ROWS
        q_bd, listed = [], []
        for u in range(ROWS):
            b = base + u
            q_bd += split_heads(block(q_ref, b))
            k_list, v_list = [], []
            for j in range(3):
                k_list.append(block(k_all, win_ref[b + j]))
                v_list.append(block(v_all, win_ref[b + j]))
            for j in range(RAND):
                at_a = rand_ref[b * 2 * RAND + j]
                at_b = rand_ref[b * 2 * RAND + RAND + j]
                k_list.append(jnp.where(first, block(k_all, at_a), block(k_all, at_b)))
                v_list.append(jnp.where(first, block(v_all, at_a), block(v_all, at_b)))
            listed.append((jnp.concatenate(k_list, axis=0), jnp.concatenate(v_list, axis=0)))
        q_bd = jnp.concatenate(q_bd, axis=0)
        s_own = jnp.concatenate(
            [qk(q_bd[2 * BLK * u : 2 * BLK * (u + 1)], listed[u][0]) for u in range(ROWS)], axis=0
        )
        s_glob = qk(q_bd, k_glob[...])
        peak = jnp.maximum(
            jnp.max(s_own, axis=1, keepdims=True), jnp.max(s_glob, axis=1, keepdims=True)
        )
        w_own = jnp.exp2((s_own - peak) * EXP2_SCALE)
        w_glob = jnp.exp2((s_glob - peak) * EXP2_SCALE)
        totals = jnp.sum(w_own, axis=1, keepdims=True) + jnp.sum(w_glob, axis=1, keepdims=True)
        o_glob = pv(w_glob, v_glob[...])
        for u in range(ROWS):
            part = slice(2 * BLK * u, 2 * BLK * (u + 1))
            o = o_glob[part] + pv(w_own[part], listed[u][1])
            where = pl.ds(pl.multiple_of((base + u) * BLK, BLK), BLK)
            out_ref[where, :] = finish(o, totals[part])
        return carry

    lax.fori_loop(0, blocks // ROWS, rows_step, 0)

    q_glob = []
    for g in range(gpd):
        q_glob += split_heads(block(q_ref, own_ref[g]))
    q_glob = jnp.concatenate(q_glob, axis=0)

    def chunk_step(c, carry):
        peak, totals, summed = carry
        span = pl.ds(pl.multiple_of(c * CHUNK, CHUNK), CHUNK)
        s = qk(q_glob, k_all[span, :])
        top = jnp.maximum(peak, jnp.max(s, axis=1, keepdims=True))
        factor = jnp.exp2((peak - top) * EXP2_SCALE)
        w = jnp.exp2((s - top) * EXP2_SCALE)
        totals = totals * factor + jnp.sum(w, axis=1, keepdims=True)
        summed = summed * factor + pv(w, v_all[span, :])
        return top, totals, summed

    height = 2 * gpd * BLK
    initial = (
        jnp.full((height, 1), -1e30, jnp.float32),
        jnp.zeros((height, 1), jnp.float32),
        jnp.zeros((height, LANES), jnp.float32),
    )
    _, totals, summed = lax.fori_loop(0, ranges * tokens // CHUNK, chunk_step, initial)
    for g in range(gpd):
        part = slice(2 * BLK * g, 2 * BLK * (g + 1))
        where = pl.ds(pl.multiple_of(own_ref[g] * BLK, BLK), BLK)
        out_ref[where, :] = finish(summed[part], totals[part])


def pair_call(pair, rand, win, glob, own, queries, k_parts, v_parts, so_far):
    tokens, columns = queries.shape
    ranges = len(k_parts)
    gpd = own.shape[0]
    smem = pl.BlockSpec(memory_space=pltpu.SMEM)
    hbm = pl.BlockSpec(memory_space=pl.ANY)
    half = pl.BlockSpec((tokens, LANES), lambda i: (0, pair))
    operands = [rand, win, glob, own, queries, *k_parts, *v_parts]
    in_specs = [smem] * 4 + [half] + [hbm] * (2 * ranges)
    aliases = {}
    if so_far is not None:
        aliases = {len(operands): 0}
        operands.append(so_far)
        in_specs.append(hbm)
    keys_all = ranges * tokens
    pairs_done = 2 * tokens * (6 + gpd * ranges) * BLK + 2 * gpd * BLK * keys_all
    return pl.pallas_call(
        functools.partial(pair_kernel, pair, ranges, gpd, tokens),
        grid=(1,),
        in_specs=in_specs,
        out_specs=half,
        out_shape=jax.ShapeDtypeStruct((tokens, columns), jnp.bfloat16),
        input_output_aliases=aliases,
        scratch_shapes=[
            pltpu.VMEM((keys_all, LANES), jnp.bfloat16),
            pltpu.VMEM((keys_all, LANES), jnp.bfloat16),
            pltpu.VMEM((gpd * ranges * BLK, LANES), jnp.bfloat16),
            pltpu.VMEM((gpd * ranges * BLK, LANES), jnp.bfloat16),
            pltpu.SemaphoreType.DMA((2 * ranges,)),
        ],
        compiler_params=pltpu.CompilerParams(vmem_limit_bytes=48 * 1024 * 1024),
        cost_estimate=pl.CostEstimate(
            flops=8 * DH * pairs_done, bytes_accessed=4 * keys_all * LANES, transcendentals=pairs_done
        ),
        name="pair",
    )(*operands)


def exchange(array, step):
    count = lax.axis_size("seq")
    return lax.ppermute(array, "seq", [(i, i ^ step) for i in range(count)])


def gathered(array, steps):
    parts = {0: array}
    for step in steps:
        parts.update({at ^ step: exchange(part, step) for at, part in list(parts.items())})
    return [parts[at] for at in range(len(parts))]


def shards(queries, keys, values, rand_blocks, global_blocks):
    tokens, columns = queries.shape
    blocks = tokens // BLK
    count = lax.axis_size("seq")
    rank = lax.axis_index("seq")
    pairs = columns // LANES
    steps = [1 << i for i in range(count.bit_length() - 1)]

    def place(ids):
        return ((ids // blocks) ^ rank) * blocks + ids % blocks

    k_all, v_all = [], []
    for pair in range(pairs):
        lanes = slice(pair * LANES, (pair + 1) * LANES)
        k_all.append(gathered(keys[:, lanes], steps))
        v_all.append(gathered(values[:, lanes], steps[::-1]))
        k_all[pair][0] = keys
        v_all[pair][0] = values
    glob = place(jnp.concatenate(gathered(global_blocks, steps)))
    own = global_blocks - rank * blocks
    win = place((rank * blocks - 1 + jnp.arange(blocks + 2)) % (count * blocks))
    rand = place(rand_blocks)
    out = None
    for pair in range(pairs):
        mine = rand[:, 2 * pair : 2 * pair + 2].reshape(-1)
        out = pair_call(pair, mine, win, glob, own, queries, k_all[pair], v_all[pair], out)
    return out


def solution(mesh):
    in_specs = (
        P(("batch", "seq"), "head"),
        P(("batch", "seq"), "head"),
        P(("batch", "seq"), "head"),
        P(("batch", "seq"), "head", None),
        P(("batch", "seq")),
    )
    out_specs = P(("batch", "seq"), "head")
    return jax.shard_map(shards, mesh=mesh, in_specs=in_specs, out_specs=out_specs, check_vma=False)
```

time: 458 us -> 107 us (0.23)
  local copies, waits for them, and re-layouts: 158 us -> 3.9 us
  matrix products: 90.8 us -> 0 us
  other arithmetic: 70.6 us -> 0.13 us
  Pallas kernels: 0 us -> 42.8 us
  blocking collectives: 42.2 us -> 0 us
  waiting for transfers between devices: 75.1 us -> 40.1 us
  starting transfers between devices: 3.02 us -> 19.7 us
  between operations: 13.6 us -> 0.1 us
    dot_general x56 -> x0, matrix products: 90.8 us -> none  [the longest x8 20.3 us: attend(): jnp.einsum('rqjk,rjkd->rqd', p_win, window_kv[..., DH:], preferred_elemen...]
    all_gather x2 -> x0, waiting for transfers between devices: 74.4 us -> none  [the longest x1 74.4 us: shards(): shard_rows = lax.all_gather(kv_heads, 'seq', axis=1, tiled=True)]
    reshape x40 -> x2, local copies, waits for them, and re-layouts: 52.8 us -> 0.29 us  [shards(): mine = rand[:, 2 * pair:2 * pair + 2].reshape(-1)]
    sub x8 -> x1, other arithmetic: 46.2 us -> 0.01 us  [shards(): own = global_blocks - rank * blocks]
    pallas_call x0 -> x2, Pallas kernels: none -> 42.8 us  [pair_call(): pl.pallas_call(functools.partial(pair_kernel, pair, ranges, gpd, tokens),...]
    all_gather x4 -> x0, blocking collectives: 42.2 us -> none  [the longest x2 15.9 us: merged(): everything = jax.tree.map(lambda part: lax.all_gather(part, axis), array)]
    ppermute x2 -> x15, waiting for transfers between devices: 0.01 us -> 40.1 us  [exchange(): return lax.ppermute(array, 'seq', [(i, i ^ step) for i in range(count)])]
    dynamic_slice x18 -> x0, local copies, waits for them, and re-layouts: 29.6 us -> none  [the longest x16 29.6 us: shards(): sparse = lax.map(per_head, (q_heads, window_kv, random_kv, glob_kv))]
  transfers between devices with their start and end apart: 4 -> 15, of which waited for: 1 -> 5; matrix products, arithmetic and copies ran while one was open for 4% -> 2% of each run, Pallas kernels for 0% -> 20%
where the time goes in v1:
time: 107 us
  Pallas kernels  42.8 us (40%)
  waiting for transfers between devices  40.1 us (37%)
  starting transfers between devices  19.7 us (18%)
  local copies, waits for them, and re-layouts  3.9 us (4%)
    pallas_call x2, Pallas kernels, pair_call(): pl.pallas_call(functools.partial(pair_kernel, pair, ranges, gpd, tokens),...  42.8 us
    ppermute x15, waiting for transfers between devices, exchange(): return lax.ppermute(array, 'seq', [(i, i ^ step) for i in range(count)])  40.1 us
    ppermute x15, starting transfers between devices, exchange(): return lax.ppermute(array, 'seq', [(i, i ^ step) for i in range(count)])  19.7 us
    slice x1, local copies, waits for them, and re-layouts, shards(): k_all.append(gathered(keys[:, lanes], steps))  2.34 us
  transfers between devices with their start and end apart: 15, of which 5 were waited for; matrix products, arithmetic and copies ran while one was open for 2% of the time, Pallas kernels for 20%

profile of v1, /device:TPU:0, one launch (start us, length us, event | category | flops | bytes accessed | tf_op | source)
XLA Modules:
  0.0 106.7 jit_solution(7381775081279244184)
XLA Ops:
  0.0 2.3 %fusion.9 = (bf16[2048,128]{1,0:T(8,128)(2,1)}, bf16[2048,128]{1,0:T(8,128)(2,1)}) fusion(bf16[2048,256]{1,0:T(8,128)(2,1)} %refs_0_.3), kind=kLoop, calls=%fused_computation.30 | loop fusion | bytes 2097152 | tf_op jit(solution)/shard_map/slice | solution.py:197
  2.3 2.9 %collective-permute-start.9 = (bf16[2048,128]{1,0:T(8,128)(2,1)}, bf16[2048,128]{1,0:T(8,128)(2,1)S(1)}, u32[]{:S(2)}, u32[]{:S(2)}) collective-permute-start(bf16[2048,128]{1,0:T(8,128)(2,1)} %get-tuple-element.7), channel_id=1, source_target_pairs={{0,8},{8,0},{16,24},{24,16},{1,9},{9,1},{17,25},{25,17},{2,10},{10... | collective-permute-start | bytes 1572872 | tf_op jit(solution)/shard_map/ppermute | solution.py:173
  5.3 1.1 fusion.8
  6.3 1.5 %collective-permute-start.13 = (bf16[2048,128]{1,0:T(8,128)(2,1)}, bf16[2048,128]{1,0:T(8,128)(2,1)S(1)}, u32[]{:S(2)}, u32[]{:S(2)}) collective-permute-start(bf16[2048,128]{1,0:T(8,128)(2,1)} %get-tuple-element.5), channel_id=1, source_target_pairs={{0,16},{8,24},{16,0},{24,8},{1,17},{9,25},{17,1},{25,9},{2,18},{10... | collective-permute-start | bytes 1572872 | tf_op jit(solution)/shard_map/ppermute | solution.py:173
  7.9 0.5 collective-permute-start.10
  8.5 2.0 %collective-permute-start.1 = (s32[2]{0:T(128)S(1)}, s32[2]{0:T(128)S(1)}, u32[]{:S(2)}, u32[]{:S(2)}) collective-permute-start(s32[2]{0:T(128)S(1)} %copy-done.4), channel_id=1, source_target_pairs={{0,16},{8,24},{16,0},{24,8},{1,17},{9,25},{17,1},{25,9},{2,18},{10... | collective-permute-start | bytes 32 | tf_op jit(solution)/shard_map/ppermute | solution.py:173
  10.4 7.1 %collective-permute-done = s32[2]{0:T(128)S(1)} collective-permute-done((s32[2]{0:T(128)S(1)}, s32[2]{0:T(128)S(1)}, u32[]{:S(2)}, u32[]{:S(2)}) %collective-permute-start) | collective-permute-done | bytes 40 | tf_op jit(solution)/shard_map/ppermute | solution.py:173
  17.5 1.7 %collective-permute-start.12 = (bf16[2048,128]{1,0:T(8,128)(2,1)}, bf16[2048,128]{1,0:T(8,128)(2,1)}, u32[]{:S(2)}, u32[]{:S(2)}) collective-permute-start(bf16[2048,128]{1,0:T(8,128)(2,1)} %get-tuple-element.5), channel_id=1, source_target_pairs={{0,8},{8,0},{16,24},{24,16},{1,9},{9,1},{17,25},{25,17},{2,10},{10... | collective-permute-start | bytes 1572872 | tf_op jit(solution)/shard_map/ppermute | solution.py:173
  19.2 12.1 %collective-permute-done.1 = s32[2]{0:T(128)S(1)} collective-permute-done((s32[2]{0:T(128)S(1)}, s32[2]{0:T(128)S(1)}, u32[]{:S(2)}, u32[]{:S(2)}) %collective-permute-start.1) | collective-permute-done | bytes 40 | tf_op jit(solution)/shard_map/ppermute | solution.py:173
  31.3 1.5 %collective-permute-start.2 = (s32[2]{0:T(128)S(1)}, s32[2]{0:T(128)S(1)}, u32[]{:S(2)}, u32[]{:S(2)}) collective-permute-start(s32[2]{0:T(128)S(1)} %collective-permute-done), channel_id=1, source_target_pairs={{0,16},{8,24},{16,0},{24,8},{1,17},{9,25},{17,1},{25,9},{2,18},{10... | collective-permute-start | bytes 32 | tf_op jit(solution)/shard_map/ppermute | solution.py:173
  32.8 2.0 %collective-permute-done.2 = s32[2]{0:T(128)S(1)} collective-permute-done((s32[2]{0:T(128)S(1)}, s32[2]{0:T(128)S(1)}, u32[]{:S(2)}, u32[]{:S(2)}) %collective-permute-start.2) | collective-permute-done | bytes 40 | tf_op jit(solution)/shard_map/ppermute | solution.py:173
  34.8 0.3 collective-permute-start.3
  35.1 1.7 %collective-permute-start.7 = (bf16[2048,128]{1,0:T(8,128)(2,1)}, bf16[2048,128]{1,0:T(8,128)(2,1)}, u32[]{:S(2)}, u32[]{:S(2)}) collective-permute-start(bf16[2048,128]{1,0:T(8,128)(2,1)} %get-tuple-element.6), channel_id=1, source_target_pairs={{0,16},{8,24},{16,0},{24,8},{1,17},{9,25},{17,1},{25,9},{2,18},{10... | collective-permute-start | bytes 1572872 | tf_op jit(solution)/shard_map/ppermute | solution.py:173
  36.9 0.3 collective-permute-start.11
  37.2 1.8 %collective-permute-start.14 = (bf16[2048,128]{1,0:T(8,128)(2,1)S(1)}, bf16[2048,128]{1,0:T(8,128)(2,1)}, u32[]{:S(2)}, u32[]{:S(2)}) collective-permute-start(bf16[2048,128]{1,0:T(8,128)(2,1)S(1)} %collective-permute-done.13.refs_6_), channel_id=1, source_target_pairs={{0,8},{8,0},{16,24},{24,16},{1,9},{9,1},{17,25},{25,17},{2,10},{10... | collective-permute-start | bytes 1572872 | tf_op jit(solution)/shard_map/ppermute | solution.py:173
  39.0 1.5 %collective-permute-start.4 = (bf16[2048,128]{1,0:T(8,128)(2,1)}, bf16[2048,128]{1,0:T(8,128)(2,1)}, u32[]{:S(2)}, u32[]{:S(2)}) collective-permute-start(bf16[2048,128]{1,0:T(8,128)(2,1)} %get-tuple-element.8), channel_id=1, source_target_pairs={{0,16},{8,24},{16,0},{24,8},{1,17},{9,25},{17,1},{25,9},{2,18},{10... | collective-permute-start | bytes 1572872 | tf_op jit(solution)/shard_map/ppermute | solution.py:173
  40.5 9.5 %collective-permute-done.3.refs_1_ = bf16[2048,128]{1,0:T(8,128)(2,1)} collective-permute-done((bf16[2048,128]{1,0:T(8,128)(2,1)}, bf16[2048,128]{1,0:T(8,128)(2,1)}, u32[]{:S(2)}, u32[]{:S(2)}) %collective-permute-start.3) | collective-permute-done | bytes 524320 | tf_op jit(solution)/shard_map/ppermute | solution.py:173
  50.0 0.3 collective-permute-start.6
  50.3 1.7 %collective-permute-start.5 = (bf16[2048,128]{1,0:T(8,128)(2,1)}, bf16[2048,128]{1,0:T(8,128)(2,1)}, u32[]{:S(2)}, u32[]{:S(2)}) collective-permute-start(bf16[2048,128]{1,0:T(8,128)(2,1)} %collective-permute-done.3.refs_1_), channel_id=1, source_target_pairs={{0,16},{8,24},{16,0},{24,8},{1,17},{9,25},{17,1},{25,9},{2,18},{10... | collective-permute-start | bytes 1572872 | tf_op jit(solution)/shard_map/ppermute | solution.py:173
  52.1 9.5 %collective-permute-done.11.refs_3_ = bf16[2048,128]{1,0:T(8,128)(2,1)} collective-permute-done((bf16[2048,128]{1,0:T(8,128)(2,1)S(1)}, bf16[2048,128]{1,0:T(8,128)(2,1)}, u32[]{:S(2)}, u32[]{:S(2)}) %collective-permute-start.11) | collective-permute-done | bytes 524320 | tf_op jit(solution)/shard_map/ppermute | solution.py:173
  61.6 1.7 %collective-permute-start.8 = (bf16[2048,128]{1,0:T(8,128)(2,1)}, bf16[2048,128]{1,0:T(8,128)(2,1)}, u32[]{:S(2)}, u32[]{:S(2)}) collective-permute-start(bf16[2048,128]{1,0:T(8,128)(2,1)} %collective-permute-done.7.refs_6_), channel_id=1, source_target_pairs={{0,8},{8,0},{16,24},{24,16},{1,9},{9,1},{17,25},{25,17},{2,10},{10... | collective-permute-start | bytes 1572872 | tf_op jit(solution)/shard_map/ppermute | solution.py:173
  63.6 0.1 reshape.6.rand_ref
  63.9 21.2 %pair.2.refs_8_ = bf16[2048,256]{1,0:T(8,128)(2,1)} custom-call(s32[192]{0:T(256)S(1)} %reshape.7.rand_ref, s32[34]{0:T(128)S(1)} %fusion.5.win_ref, s32[8]{0:T(128)S(1)} %fusion.6.glob_ref, s32[2]{0:T(128)S(1)} %broadcast_subtract_fusion.own_ref, bf16[2048,256]{1,0:T(8,128)(2,1)S(1)} %copy-done.1, bf16[2048,256]{1,0:T(8,128)(2,1)S(1)} %copy-done, ...), custom_call_target="tpu_custom_call" | custom-call | flops 2952790016 | bytes 4194304 | tf_op jit(solution)/shard_map/pair/pallas_call | solution.py:149
  85.2 21.5 %pair.3 = bf16[2048,256]{1,0:T(8,128)(2,1)} custom-call(s32[192]{0:T(256)S(1)} %reshape.6.rand_ref, s32[34]{0:T(128)S(1)} %fusion.5.win_ref, s32[8]{0:T(128)S(1)} %fusion.6.glob_ref, s32[2]{0:T(128)S(1)} %broadcast_subtract_fusion.own_ref, bf16[2048,256]{1,0:T(8,128)(2,1)S(1)} %copy-done.1, ...), custom_call_target="tpu_custom_call", output_to_operand_aliasing={{}: (13, {})} | custom-call | flops 2952790016 | bytes 4194304 | tf_op jit(solution)/shard_map/pair/pallas_call | solution.py:149
  (29 shorter events, 0.6 us)
Async XLA Ops:
  0.0 5.3 %copy-start.2 = (bf16[2048,256]{1,0:T(8,128)(2,1)S(1)}, bf16[2048,256]{1,0:T(8,128)(2,1)}, u32[]{:S(2)}) copy-start(bf16[2048,256]{1,0:T(8,128)(2,1)} %refs_4_.3) | copy-start | bytes 3145732
  2.3 61.6 %copy-start = (bf16[2048,256]{1,0:T(8,128)(2,1)S(1)}, bf16[2048,256]{1,0:T(8,128)(2,1)}, u32[]{:S(2)}) copy-start(bf16[2048,256]{1,0:T(8,128)(2,1)} %refs_0_.3) | copy-start | bytes 3145732
  2.3 61.6 %copy-start.1 = (bf16[2048,256]{1,0:T(8,128)(2,1)S(1)}, bf16[2048,256]{1,0:T(8,128)(2,1)}, u32[]{:S(2)}) copy-start(bf16[2048,256]{1,0:T(8,128)(2,1)} %q_ref.3) | copy-start | bytes 3145732
  2.3 32.8 %collective-permute-start.9 = (bf16[2048,128]{1,0:T(8,128)(2,1)}, bf16[2048,128]{1,0:T(8,128)(2,1)S(1)}, u32[]{:S(2)}, u32[]{:S(2)}) collective-permute-start(bf16[2048,128]{1,0:T(8,128)(2,1)} %get-tuple-element.7), channel_id=1, source_target_pairs={{0,8},{8,0},{16,24},{24,16},{1,9},{9,1},{17,25},{25,17},{2,10},{10... | collective-permute-start | bytes 1572872 | tf_op jit(solution)/shard_map/ppermute | solution.py:173
  6.3 2.0 %copy-start.4 = (s32[2]{0:T(128)S(1)}, s32[2]{0:T(128)}, u32[]{:S(2)}) copy-start(s32[2]{0:T(128)} %param.9) | copy-start | bytes 28
  6.3 30.8 %copy-start.3 = (s32[32,4,3]{0,1,2:T(4,128)S(1)}, s32[32,4,3]{0,1,2:T(4,128)}, u32[]{:S(2)}) copy-start(s32[32,4,3]{0,1,2:T(4,128)} %param.8) | copy-start | bytes 4612
  6.3 30.5 %collective-permute-start.13 = (bf16[2048,128]{1,0:T(8,128)(2,1)}, bf16[2048,128]{1,0:T(8,128)(2,1)S(1)}, u32[]{:S(2)}, u32[]{:S(2)}) collective-permute-start(bf16[2048,128]{1,0:T(8,128)(2,1)} %get-tuple-element.5), channel_id=1, source_target_pairs={{0,16},{8,24},{16,0},{24,8},{1,17},{9,25},{17,1},{25,9},{2,18},{10... | collective-permute-start | bytes 1572872 | tf_op jit(solution)/shard_map/ppermute | solution.py:173
  7.9 29.3 %collective-permute-start.10 = (bf16[2048,128]{1,0:T(8,128)(2,1)}, bf16[2048,128]{1,0:T(8,128)(2,1)}, u32[]{:S(2)}, u32[]{:S(2)}) collective-permute-start(bf16[2048,128]{1,0:T(8,128)(2,1)} %get-tuple-element.7), channel_id=1, source_target_pairs={{0,16},{8,24},{16,0},{24,8},{1,17},{9,25},{17,1},{25,9},{2,18},{10... | collective-permute-start | bytes 1572872 | tf_op jit(solution)/shard_map/ppermute | solution.py:173
  8.4 9.1 %collective-permute-start = (s32[2]{0:T(128)S(1)}, s32[2]{0:T(128)S(1)}, u32[]{:S(2)}, u32[]{:S(2)}) collective-permute-start(s32[2]{0:T(128)S(1)} %copy-done.4), channel_id=1, source_target_pairs={{0,8},{8,0},{16,24},{24,16},{1,9},{9,1},{17,25},{25,17},{2,10},{10... | collective-permute-start | bytes 32 | tf_op jit(solution)/shard_map/ppermute | solution.py:173
  8.5 22.8 %collective-permute-start.1 = (s32[2]{0:T(128)S(1)}, s32[2]{0:T(128)S(1)}, u32[]{:S(2)}, u32[]{:S(2)}) collective-permute-start(s32[2]{0:T(128)S(1)} %copy-done.4), channel_id=1, source_target_pairs={{0,16},{8,24},{16,0},{24,8},{1,17},{9,25},{17,1},{25,9},{2,18},{10... | collective-permute-start | bytes 32 | tf_op jit(solution)/shard_map/ppermute | solution.py:173
  17.5 21.5 %collective-permute-start.12 = (bf16[2048,128]{1,0:T(8,128)(2,1)}, bf16[2048,128]{1,0:T(8,128)(2,1)}, u32[]{:S(2)}, u32[]{:S(2)}) collective-permute-start(bf16[2048,128]{1,0:T(8,128)(2,1)} %get-tuple-element.5), channel_id=1, source_target_pairs={{0,8},{8,0},{16,24},{24,16},{1,9},{9,1},{17,25},{25,17},{2,10},{10... | collective-permute-start | bytes 1572872 | tf_op jit(solution)/shard_map/ppermute | solution.py:173
  31.3 3.5 %collective-permute-start.2 = (s32[2]{0:T(128)S(1)}, s32[2]{0:T(128)S(1)}, u32[]{:S(2)}, u32[]{:S(2)}) collective-permute-start(s32[2]{0:T(128)S(1)} %collective-permute-done), channel_id=1, source_target_pairs={{0,16},{8,24},{16,0},{24,8},{1,17},{9,25},{17,1},{25,9},{2,18},{10... | collective-permute-start | bytes 32 | tf_op jit(solution)/shard_map/ppermute | solution.py:173
  34.8 15.2 %collective-permute-start.3 = (bf16[2048,128]{1,0:T(8,128)(2,1)}, bf16[2048,128]{1,0:T(8,128)(2,1)}, u32[]{:S(2)}, u32[]{:S(2)}) collective-permute-start(bf16[2048,128]{1,0:T(8,128)(2,1)} %get-tuple-element.8), channel_id=1, source_target_pairs={{0,8},{8,0},{16,24},{24,16},{1,9},{9,1},{17,25},{25,17},{2,10},{10... | collective-permute-start | bytes 1572872 | tf_op jit(solution)/shard_map/ppermute | solution.py:173
  35.1 15.2 %collective-permute-start.7 = (bf16[2048,128]{1,0:T(8,128)(2,1)}, bf16[2048,128]{1,0:T(8,128)(2,1)}, u32[]{:S(2)}, u32[]{:S(2)}) collective-permute-start(bf16[2048,128]{1,0:T(8,128)(2,1)} %get-tuple-element.6), channel_id=1, source_target_pairs={{0,16},{8,24},{16,0},{24,8},{1,17},{9,25},{17,1},{25,9},{2,18},{10... | collective-permute-start | bytes 1572872 | tf_op jit(solution)/shard_map/ppermute | solution.py:173
  36.9 24.7 %collective-permute-start.11 = (bf16[2048,128]{1,0:T(8,128)(2,1)S(1)}, bf16[2048,128]{1,0:T(8,128)(2,1)}, u32[]{:S(2)}, u32[]{:S(2)}) collective-permute-start(bf16[2048,128]{1,0:T(8,128)(2,1)S(1)} %collective-permute-done.9.refs_1_), channel_id=1, source_target_pairs={{0,16},{8,24},{16,0},{24,8},{1,17},{9,25},{17,1},{25,9},{2,18},{10... | collective-permute-start | bytes 1572872 | tf_op jit(solution)/shard_map/ppermute | solution.py:173
  37.2 26.7 %collective-permute-start.14 = (bf16[2048,128]{1,0:T(8,128)(2,1)S(1)}, bf16[2048,128]{1,0:T(8,128)(2,1)}, u32[]{:S(2)}, u32[]{:S(2)}) collective-permute-start(bf16[2048,128]{1,0:T(8,128)(2,1)S(1)} %collective-permute-done.13.refs_6_), channel_id=1, source_target_pairs={{0,8},{8,0},{16,24},{24,16},{1,9},{9,1},{17,25},{25,17},{2,10},{10... | collective-permute-start | bytes 1572872 | tf_op jit(solution)/shard_map/ppermute | solution.py:173
  39.0 46.2 %collective-permute-start.4 = (bf16[2048,128]{1,0:T(8,128)(2,1)}, bf16[2048,128]{1,0:T(8,128)(2,1)}, u32[]{:S(2)}, u32[]{:S(2)}) collective-permute-start(bf16[2048,128]{1,0:T(8,128)(2,1)} %get-tuple-element.8), channel_id=1, source_target_pairs={{0,16},{8,24},{16,0},{24,8},{1,17},{9,25},{17,1},{25,9},{2,18},{10... | collective-permute-start | bytes 1572872 | tf_op jit(solution)/shard_map/ppermute | solution.py:173
  50.0 35.2 %collective-permute-start.6 = (bf16[2048,128]{1,0:T(8,128)(2,1)}, bf16[2048,128]{1,0:T(8,128)(2,1)}, u32[]{:S(2)}, u32[]{:S(2)}) collective-permute-start(bf16[2048,128]{1,0:T(8,128)(2,1)} %get-tuple-element.6), channel_id=1, source_target_pairs={{0,8},{8,0},{16,24},{24,16},{1,9},{9,1},{17,25},{25,17},{2,10},{10... | collective-permute-start | bytes 1572872 | tf_op jit(solution)/shard_map/ppermute | solution.py:173
  50.3 34.9 %collective-permute-start.5 = (bf16[2048,128]{1,0:T(8,128)(2,1)}, bf16[2048,128]{1,0:T(8,128)(2,1)}, u32[]{:S(2)}, u32[]{:S(2)}) collective-permute-start(bf16[2048,128]{1,0:T(8,128)(2,1)} %collective-permute-done.3.refs_1_), channel_id=1, source_target_pairs={{0,16},{8,24},{16,0},{24,8},{1,17},{9,25},{17,1},{25,9},{2,18},{10... | collective-permute-start | bytes 1572872 | tf_op jit(solution)/shard_map/ppermute | solution.py:173
  61.6 23.6 %collective-permute-start.8 = (bf16[2048,128]{1,0:T(8,128)(2,1)}, bf16[2048,128]{1,0:T(8,128)(2,1)}, u32[]{:S(2)}, u32[]{:S(2)}) collective-permute-start(bf16[2048,128]{1,0:T(8,128)(2,1)} %collective-permute-done.7.refs_6_), channel_id=1, source_target_pairs={{0,8},{8,0},{16,24},{24,16},{1,9},{9,1},{17,25},{25,17},{2,10},{10... | collective-permute-start | bytes 1572872 | tf_op jit(solution)/shard_map/ppermute | solution.py:173

commit v2 on v1

v2 whole, which is shorter than its diff:
```python
import functools

import jax
import jax.numpy as jnp
from jax import lax
from jax.experimental import pallas as pl
from jax.experimental.pallas import tpu as pltpu
from jax.sharding import PartitionSpec as P

DH = 64
BLK = 64
RAND = 3
LANES = 2 * DH
ROWS = 4
CHUNK = 1024
EXP2_SCALE = 0.125 * 1.4426950408889634


def qk(q, k):
    return lax.dot_general(q, k, (((1,), (1,)), ((), ())), preferred_element_type=jnp.float32)


def part_kernel(
    pair, wide, gpd, tokens, shared, late, lists_ref, glob_ref, own_ref, q_ref, *refs
):
    ranges = len(wide)
    k_refs, v_refs, refs = refs[:ranges], refs[ranges : 2 * ranges], refs[2 * ranges :]
    if late:
        state_o_ref, state_l_ref, refs = refs[0], refs[1], refs[2:]
        if pair > 0:
            refs = refs[1:]
        out_ref, k_all, v_all, units, k_glob, v_glob, sems = refs
    else:
        out_ref, out_l_ref, k_all, v_all, units, k_glob, v_glob, sems = refs
    blocks = tokens // BLK
    globs = gpd * ranges
    empty = ranges * blocks

    copies = []
    for j in range(ranges):
        span = pl.ds(j * tokens, tokens)
        lanes = pl.ds(pair * LANES, LANES)
        for side, (source, target) in enumerate(((k_refs[j], k_all), (v_refs[j], v_all))):
            source = source.at[:, lanes] if wide[j] else source
            copies.append(pltpu.make_async_copy(source, target.at[span], sems.at[2 * j + side]))
    for copy in copies:
        copy.start()
    v_all[empty * BLK :, :] = jnp.zeros((BLK, LANES), jnp.bfloat16)
    units[:BLK, :] = jnp.ones((BLK, LANES), jnp.bfloat16)
    units[BLK:, :] = jnp.zeros((BLK, LANES), jnp.bfloat16)
    for copy in copies:
        copy.wait()

    first = lax.broadcasted_iota(jnp.int32, (BLK, LANES), 1) < DH

    def split_heads(q):
        zero = jnp.zeros_like(q)
        return [jnp.where(first, q, zero), jnp.where(first, zero, q)]

    def block(ref, position):
        return ref[pl.ds(pl.multiple_of(position * BLK, BLK), BLK), :]

    def unit(position):
        return block(units, (position == empty).astype(jnp.int32))

    def weighted(p, v, ones):
        return jnp.dot(
            p.astype(jnp.bfloat16), jnp.concatenate([v, ones], axis=1),
            preferred_element_type=jnp.float32,
        )

    def fold(rows):
        return jnp.where(first, rows[:BLK], rows[BLK:])

    def finish(b, target, peak, sums):
        top = fold(jnp.broadcast_to(peak, (2 * BLK, LANES))) * EXP2_SCALE
        o, total = fold(sums[:, :LANES]), fold(sums[:, LANES:])
        where = pl.ds(pl.multiple_of(target * BLK, BLK), BLK)
        if late:
            old_o, old_l = block(state_o_ref, b), block(state_l_ref, b)
            level = jnp.maximum(top, old_l)
            old_factor, factor = jnp.exp2(old_l - level), jnp.exp2(top - level)
            o = (old_o * old_factor + o * factor) / (old_factor + total * factor)
            out_ref[where, :] = o.astype(jnp.bfloat16)
        else:
            out_ref[where, :] = o / total
            out_l_ref[where, :] = top + jnp.log2(total)

    for g in range(globs):
        k_glob[g * BLK : (g + 1) * BLK, :] = block(k_all, glob_ref[g])
        v_glob[g * BLK : (g + 1) * BLK, :] = block(v_all, glob_ref[g])

    slots = shared + 2 * RAND

    def rows_step(step, carry):
        base = step * ROWS
        q_bd, k_lists, v_lists = [], [], []
        for u in range(ROWS):
            at = (base + u) * 2 * slots
            q_bd += split_heads(block(q_ref, base + u))
            k_list, v_list, one_list = [], [], []
            for j in range(shared):
                k_at, v_at = lists_ref[at + j], lists_ref[at + slots + j]
                k_list.append(block(k_all, k_at))
                v_list.append(block(v_all, v_at))
                one_list.append(unit(v_at))
            for j in range(shared, shared + RAND):
                k_a, k_b = lists_ref[at + j], lists_ref[at + RAND + j]
                v_a, v_b = lists_ref[at + slots + j], lists_ref[at + slots + RAND + j]
                k_list.append(jnp.where(first, block(k_all, k_a), block(k_all, k_b)))
                v_list.append(jnp.where(first, block(v_all, v_a), block(v_all, v_b)))
                one_list.append(jnp.where(first, unit(v_a), unit(v_b)))
            k_lists.append(jnp.concatenate(k_list, axis=0))
            v_lists.append((jnp.concatenate(v_list, axis=0), jnp.concatenate(one_list, axis=0)))
        q_bd = jnp.concatenate(q_bd, axis=0)
        parts = [slice(2 * BLK * u, 2 * BLK * (u + 1)) for u in range(ROWS)]
        s_own = jnp.concatenate([qk(q_bd[parts[u]], k_lists[u]) for u in range(ROWS)], axis=0)
        s_glob = qk(q_bd, k_glob[...])
        peak = jnp.maximum(
            jnp.max(s_own, axis=1, keepdims=True), jnp.max(s_glob, axis=1, keepdims=True)
        )
        w_own = jnp.exp2((s_own - peak) * EXP2_SCALE)
        w_glob = jnp.exp2((s_glob - peak) * EXP2_SCALE)
        sums_glob = weighted(w_glob, v_glob[...], jnp.ones((globs * BLK, LANES), jnp.bfloat16))
        for u in range(ROWS):
            sums = sums_glob[parts[u]] + weighted(w_own[parts[u]], *v_lists[u])
            finish(base + u, base + u, peak[parts[u]], sums)
        return carry

    lax.fori_loop(0, blocks // ROWS, rows_step, 0)

    q_glob = []
    for g in range(gpd):
        q_glob += split_heads(block(q_ref, own_ref[g]))
    q_glob = jnp.concatenate(q_glob, axis=0)
    chunk_ones = jnp.ones((CHUNK, LANES), jnp.bfloat16)

    def chunk_step(c, carry):
        peak, sums = carry
        span = pl.ds(pl.multiple_of(c * CHUNK, CHUNK), CHUNK)
        s = qk(q_glob, k_all[span, :])
        top = jnp.maximum(peak, jnp.max(s, axis=1, keepdims=True))
        w = jnp.exp2((s - top) * EXP2_SCALE)
        sums = sums * jnp.exp2((peak - top) * EXP2_SCALE) + weighted(w, v_all[span, :], chunk_ones)
        return top, sums

    height = 2 * gpd * BLK
    initial = (
        jnp.full((height, 1), -1e30, jnp.float32),
        jnp.zeros((height, 2 * LANES), jnp.float32),
    )
    peak, sums = lax.fori_loop(0, ranges * tokens // CHUNK, chunk_step, initial)
    for g in range(gpd):
        part = slice(2 * BLK * g, 2 * BLK * (g + 1))
        finish(blocks + g, own_ref[g] if late else blocks + g, peak[part], sums[part])


def part_call(pair, shared, lists, glob, own, queries, k_parts, v_parts, state=None, so_far=None):
    tokens, columns = queries.shape
    ranges = len(k_parts)
    gpd = own.shape[0]
    late = state is not None
    smem = pl.BlockSpec(memory_space=pltpu.SMEM)
    hbm = pl.BlockSpec(memory_space=pl.ANY)
    half = pl.BlockSpec((tokens, LANES), lambda i: (0, pair))
    state_rows = tokens + gpd * BLK
    full = pl.BlockSpec((state_rows, LANES), lambda i: (0, 0))
    operands = [lists, glob, own, queries, *k_parts, *v_parts]
    in_specs = [smem] * 3 + [half] + [hbm] * (2 * ranges)
    aliases = {}
    if late:
        operands += state
        in_specs += [full, full]
        out_specs = half
        out_shape = jax.ShapeDtypeStruct((tokens, columns), jnp.bfloat16)
        if so_far is not None:
            aliases = {len(operands): 0}
            operands.append(so_far)
            in_specs.append(hbm)
    else:
        out_specs = [full, full]
        out_shape = [jax.ShapeDtypeStruct((state_rows, LANES), jnp.float32)] * 2
    keys_all = ranges * tokens
    globs = gpd * ranges * BLK
    listed = (shared + RAND) * BLK
    pairs_done = 2 * tokens * (listed + globs) + 2 * gpd * BLK * keys_all
    wide = tuple(part.shape[1] > LANES for part in k_parts)
    return pl.pallas_call(
        functools.partial(part_kernel, pair, wide, gpd, tokens, shared, late),
        grid=(1,),
        in_specs=in_specs,
        out_specs=out_specs,
        out_shape=out_shape,
        input_output_aliases=aliases,
        scratch_shapes=[
            pltpu.VMEM((keys_all, LANES), jnp.bfloat16),
            pltpu.VMEM((keys_all + BLK, LANES), jnp.bfloat16),
            pltpu.VMEM((2 * BLK, LANES), jnp.bfloat16),
            pltpu.VMEM((globs, LANES), jnp.bfloat16),
            pltpu.VMEM((globs, LANES), jnp.bfloat16),
            pltpu.SemaphoreType.DMA((2 * ranges,)),
        ],
        compiler_params=pltpu.CompilerParams(vmem_limit_bytes=48 * 1024 * 1024),
        cost_estimate=pl.CostEstimate(
            flops=16 * DH * pairs_done,
            bytes_accessed=4 * keys_all * LANES,
            transcendentals=pairs_done,
        ),
        name="late" if late else "early",
    )(*operands)


def exchange(array, step):
    count = lax.axis_size("seq")
    return lax.ppermute(array, "seq", [(i, i ^ step) for i in range(count)])


def gathered(array, steps):
    parts = {0: array}
    last = (1 << len(steps)) - 1
    for step in steps:
        for at, part in list(parts.items()):
            if at ^ step != last:
                parts[at ^ step] = exchange(part, step)
    return [parts[at] for at in range(last)], parts[last ^ steps[-1]]


def shards(queries, keys, values, rand_blocks, global_blocks):
    tokens, columns = queries.shape
    blocks = tokens // BLK
    gpd = global_blocks.shape[0]
    count = lax.axis_size("seq")
    rank = lax.axis_index("seq")
    pairs = columns // LANES
    steps = [1 << i for i in range(count.bit_length() - 1)]
    back = steps[::-1]
    early = count - 1

    k_early, k_send = gathered(keys, steps)
    v_early, v_send = gathered(values, back)
    g_early, g_send = gathered(global_blocks, steps)
    glob = jnp.concatenate(g_early + [exchange(g_send, steps[-1])])
    own = global_blocks - rank * blocks
    k_late, v_late = [], []
    for pair in range(pairs):
        lanes = slice(pair * LANES, (pair + 1) * LANES)
        k_late.append(exchange(k_send[:, lanes], steps[-1]))
        v_late.append(exchange(v_send[:, lanes], back[-1]))

    def place(ids):
        return ((ids // blocks) ^ rank) * blocks + ids % blocks

    glob = place(glob)
    row = jnp.arange(blocks)[:, None]
    window = place((rank * blocks + row + jnp.arange(-1, 2)) % (count * blocks))
    rand = place(rand_blocks)
    glob_early, glob_late = glob[: gpd * early], glob[gpd * early :] - early * blocks
    own_row = jnp.broadcast_to(row, window.shape)
    window_early = window < early * blocks
    window_k = jnp.where(window_early, window, own_row)
    window_v = jnp.where(window_early, window, early * blocks)
    halo = jnp.where(row == 0, window[:, :1], window[:, 2:])
    halo_late = halo >= early * blocks
    halo_k = jnp.where(halo_late, halo - early * blocks, glob_late[0])
    halo_v = jnp.where(halo_late, halo - early * blocks, blocks)

    early_state, out = [], None
    for pair in range(pairs):
        mine = rand[:, 2 * pair : 2 * pair + 2].reshape(blocks, 2 * RAND)
        in_early = mine < early * blocks
        lists = jnp.concatenate(
            [window_k, jnp.where(in_early, mine, row), window_v, jnp.where(in_early, mine, early * blocks)],
            axis=1,
        ).reshape(-1)
        early_state.append(
            part_call(pair, 3, lists, glob_early, own, queries, k_early, v_early)
        )
    for pair in range(pairs):
        mine = rand[:, 2 * pair : 2 * pair + 2].reshape(blocks, 2 * RAND)
        in_late = mine >= early * blocks
        lists = jnp.concatenate(
            [
                halo_k,
                jnp.where(in_late, mine - early * blocks, glob_late[0]),
                halo_v,
                jnp.where(in_late, mine - early * blocks, blocks),
            ],
            axis=1,
        ).reshape(-1)
        out = part_call(
            pair, 1, lists, glob_late, own, queries, [k_late[pair]], [v_late[pair]],
            early_state[pair], out,
        )
    return out


def solution(mesh):
    in_specs = (
        P(("batch", "seq"), "head"),
        P(("batch", "seq"), "head"),
        P(("batch", "seq"), "head"),
        P(("batch", "seq"), "head", None),
        P(("batch", "seq")),
    )
    out_specs = P(("batch", "seq"), "head")
    return jax.shard_map(shards, mesh=mesh, in_specs=in_specs, out_specs=out_specs, check_vma=False)
```

time: 107 us -> 109 us (1.019)
  Pallas kernels: 42.8 us -> 50.9 us
  starting transfers between devices: 19.7 us -> 13.4 us
  local copies, waits for them, and re-layouts: 3.9 us -> 0.96 us
  other arithmetic: 0.13 us -> 2.4 us
  waiting for transfers between devices: 40.1 us -> 41.2 us
    pallas_call x2 -> x4, Pallas kernels: 42.8 us -> 50.9 us  [part_call(): pl.pallas_call(functools.partial(part_kernel, pair, wide, gpd, tokens, sh...]
    ppermute x15 -> x11, starting transfers between devices: 19.7 us -> 13.4 us  [exchange(): return lax.ppermute(array, 'seq', [(i, i ^ step) for i in range(count)])]
    slice x5, local copies, waits for them, and re-layouts: 3.59 us -> 0.15 us  [the longest x1 0.07 us: shards(): v_late.append(exchange(v_send[:, lanes], back[-1]))]
    add x3 -> x2, other arithmetic: 0.13 us -> 1.45 us  [place(): return (ids // blocks ^ rank) * blocks + ids % blocks]
    ppermute x15 -> x11, waiting for transfers between devices: 40.1 us -> 41.2 us  [exchange(): return lax.ppermute(array, 'seq', [(i, i ^ step) for i in range(count)])]
  transfers between devices with their start and end apart: 15 -> 11, of which waited for: 5 -> 1; matrix products, arithmetic and copies ran while one was open for 2% -> 3% of each run, Pallas kernels for 20% -> 39%
where the time goes in v2:
time: 109 us
  Pallas kernels  50.9 us (47%)
  waiting for transfers between devices  41.2 us (38%)
  starting transfers between devices  13.4 us (12%)
  other arithmetic  2.4 us (2%)
    pallas_call x4, Pallas kernels, part_call(): pl.pallas_call(functools.partial(part_kernel, pair, wide, gpd, tokens, sh...  50.9 us
    ppermute x11, waiting for transfers between devices, exchange(): return lax.ppermute(array, 'seq', [(i, i ^ step) for i in range(count)])  41.2 us
    ppermute x11, starting transfers between devices, exchange(): return lax.ppermute(array, 'seq', [(i, i ^ step) for i in range(count)])  13.4 us
  transfers between devices with their start and end apart: 11, of which 1 were waited for; matrix products, arithmetic and copies ran while one was open for 3% of the time, Pallas kernels for 39%

profile of v2, /device:TPU:0, one launch (start us, length us, event | category | flops | bytes accessed | tf_op | source)
XLA Modules:
  0.0 109.1 jit_solution(13840341742589837503)
XLA Ops:
  0.0 2.9 %collective-permute-start = (s32[2]{0:T(128)}, s32[2]{0:T(128)S(1)}, u32[]{:S(2)}, u32[]{:S(2)}) collective-permute-start(s32[2]{0:T(128)} %param.9), channel_id=1, source_target_pairs={{0,8},{8,0},{16,24},{24,16},{1,9},{9,1},{17,25},{25,17},{2,10},{10... | collective-permute-start | bytes 32 | tf_op jit(solution)/shard_map/ppermute | solution.py:215
  2.9 1.5 %collective-permute-start.1 = (s32[2]{0:T(128)}, s32[2]{0:T(128)S(1)}, u32[]{:S(2)}, u32[]{:S(2)}) collective-permute-start(s32[2]{0:T(128)} %param.9), channel_id=1, source_target_pairs={{0,16},{8,24},{16,0},{24,8},{1,17},{9,25},{17,1},{25,9},{2,18},{10... | collective-permute-start | bytes 32 | tf_op jit(solution)/shard_map/ppermute | solution.py:215
  4.5 0.5 collective-permute-start.3
  5.0 2.0 %collective-permute-start.5 = (bf16[2048,256]{1,0:T(8,128)(2,1)}, bf16[2048,256]{1,0:T(8,128)(2,1)S(1)}, u32[]{:S(2)}, u32[]{:S(2)}) collective-permute-start(bf16[2048,256]{1,0:T(8,128)(2,1)} %refs_3_.3), channel_id=1, source_target_pairs={{0,16},{8,24},{16,0},{24,8},{1,17},{9,25},{17,1},{25,9},{2,18},{10... | collective-permute-start | bytes 3145736 | tf_op jit(solution)/shard_map/ppermute | solution.py:215
  7.0 0.7 fusion.6
  7.8 0.1 compare_select_fusion.5
  7.9 0.7 broadcast_subtract_fusion.own_ref
  8.5 1.6 %collective-permute-start.8 = (bf16[2048,256]{1,0:T(8,128)(2,1)}, bf16[2048,256]{1,0:T(8,128)(2,1)}, u32[]{:S(2)}, u32[]{:S(2)}) collective-permute-start(bf16[2048,256]{1,0:T(8,128)(2,1)} %refs_3_.3), channel_id=1, source_target_pairs={{0,8},{8,0},{16,24},{24,16},{1,9},{9,1},{17,25},{25,17},{2,10},{10... | collective-permute-start | bytes 3145736 | tf_op jit(solution)/shard_map/ppermute | solution.py:215
  10.1 0.5 collective-permute-start.2
  10.6 41.2 %collective-permute-done.2 = s32[2]{0:T(128)S(1)} collective-permute-done((s32[2]{0:T(128)S(1)}, s32[2]{0:T(128)S(1)}, u32[]{:S(2)}, u32[]{:S(2)}) %collective-permute-start.2) | collective-permute-done | bytes 40 | tf_op jit(solution)/shard_map/ppermute | solution.py:215
  51.8 0.7 fusion.15
  52.8 0.1 reshape.42.lists_ref
  52.9 0.1 copy.11
  53.0 0.1 reshape.41.lists_ref
  53.2 0.1 reshape.39.lists_ref
  53.4 0.1 reshape.38.lists_ref
  53.7 1.6 %collective-permute-start.10 = (bf16[2048,128]{1,0:T(8,128)(2,1)S(1)}, bf16[2048,128]{1,0:T(8,128)(2,1)S(1)}, u32[]{:S(2)}, u32[]{:S(2)}) collective-permute-start(bf16[2048,128]{1,0:T(8,128)(2,1)S(1)} %get-tuple-element.13), channel_id=1, source_target_pairs={{0,8},{8,0},{16,24},{24,16},{1,9},{9,1},{17,25},{25,17},{2,10},{10... | collective-permute-start | bytes 1572872 | tf_op jit(solution)/shard_map/ppermute | solution.py:215
  55.3 0.6 collective-permute-start.9
  55.9 1.5 %collective-permute-start.4 = (bf16[2048,128]{1,0:T(8,128)(2,1)S(1)}, bf16[2048,128]{1,0:T(8,128)(2,1)S(1)}, u32[]{:S(2)}, u32[]{:S(2)}) collective-permute-start(bf16[2048,128]{1,0:T(8,128)(2,1)S(1)} %get-tuple-element.16), channel_id=1, source_target_pairs={{0,16},{8,24},{16,0},{24,8},{1,17},{9,25},{17,1},{25,9},{2,18},{10... | collective-permute-start | bytes 1572872 | tf_op jit(solution)/shard_map/ppermute | solution.py:215
  57.4 0.6 collective-permute-start.6
  58.1 16.6 %early.3 = (f32[2176,128]{1,0:T(8,128)}, f32[2176,128]{1,0:T(8,128)}) custom-call(s32[576]{0:T(1024)S(1)} %reshape.42.lists_ref, s32[6]{0:T(128)S(1)} %bitcast.9, s32[2]{0:T(128)S(1)} %broadcast_subtract_fusion.own_ref, bf16[2048,256]{1,0:T(8,128)(2,1)S(1)} %copy-done.2, bf16[2048,256]{1,0:T(8,128)(2,1)S(1)} %copy-done, ...), custom_call_target="tpu_custom_call" | custom-call | flops 4831838208 | bytes 3145728 | tf_op jit(solution)/shard_map/early/pallas_call | solution.py:188
  74.7 16.6 %early.2 = (f32[2176,128]{1,0:T(8,128)}, f32[2176,128]{1,0:T(8,128)}) custom-call(s32[576]{0:T(1024)S(1)} %reshape.39.lists_ref, s32[6]{0:T(128)S(1)} %bitcast.10, s32[2]{0:T(128)S(1)} %broadcast_subtract_fusion.own_ref, bf16[2048,256]{1,0:T(8,128)(2,1)S(1)} %copy-done.2, bf16[2048,256]{1,0:T(8,128)(2,1)S(1)} %copy-done, ...), custom_call_target="tpu_custom_call" | custom-call | flops 4831838208 | bytes 3145728 | tf_op jit(solution)/shard_map/early/pallas_call | solution.py:188
  91.3 8.8 %late.2.refs_4_ = bf16[2048,256]{1,0:T(8,128)(2,1)} custom-call(s32[448]{0:T(512)S(1)} %reshape.41.lists_ref, s32[2]{0:T(128)S(1)} %slice_add_fusion.glob_ref, s32[2]{0:T(128)S(1)} %broadcast_subtract_fusion.own_ref, bf16[2048,256]{1,0:T(8,128)(2,1)S(1)} %copy-done.2, bf16[2048,128]{1,0:T(8,128)(2,1)S(1)} %collective-permute-done.9.refs_0_, ...), custom_call_target="tpu_custom_call" | custom-call | flops 2147483648 | bytes 1048576 | tf_op jit(solution)/shard_map/late/pallas_call | solution.py:188
  100.2 8.8 %late.3 = bf16[2048,256]{1,0:T(8,128)(2,1)} custom-call(s32[448]{0:T(512)S(1)} %reshape.38.lists_ref, s32[2]{0:T(128)S(1)} %slice_add_fusion.glob_ref, s32[2]{0:T(128)S(1)} %broadcast_subtract_fusion.own_ref, bf16[2048,256]{1,0:T(8,128)(2,1)S(1)} %copy-done.2, bf16[2048,128]{1,0:T(8,128)(2,1)S(1)} %collective-permute-done.4.refs_0_, ...), custom_call_target="tpu_custom_call", output_to_operand_aliasing={{}: (8, {})} | custom-call | flops 2147483648 | bytes 1048576 | tf_op jit(solution)/shard_map/late/pallas_call | solution.py:188
  (44 shorter events, 0.7 us)
Async XLA Ops:
  0.0 8.5 %collective-permute-start = (s32[2]{0:T(128)}, s32[2]{0:T(128)S(1)}, u32[]{:S(2)}, u32[]{:S(2)}) collective-permute-start(s32[2]{0:T(128)} %param.9), channel_id=1, source_target_pairs={{0,8},{8,0},{16,24},{24,16},{1,9},{9,1},{17,25},{25,17},{2,10},{10... | collective-permute-start | bytes 32 | tf_op jit(solution)/shard_map/ppermute | solution.py:215
  2.9 7.2 %collective-permute-start.1 = (s32[2]{0:T(128)}, s32[2]{0:T(128)S(1)}, u32[]{:S(2)}, u32[]{:S(2)}) collective-permute-start(s32[2]{0:T(128)} %param.9), channel_id=1, source_target_pairs={{0,16},{8,24},{16,0},{24,8},{1,17},{9,25},{17,1},{25,9},{2,18},{10... | collective-permute-start | bytes 32 | tf_op jit(solution)/shard_map/ppermute | solution.py:215
  4.5 50.8 %collective-permute-start.3 = (bf16[2048,256]{1,0:T(8,128)(2,1)}, bf16[2048,256]{1,0:T(8,128)(2,1)S(1)}, u32[]{:S(2)}, u32[]{:S(2)}) collective-permute-start(bf16[2048,256]{1,0:T(8,128)(2,1)} %refs_0_.3), channel_id=1, source_target_pairs={{0,8},{8,0},{16,24},{24,16},{1,9},{9,1},{17,25},{25,17},{2,10},{10... | collective-permute-start | bytes 3145736 | tf_op jit(solution)/shard_map/ppermute | solution.py:215
  5.0 52.4 %collective-permute-start.7 = (bf16[2048,256]{1,0:T(8,128)(2,1)}, bf16[2048,256]{1,0:T(8,128)(2,1)S(1)}, u32[]{:S(2)}, u32[]{:S(2)}) collective-permute-start(bf16[2048,256]{1,0:T(8,128)(2,1)} %refs_0_.3), channel_id=1, source_target_pairs={{0,16},{8,24},{16,0},{24,8},{1,17},{9,25},{17,1},{25,9},{2,18},{10... | collective-permute-start | bytes 3145736 | tf_op jit(solution)/shard_map/ppermute | solution.py:215
  5.0 48.5 %collective-permute-start.5 = (bf16[2048,256]{1,0:T(8,128)(2,1)}, bf16[2048,256]{1,0:T(8,128)(2,1)S(1)}, u32[]{:S(2)}, u32[]{:S(2)}) collective-permute-start(bf16[2048,256]{1,0:T(8,128)(2,1)} %refs_3_.3), channel_id=1, source_target_pairs={{0,16},{8,24},{16,0},{24,8},{1,17},{9,25},{17,1},{25,9},{2,18},{10... | collective-permute-start | bytes 3145736 | tf_op jit(solution)/shard_map/ppermute | solution.py:215
  8.5 49.5 %collective-permute-start.8 = (bf16[2048,256]{1,0:T(8,128)(2,1)}, bf16[2048,256]{1,0:T(8,128)(2,1)}, u32[]{:S(2)}, u32[]{:S(2)}) collective-permute-start(bf16[2048,256]{1,0:T(8,128)(2,1)} %refs_3_.3), channel_id=1, source_target_pairs={{0,8},{8,0},{16,24},{24,16},{1,9},{9,1},{17,25},{25,17},{2,10},{10... | collective-permute-start | bytes 3145736 | tf_op jit(solution)/shard_map/ppermute | solution.py:215
  10.1 41.7 %collective-permute-start.2 = (s32[2]{0:T(128)S(1)}, s32[2]{0:T(128)S(1)}, u32[]{:S(2)}, u32[]{:S(2)}) collective-permute-start(s32[2]{0:T(128)S(1)} %collective-permute-done), channel_id=1, source_target_pairs={{0,16},{8,24},{16,0},{24,8},{1,17},{9,25},{17,1},{25,9},{2,18},{10... | collective-permute-start | bytes 32 | tf_op jit(solution)/shard_map/ppermute | solution.py:215
  53.5 1.8 %copy-start.7 = (bf16[2048,256]{1,0:T(8,128)(2,1)}, bf16[2048,256]{1,0:T(8,128)(2,1)S(1)}, u32[]{:S(2)}) copy-start(bf16[2048,256]{1,0:T(8,128)(2,1)S(1)} %collective-permute-done.5.refs_5_) | copy-start | bytes 3145732
  53.5 4.5 %copy-start.2 = (bf16[2048,256]{1,0:T(8,128)(2,1)S(1)}, bf16[2048,256]{1,0:T(8,128)(2,1)}, u32[]{:S(2)}) copy-start(bf16[2048,256]{1,0:T(8,128)(2,1)} %q_ref.7) | copy-start | bytes 3145732
  53.6 4.4 %copy-start = (bf16[2048,256]{1,0:T(8,128)(2,1)S(1)}, bf16[2048,256]{1,0:T(8,128)(2,1)}, u32[]{:S(2)}) copy-start(bf16[2048,256]{1,0:T(8,128)(2,1)} %refs_0_.3) | copy-start | bytes 3145732
  53.6 4.4 %copy-start.1 = (bf16[2048,256]{1,0:T(8,128)(2,1)S(1)}, bf16[2048,256]{1,0:T(8,128)(2,1)}, u32[]{:S(2)}) copy-start(bf16[2048,256]{1,0:T(8,128)(2,1)} %refs_3_.3) | copy-start | bytes 3145732
  53.7 37.6 %collective-permute-start.10 = (bf16[2048,128]{1,0:T(8,128)(2,1)S(1)}, bf16[2048,128]{1,0:T(8,128)(2,1)S(1)}, u32[]{:S(2)}, u32[]{:S(2)}) collective-permute-start(bf16[2048,128]{1,0:T(8,128)(2,1)S(1)} %get-tuple-element.13), channel_id=1, source_target_pairs={{0,8},{8,0},{16,24},{24,16},{1,9},{9,1},{17,25},{25,17},{2,10},{10... | collective-permute-start | bytes 1572872 | tf_op jit(solution)/shard_map/ppermute | solution.py:215
  55.3 36.0 %collective-permute-start.9 = (bf16[2048,128]{1,0:T(8,128)(2,1)S(1)}, bf16[2048,128]{1,0:T(8,128)(2,1)S(1)}, u32[]{:S(2)}, u32[]{:S(2)}) collective-permute-start(bf16[2048,128]{1,0:T(8,128)(2,1)S(1)} %get-tuple-element.15), channel_id=1, source_target_pairs={{0,16},{8,24},{16,0},{24,8},{1,17},{9,25},{17,1},{25,9},{2,18},{10... | collective-permute-start | bytes 1572872 | tf_op jit(solution)/shard_map/ppermute | solution.py:215
  55.9 44.3 %collective-permute-start.4 = (bf16[2048,128]{1,0:T(8,128)(2,1)S(1)}, bf16[2048,128]{1,0:T(8,128)(2,1)S(1)}, u32[]{:S(2)}, u32[]{:S(2)}) collective-permute-start(bf16[2048,128]{1,0:T(8,128)(2,1)S(1)} %get-tuple-element.16), channel_id=1, source_target_pairs={{0,16},{8,24},{16,0},{24,8},{1,17},{9,25},{17,1},{25,9},{2,18},{10... | collective-permute-start | bytes 1572872 | tf_op jit(solution)/shard_map/ppermute | solution.py:215
  57.4 42.8 %collective-permute-start.6 = (bf16[2048,128]{1,0:T(8,128)(2,1)S(1)}, bf16[2048,128]{1,0:T(8,128)(2,1)S(1)}, u32[]{:S(2)}, u32[]{:S(2)}) collective-permute-start(bf16[2048,128]{1,0:T(8,128)(2,1)S(1)} %get-tuple-element.14), channel_id=1, source_target_pairs={{0,8},{8,0},{16,24},{24,16},{1,9},{9,1},{17,25},{25,17},{2,10},{10... | collective-permute-start | bytes 1572872 | tf_op jit(solution)/shard_map/ppermute | solution.py:215
  74.7 16.7 %copy-start.5 = (f32[2176,128]{1,0:T(8,128)S(1)}, f32[2176,128]{1,0:T(8,128)}, u32[]{:S(2)}) copy-start(f32[2176,128]{1,0:T(8,128)} %get-tuple-element.11.refs_2_) | copy-start | bytes 3342340
  74.7 16.7 %copy-start.6 = (f32[2176,128]{1,0:T(8,128)S(1)}, f32[2176,128]{1,0:T(8,128)}, u32[]{:S(2)}) copy-start(f32[2176,128]{1,0:T(8,128)} %get-tuple-element.12.refs_3_) | copy-start | bytes 3342340
  91.3 8.9 %copy-start.3 = (f32[2176,128]{1,0:T(8,128)S(1)}, f32[2176,128]{1,0:T(8,128)}, u32[]{:S(2)}) copy-start(f32[2176,128]{1,0:T(8,128)} %get-tuple-element.9.refs_2_) | copy-start | bytes 3342340
  91.3 8.9 %copy-start.4 = (f32[2176,128]{1,0:T(8,128)S(1)}, f32[2176,128]{1,0:T(8,128)}, u32[]{:S(2)}) copy-start(f32[2176,128]{1,0:T(8,128)} %get-tuple-element.10.refs_3_) | copy-start | bytes 3342340

commit v3 on v2

v3 whole, which is shorter than its diff:
```python
import functools

import jax
import jax.numpy as jnp
from jax import lax
from jax.experimental import pallas as pl
from jax.experimental.pallas import tpu as pltpu
from jax.sharding import PartitionSpec as P

DH = 64
BLK = 64
RAND = 3
LANES = 2 * DH
ROWS = 8
CHUNK = 2048
VMEM_BYTES = 16 * 1024 * 1024
EXP2_SCALE = 0.125 * 1.4426950408889634


def qk(q, k):
    return lax.dot_general(q, k, (((1,), (1,)), ((), ())), preferred_element_type=jnp.float32)


def part_kernel(
    pair, kind, wide, gpd, tokens, shared, lists_ref, flags_ref, glob_ref, own_ref, q_ref, *refs
):
    ranges = len(wide)
    blocks = tokens // BLK
    globs = gpd * ranges
    k_parts, v_parts, refs = refs[:ranges], refs[ranges : 2 * ranges], refs[2 * ranges :]
    if kind == "late":
        state_o_ref, state_l_ref = refs[:2]
        out_ref, k_glob, v_glob = refs[3:] if pair > 0 else refs[2:]
        k_all, v_all = k_parts[0], v_parts[0]
    else:
        if kind == "early":
            out_l_ref, refs = refs[1], refs[:1] + refs[2:]
        elif pair > 0:
            refs = refs[1:]
        out_ref, k_glob, v_glob, k_all, v_all, sems = refs
        copies = []
        for j in range(ranges):
            span = pl.ds(j * tokens, tokens)
            lanes = pl.ds(pair * LANES, LANES)
            for side, (source, target) in enumerate(((k_parts[j], k_all), (v_parts[j], v_all))):
                source = source.at[:, lanes] if wide[j][side] else source
                copies.append(pltpu.make_async_copy(source, target.at[span], sems.at[2 * j + side]))
        for copy in copies:
            copy.start()
        for copy in copies:
            copy.wait()

    first = lax.broadcasted_iota(jnp.int32, (BLK, LANES), 1) < DH
    first_few = lax.broadcasted_iota(jnp.int32, (16, LANES), 1) < DH
    block_ones = jnp.ones((BLK, LANES), jnp.bfloat16)

    def split_heads(q):
        zero = jnp.zeros_like(q)
        return [jnp.where(first, q, zero), jnp.where(first, zero, q)]

    def block(ref, position):
        return ref[pl.ds(pl.multiple_of(position * BLK, BLK), BLK), :]

    def listed(flag_a, flag_b):
        few = jnp.where(first_few, flag_a, flag_b).astype(jnp.bfloat16)
        return jnp.concatenate([few] * (BLK // 16), axis=0)

    def weighted(p, v, ones):
        return jnp.dot(
            p.astype(jnp.bfloat16), jnp.concatenate([v, ones], axis=1),
            preferred_element_type=jnp.float32,
        )

    def fold(rows):
        return jnp.where(first, rows[:BLK], rows[BLK:])

    def finish(b, target, peak, sums):
        o, total = fold(sums[:, :LANES]), fold(sums[:, LANES:])
        where = pl.ds(pl.multiple_of(target * BLK, BLK), BLK)
        if kind == "full":
            out_ref[where, :] = (o / total).astype(jnp.bfloat16)
            return
        top = fold(jnp.broadcast_to(peak, (2 * BLK, LANES))) * EXP2_SCALE
        if kind == "late":
            old_o, old_l = block(state_o_ref, b), block(state_l_ref, b)
            level = jnp.maximum(top, old_l)
            old_factor, factor = jnp.exp2(old_l - level), jnp.exp2(top - level)
            o = (old_o * old_factor + o * factor) / (old_factor + total * factor)
            out_ref[where, :] = o.astype(jnp.bfloat16)
        else:
            out_ref[where, :] = o / total
            out_l_ref[where, :] = top + jnp.log2(total)

    for g in range(globs):
        k_glob[g * BLK : (g + 1) * BLK, :] = block(k_all, glob_ref[g])
        v_glob[g * BLK : (g + 1) * BLK, :] = block(v_all, glob_ref[g])

    slots = shared + 2 * RAND

    def rows_step(step, carry):
        base = step * ROWS
        q_bd, k_lists, v_lists = [], [], []
        for u in range(ROWS):
            at = (base + u) * slots
            q_bd += split_heads(block(q_ref, base + u))
            k_list, v_list, one_list = [], [], []
            for j in range(shared + RAND):
                a, b = (at + j, at + j) if j < shared else (at + j, at + RAND + j)
                k, v = block(k_all, lists_ref[a]), block(v_all, lists_ref[a])
                if j >= shared:
                    k = jnp.where(first, k, block(k_all, lists_ref[b]))
                    v = jnp.where(first, v, block(v_all, lists_ref[b]))
                if kind == "full" or (kind == "early" and j == 1):
                    ones = block_ones
                else:
                    ones = listed(flags_ref[a], flags_ref[b])
                    v = v * ones
                k_list.append(k)
                v_list.append(v)
                one_list.append(ones)
            k_lists.append(jnp.concatenate(k_list, axis=0))
            v_lists.append((jnp.concatenate(v_list, axis=0), jnp.concatenate(one_list, axis=0)))
        q_bd = jnp.concatenate(q_bd, axis=0)
        parts = [slice(2 * BLK * u, 2 * BLK * (u + 1)) for u in range(ROWS)]
        s_own = jnp.concatenate([qk(q_bd[parts[u]], k_lists[u]) for u in range(ROWS)], axis=0)
        s_glob = qk(q_bd, k_glob[...])
        peak = jnp.maximum(
            jnp.max(s_own, axis=1, keepdims=True), jnp.max(s_glob, axis=1, keepdims=True)
        )
        w_own = jnp.exp2((s_own - peak) * EXP2_SCALE)
        w_glob = jnp.exp2((s_glob - peak) * EXP2_SCALE)
        sums_glob = weighted(w_glob, v_glob[...], jnp.ones((globs * BLK, LANES), jnp.bfloat16))
        for u in range(ROWS):
            sums = sums_glob[parts[u]] + weighted(w_own[parts[u]], *v_lists[u])
            finish(base + u, base + u, peak[parts[u]], sums)
        return carry

    lax.fori_loop(0, blocks // ROWS, rows_step, 0)

    q_glob = []
    for g in range(gpd):
        q_glob += split_heads(block(q_ref, own_ref[g]))
    q_glob = jnp.concatenate(q_glob, axis=0)
    chunk_ones = jnp.ones((CHUNK, LANES), jnp.bfloat16)

    def chunk_step(c, carry):
        peak, sums = carry
        span = pl.ds(pl.multiple_of(c * CHUNK, CHUNK), CHUNK)
        s = qk(q_glob, k_all[span, :])
        top = jnp.maximum(peak, jnp.max(s, axis=1, keepdims=True))
        w = jnp.exp2((s - top) * EXP2_SCALE)
        sums = sums * jnp.exp2((peak - top) * EXP2_SCALE) + weighted(w, v_all[span, :], chunk_ones)
        return top, sums

    height = 2 * gpd * BLK
    initial = (
        jnp.full((height, 1), -1e30, jnp.float32),
        jnp.zeros((height, 2 * LANES), jnp.float32),
    )
    peak, sums = lax.fori_loop(0, ranges * tokens // CHUNK, chunk_step, initial)
    for g in range(gpd):
        part = slice(2 * BLK * g, 2 * BLK * (g + 1))
        target = blocks + g if kind == "early" else own_ref[g]
        finish(blocks + g, target, peak[part], sums[part])


def part_call(
    pair, kind, shared, lists, flags, glob, own, queries, k_parts, v_parts, state=(), so_far=None
):
    tokens, columns = queries.shape
    ranges = len(k_parts)
    gpd = own.shape[0]
    smem = pl.BlockSpec(memory_space=pltpu.SMEM)
    hbm = pl.BlockSpec(memory_space=pl.ANY)
    half = pl.BlockSpec((tokens, LANES), lambda i: (0, pair))
    state_rows = tokens + gpd * BLK

    def full(rows):
        return pl.BlockSpec((rows, LANES), lambda i: (0, 0))

    operands = [lists, flags, glob, own, queries, *k_parts, *v_parts, *state]
    in_specs = [smem] * 4 + [half] + [full(tokens) if kind == "late" else hbm] * (2 * ranges)
    in_specs += [full(state_rows)] * len(state)
    aliases = {}
    if so_far is not None:
        aliases = {len(operands): 0}
        operands.append(so_far)
        in_specs.append(hbm)
    if kind == "early":
        out_specs = [full(state_rows)] * 2
        out_shape = [jax.ShapeDtypeStruct((state_rows, LANES), jnp.float32)] * 2
    else:
        out_specs = half
        out_shape = jax.ShapeDtypeStruct((tokens, columns), jnp.bfloat16)
    keys_all = ranges * tokens
    globs = gpd * ranges * BLK
    pairs_done = 2 * tokens * ((shared + RAND) * BLK + globs) + 2 * gpd * BLK * keys_all
    wide = tuple((k.shape[1] > LANES, v.shape[1] > LANES) for k, v in zip(k_parts, v_parts))
    scratch = [pltpu.VMEM((globs, LANES), jnp.bfloat16)] * 2
    if kind != "late":
        scratch += [pltpu.VMEM((keys_all, LANES), jnp.bfloat16)] * 2
        scratch.append(pltpu.SemaphoreType.DMA((2 * ranges,)))
    return pl.pallas_call(
        functools.partial(part_kernel, pair, kind, wide, gpd, tokens, shared),
        grid=(1,),
        in_specs=in_specs,
        out_specs=out_specs,
        out_shape=out_shape,
        input_output_aliases=aliases,
        scratch_shapes=scratch,
        compiler_params=pltpu.CompilerParams(vmem_limit_bytes=VMEM_BYTES + 8 * keys_all * LANES),
        cost_estimate=pl.CostEstimate(
            flops=16 * DH * pairs_done,
            bytes_accessed=4 * keys_all * LANES,
            transcendentals=pairs_done,
        ),
        name=kind,
    )(*operands)


def exchange(array, step):
    count = lax.axis_size("seq")
    return lax.ppermute(array, "seq", [(i, i ^ step) for i in range(count)])


def shards(queries, keys, values, rand_blocks, global_blocks):
    tokens, columns = queries.shape
    blocks = tokens // BLK
    gpd = global_blocks.shape[0]
    count = lax.axis_size("seq")
    rank = lax.axis_index("seq")
    pairs = columns // LANES
    steps = [1 << i for i in range(count.bit_length() - 1)]
    last = count - 1

    def place(ids):
        return ((ids // blocks) ^ rank) * blocks + ids % blocks

    row = jnp.arange(blocks)[:, None]
    window = place((rank * blocks + row + jnp.arange(-1, 2)) % (count * blocks))
    rand = place(rand_blocks)
    glob = jnp.concatenate([global_blocks] + [exchange(global_blocks, j) for j in range(1, count)])
    glob = place(glob)

    back = steps[::-1]
    k_first, v_first = exchange(keys, steps[0]), exchange(values, back[0])
    k_held, v_held, rand, window, glob = lax.optimization_barrier((keys, values, rand, window, glob))
    k_sent, v_sent = [], []
    for pair in range(pairs):
        lanes = slice(pair * LANES, (pair + 1) * LANES)
        k_parts = {0: k_held[:, lanes], steps[0]: k_first[:, lanes]}
        v_parts = {0: v_held[:, lanes], back[0]: v_first[:, lanes]}
        done = []
        for k_step, v_step in zip(steps[1:], back[1:]):
            for k_at, v_at in list(zip(k_parts, v_parts)):
                outgoing = (k_parts[k_at], v_parts[v_at])
                if pair > 0 and not done:
                    outgoing = lax.optimization_barrier(outgoing + (k_first, v_first))[:2]
                done.append((exchange(outgoing[0], k_step), exchange(outgoing[1], v_step)))
                k_parts[k_at ^ k_step], v_parts[v_at ^ v_step] = done[-1]
        k_parts.update({0: keys, steps[0]: k_first})
        v_parts.update({0: values, back[0]: v_first})
        k_sent.append([k_parts[at] for at in range(count)])
        v_sent.append([v_parts[at] for at in range(count)])

    own = global_blocks - rank * blocks

    def call(kind, pair, shared, listed, spare, start, stop, state=(), so_far=None):
        mine = rand[:, 2 * pair : 2 * pair + 2].reshape(blocks, 2 * RAND)
        lists = jnp.concatenate([listed, mine], axis=1)
        inside = (lists >= start * blocks) & (lists < stop * blocks)
        lists = jnp.where(inside, lists - start * blocks, spare)
        return part_call(
            pair, kind, shared, lists.reshape(-1), inside.astype(jnp.float32).reshape(-1),
            glob[gpd * start : gpd * stop] - start * blocks, own, queries,
            k_sent[pair][start:stop], v_sent[pair][start:stop], state, so_far,
        )

    out = None
    for pair in range(pairs - 1):
        out = call("full", pair, 3, window, row, 0, count, so_far=out)
    state = call("early", pairs - 1, 3, window, row, 0, last)
    halo = jnp.where(row == 0, window[:, :1], window[:, 2:])
    spare = glob[gpd * last] - last * blocks
    return call("late", pairs - 1, 1, halo, spare, last, count, state=state, so_far=out)


def solution(mesh):
    in_specs = (
        P(("batch", "seq"), "head"),
        P(("batch", "seq"), "head"),
        P(("batch", "seq"), "head"),
        P(("batch", "seq"), "head", None),
        P(("batch", "seq")),
    )
    out_specs = P(("batch", "seq"), "head")
    return jax.shard_map(shards, mesh=mesh, in_specs=in_specs, out_specs=out_specs, check_vma=False)
```

time: 109 us -> 101 us (0.927)
  Pallas kernels: 50.9 us -> 37 us
  local copies, waits for them, and re-layouts: 0.96 us -> 12.3 us
  waiting for transfers between devices: 41.2 us -> 32.8 us
  starting transfers between devices: 13.4 us -> 15.2 us
    pallas_call x4 -> x3, Pallas kernels: 50.9 us -> 37 us  [part_call(): pl.pallas_call(functools.partial(part_kernel, pair, kind, wide, gpd, toke...]
    ppermute x11 -> x13, waiting for transfers between devices: 41.2 us -> 32.8 us  [exchange(): return lax.ppermute(array, 'seq', [(i, i ^ step) for i in range(count)])]
    slice x5 -> x8, local copies, waits for them, and re-layouts: 0.15 us -> 7.09 us  [the longest x2 3.35 us: shards(): v_parts = {0: v_held[:, lanes], back[0]: v_first[:, lanes]}]
    unnamed x16 -> x18, local copies, waits for them, and re-layouts: 0.04 us -> 4.32 us
    ppermute x11 -> x13, starting transfers between devices: 13.4 us -> 15.2 us  [exchange(): return lax.ppermute(array, 'seq', [(i, i ^ step) for i in range(count)])]
  transfers between devices with their start and end apart: 11 -> 13, of which waited for: 1 -> 3; matrix products, arithmetic and copies ran while one was open for 3% -> 10% of each run, Pallas kernels for 39% -> 30%
where the time goes in v3:
time: 101 us; the launch traced here: 100 us
  Pallas kernels  37 us (37%)
  waiting for transfers between devices  32.8 us (32%)
  starting transfers between devices  15.2 us (15%)
  local copies, waits for them, and re-layouts  12.3 us (12%)
  other arithmetic  2.33 us (2%)
    pallas_call x3, Pallas kernels, part_call(): pl.pallas_call(functools.partial(part_kernel, pair, kind, wide, gpd, toke...  37 us
    ppermute x13, waiting for transfers between devices, exchange(): return lax.ppermute(array, 'seq', [(i, i ^ step) for i in range(count)])  32.8 us
    ppermute x13, starting transfers between devices, exchange(): return lax.ppermute(array, 'seq', [(i, i ^ step) for i in range(count)])  15.2 us
    unnamed x18, local copies, waits for them, and re-layouts  4.32 us
    slice x2, local copies, waits for them, and re-layouts, shards(): v_parts = {0: v_held[:, lanes], back[0]: v_first[:, lanes]}  3.35 us
    slice x2, local copies, waits for them, and re-layouts, shards(): k_parts = {0: k_held[:, lanes], steps[0]: k_first[:, lanes]}  3.14 us
  transfers between devices with their start and end apart: 13, of which 3 were waited for; matrix products, arithmetic and copies ran while one was open for 10% of the time, Pallas kernels for 30%

profile of v3, /device:TPU:0, one launch (start us, length us, event | category | flops | bytes accessed | tf_op | source)
XLA Modules:
  0.0 100.5 jit_solution(17973121999789043870)
XLA Ops:
  0.0 3.9 %collective-permute-start.2 = (s32[2]{0:T(128)}, s32[2]{0:T(128)S(1)}, u32[]{:S(2)}, u32[]{:S(2)}) collective-permute-start(s32[2]{0:T(128)} %param.9), channel_id=1, source_target_pairs={{0,24},{8,16},{16,8},{24,0},{1,25},{9,17},{17,9},{25,1},{2,26},{10... | collective-permute-start | bytes 32 | tf_op jit(solution)/shard_map/ppermute | solution.py:223
  4.5 2.0 %collective-permute-start.3 = (bf16[2048,256]{1,0:T(8,128)(2,1)}, bf16[2048,256]{1,0:T(8,128)(2,1)S(1)}, u32[]{:S(2)}, u32[]{:S(2)}) collective-permute-start(bf16[2048,256]{1,0:T(8,128)(2,1)} %refs_0_.3), channel_id=1, source_target_pairs={{0,8},{8,0},{16,24},{24,16},{1,9},{9,1},{17,25},{25,17},{2,10},{10... | collective-permute-start | bytes 3145736 | tf_op jit(solution)/shard_map/ppermute | solution.py:223
  6.4 1.5 %collective-permute-start.5 = (bf16[2048,256]{1,0:T(8,128)(2,1)}, bf16[2048,256]{1,0:T(8,128)(2,1)S(1)}, u32[]{:S(2)}, u32[]{:S(2)}) collective-permute-start(bf16[2048,256]{1,0:T(8,128)(2,1)} %refs_4_.1), channel_id=1, source_target_pairs={{0,16},{8,24},{16,0},{24,8},{1,17},{9,25},{17,1},{25,9},{2,18},{10... | collective-permute-start | bytes 3145736 | tf_op jit(solution)/shard_map/ppermute | solution.py:223
  7.9 0.7 broadcast_subtract_fusion.own_ref
  8.6 0.7 fusion.2
  9.6 0.7 fusion.12.glob_ref
  11.6 2.1 %fusion.20 = (bf16[2048,128]{1,0:T(8,128)(2,1)}, bf16[2048,128]{1,0:T(8,128)(2,1)S(1)}) fusion(bf16[2048,256]{1,0:T(8,128)(2,1)} %refs_0_.3), kind=kLoop, calls=%fused_computation.55 | loop fusion | bytes 2097152 | tf_op jit(solution)/shard_map/slice | solution.py:251
  14.2 1.1 %fusion.18 = (bf16[2048,128]{1,0:T(8,128)(2,1)}, bf16[2048,128]{1,0:T(8,128)(2,1)}) fusion(bf16[2048,256]{1,0:T(8,128)(2,1)S(1)} %copy-done.1), kind=kLoop, calls=%fused_computation.53 | loop fusion | bytes 2097152 | tf_op jit(solution)/shard_map/slice | solution.py:252
  16.1 14.7 %collective-permute-done.3.refs_1_ = bf16[2048,256]{1,0:T(8,128)(2,1)S(1)} collective-permute-done((bf16[2048,256]{1,0:T(8,128)(2,1)}, bf16[2048,256]{1,0:T(8,128)(2,1)S(1)}, u32[]{:S(2)}, u32[]{:S(2)}) %collective-permute-start.3) | collective-permute-done | bytes 1048608 | tf_op jit(solution)/shard_map/ppermute | solution.py:223
  30.8 2.0 %collective-permute-done.5.refs_5_.refs_6_ = bf16[2048,256]{1,0:T(8,128)(2,1)S(1)} collective-permute-done((bf16[2048,256]{1,0:T(8,128)(2,1)}, bf16[2048,256]{1,0:T(8,128)(2,1)S(1)}, u32[]{:S(2)}, u32[]{:S(2)}) %collective-permute-start.5) | collective-permute-done | bytes 1048608 | tf_op jit(solution)/shard_map/ppermute | solution.py:223
  32.7 1.5 %collective-permute-start.7 = (bf16[2048,128]{1,0:T(8,128)(2,1)S(1)}, bf16[2048,128]{1,0:T(8,128)(2,1)S(1)}, u32[]{:S(2)}, u32[]{:S(2)}) collective-permute-start(bf16[2048,128]{1,0:T(8,128)(2,1)S(1)} %get-tuple-element.19), channel_id=1, source_target_pairs={{0,16},{8,24},{16,0},{24,8},{1,17},{9,25},{17,1},{25,9},{2,18},{10... | collective-permute-start | bytes 1572872 | tf_op jit(solution)/shard_map/ppermute | solution.py:223
  34.3 1.1 %fusion.19 = (bf16[2048,128]{1,0:T(8,128)(2,1)}, bf16[2048,128]{1,0:T(8,128)(2,1)}) fusion(bf16[2048,256]{1,0:T(8,128)(2,1)S(1)} %collective-permute-done.3.refs_1_), kind=kLoop, calls=%fused_computation.54 | loop fusion | bytes 2097152 | tf_op jit(solution)/shard_map/slice | solution.py:251
  35.3 1.0 collective-permute-start.10
  36.8 2.3 %fusion.17 = (bf16[2048,128]{1,0:T(8,128)(2,1)}, bf16[2048,128]{1,0:T(8,128)(2,1)}) fusion(bf16[2048,256]{1,0:T(8,128)(2,1)} %copy-done.2), kind=kLoop, calls=%fused_computation.52 | loop fusion | bytes 2097152 | tf_op jit(solution)/shard_map/slice | solution.py:252
  39.1 16.1 %collective-permute-done.7.refs_2_ = bf16[2048,128]{1,0:T(8,128)(2,1)S(1)} collective-permute-done((bf16[2048,128]{1,0:T(8,128)(2,1)S(1)}, bf16[2048,128]{1,0:T(8,128)(2,1)S(1)}, u32[]{:S(2)}, u32[]{:S(2)}) %collective-permute-start.7) | collective-permute-done | bytes 524320 | tf_op jit(solution)/shard_map/ppermute | solution.py:223
  55.2 0.8 copy-done.6
  56.3 2.1 %collective-permute-start.4 = (bf16[2048,128]{1,0:T(8,128)(2,1)}, bf16[2048,128]{1,0:T(8,128)(2,1)S(1)}, u32[]{:S(2)}, u32[]{:S(2)}) collective-permute-start(bf16[2048,128]{1,0:T(8,128)(2,1)} %get-tuple-element.28), channel_id=1, source_target_pairs={{0,16},{8,24},{16,0},{24,8},{1,17},{9,25},{17,1},{25,9},{2,18},{10... | collective-permute-start | bytes 1572872 | tf_op jit(solution)/shard_map/ppermute | solution.py:223
  58.4 1.2 %copy-done.3 = bf16[2048,256]{1,0:T(8,128)(2,1)S(1)} copy-done((bf16[2048,256]{1,0:T(8,128)(2,1)S(1)}, bf16[2048,256]{1,0:T(8,128)(2,1)}, u32[]{:S(2)}) %copy-start.3) | copy-done | bytes 1048600
  59.6 1.2 %copy-done.5 = bf16[2048,256]{1,0:T(8,128)(2,1)S(1)} copy-done((bf16[2048,256]{1,0:T(8,128)(2,1)S(1)}, bf16[2048,256]{1,0:T(8,128)(2,1)}, u32[]{:S(2)}) %copy-start.5) | copy-done | bytes 1048600
  60.8 1.0 %copy-done.7 = bf16[2048,128]{1,0:T(8,128)(2,1)S(1)} copy-done((bf16[2048,128]{1,0:T(8,128)(2,1)S(1)}, bf16[2048,128]{1,0:T(8,128)(2,1)}, u32[]{:S(2)}) %copy-start.7) | copy-done | bytes 524312
  61.9 12.9 %early.1 = (f32[2176,128]{1,0:T(8,128)S(1)}, f32[2176,128]{1,0:T(8,128)S(1)}) custom-call(s32[288]{0:T(512)S(1)} %get-tuple-element.34.lists_ref, f32[288]{0:T(512)S(1)} %fusion.13.flags_ref, s32[6]{0:T(128)S(1)} %bitcast.6, s32[2]{0:T(128)S(1)} %broadcast_subtract_fusion.own_ref, bf16[2048,256]{1,0:T(8,128)(2,1)S(1)} %copy-done.5, ...), custom_call_target="tpu_custom_call" | custom-call | flops 4831838208 | bytes 3145728 | tf_op jit(solution)/shard_map/early/pallas_call | solution.py:203
  74.8 1.6 %collective-permute-start.6 = (bf16[2048,128]{1,0:T(8,128)(2,1)S(1)}, bf16[2048,128]{1,0:T(8,128)(2,1)S(1)}, u32[]{:S(2)}, u32[]{:S(2)}) collective-permute-start(bf16[2048,128]{1,0:T(8,128)(2,1)S(1)} %copy-done.8), channel_id=1, source_target_pairs={{0,8},{8,0},{16,24},{24,16},{1,9},{9,1},{17,25},{25,17},{2,10},{10... | collective-permute-start | bytes 1572872 | tf_op jit(solution)/shard_map/ppermute | solution.py:223
  76.4 16.8 %full.1.refs_4_ = bf16[2048,256]{1,0:T(8,128)(2,1)} custom-call(s32[288]{0:T(512)S(1)} %get-tuple-element.33.lists_ref, f32[288]{0:T(512)S(1)} %fusion.15.flags_ref, s32[8]{0:T(128)S(1)} %fusion.12.glob_ref, s32[2]{0:T(128)S(1)} %broadcast_subtract_fusion.own_ref, bf16[2048,256]{1,0:T(8,128)(2,1)S(1)} %copy-done.5, bf16[2048,256]{1,0:T(8,128)(2,1)S(1)} %copy-done, ...), custom_call_target="tpu_custom_call" | custom-call | flops 5905580032 | bytes 4194304 | tf_op jit(solution)/shard_map/full/pallas_call | solution.py:203
  93.2 7.3 %late.1 = bf16[2048,256]{1,0:T(8,128)(2,1)} custom-call(s32[224]{0:T(256)S(1)} %select_n.68.lists_ref, f32[224]{0:T(256)S(1)} %reshape.53.flags_ref, s32[2]{0:T(128)S(1)} %slice_add_fusion.glob_ref, s32[2]{0:T(128)S(1)} %broadcast_subtract_fusion.own_ref, bf16[2048,256]{1,0:T(8,128)(2,1)S(1)} %copy-done.5, ...), custom_call_target="tpu_custom_call", output_to_operand_aliasing={{}: (9, {})} | custom-call | flops 2147483648 | bytes 1048576 | tf_op jit(solution)/shard_map/late/pallas_call | solution.py:203
  (57 shorter events, 3.5 us)
Async XLA Ops:
  0.0 9.5 %collective-permute-start.2 = (s32[2]{0:T(128)}, s32[2]{0:T(128)S(1)}, u32[]{:S(2)}, u32[]{:S(2)}) collective-permute-start(s32[2]{0:T(128)} %param.9), channel_id=1, source_target_pairs={{0,24},{8,16},{16,8},{24,0},{1,25},{9,17},{17,9},{25,1},{2,26},{10... | collective-permute-start | bytes 32 | tf_op jit(solution)/shard_map/ppermute | solution.py:223
  3.9 5.6 %collective-permute-start.1 = (s32[2]{0:T(128)}, s32[2]{0:T(128)S(1)}, u32[]{:S(2)}, u32[]{:S(2)}) collective-permute-start(s32[2]{0:T(128)} %param.9), channel_id=1, source_target_pairs={{0,16},{8,24},{16,0},{24,8},{1,17},{9,25},{17,1},{25,9},{2,18},{10... | collective-permute-start | bytes 32 | tf_op jit(solution)/shard_map/ppermute | solution.py:223
  4.4 5.2 %collective-permute-start = (s32[2]{0:T(128)}, s32[2]{0:T(128)S(1)}, u32[]{:S(2)}, u32[]{:S(2)}) collective-permute-start(s32[2]{0:T(128)} %param.9), channel_id=1, source_target_pairs={{0,8},{8,0},{16,24},{24,16},{1,9},{9,1},{17,25},{25,17},{2,10},{10... | collective-permute-start | bytes 32 | tf_op jit(solution)/shard_map/ppermute | solution.py:223
  4.5 26.3 %collective-permute-start.3 = (bf16[2048,256]{1,0:T(8,128)(2,1)}, bf16[2048,256]{1,0:T(8,128)(2,1)S(1)}, u32[]{:S(2)}, u32[]{:S(2)}) collective-permute-start(bf16[2048,256]{1,0:T(8,128)(2,1)} %refs_0_.3), channel_id=1, source_target_pairs={{0,8},{8,0},{16,24},{24,16},{1,9},{9,1},{17,25},{25,17},{2,10},{10... | collective-permute-start | bytes 3145736 | tf_op jit(solution)/shard_map/ppermute | solution.py:223
  6.4 26.3 %collective-permute-start.5 = (bf16[2048,256]{1,0:T(8,128)(2,1)}, bf16[2048,256]{1,0:T(8,128)(2,1)S(1)}, u32[]{:S(2)}, u32[]{:S(2)}) collective-permute-start(bf16[2048,256]{1,0:T(8,128)(2,1)} %refs_4_.1), channel_id=1, source_target_pairs={{0,16},{8,24},{16,0},{24,8},{1,17},{9,25},{17,1},{25,9},{2,18},{10... | collective-permute-start | bytes 3145736 | tf_op jit(solution)/shard_map/ppermute | solution.py:223
  11.0 3.2 %copy-start.1 = (bf16[2048,256]{1,0:T(8,128)(2,1)S(1)}, bf16[2048,256]{1,0:T(8,128)(2,1)}, u32[]{:S(2)}) copy-start(bf16[2048,256]{1,0:T(8,128)(2,1)} %refs_4_.1) | copy-start | bytes 3145732
  13.7 61.2 %collective-permute-start.9 = (bf16[2048,128]{1,0:T(8,128)(2,1)}, bf16[2048,128]{1,0:T(8,128)(2,1)}, u32[]{:S(2)}, u32[]{:S(2)}) collective-permute-start(bf16[2048,128]{1,0:T(8,128)(2,1)} %get-tuple-element.29), channel_id=1, source_target_pairs={{0,16},{8,24},{16,0},{24,8},{1,17},{9,25},{17,1},{25,9},{2,18},{10... | collective-permute-start | bytes 1572872 | tf_op jit(solution)/shard_map/ppermute | solution.py:223
  15.2 61.1 %collective-permute-start.11 = (bf16[2048,128]{1,0:T(8,128)(2,1)}, bf16[2048,128]{1,0:T(8,128)(2,1)}, u32[]{:S(2)}, u32[]{:S(2)}) collective-permute-start(bf16[2048,128]{1,0:T(8,128)(2,1)} %get-tuple-element.25), channel_id=1, source_target_pairs={{0,8},{8,0},{16,24},{24,16},{1,9},{9,1},{17,25},{25,17},{2,10},{10... | collective-permute-start | bytes 1572872 | tf_op jit(solution)/shard_map/ppermute | solution.py:223
  32.7 1.5 %copy-start.2 = (bf16[2048,256]{1,0:T(8,128)(2,1)}, bf16[2048,256]{1,0:T(8,128)(2,1)S(1)}, u32[]{:S(2)}) copy-start(bf16[2048,256]{1,0:T(8,128)(2,1)S(1)} %collective-permute-done.5.refs_5_.refs_6_) | copy-start | bytes 3145732
  32.7 22.5 %collective-permute-start.7 = (bf16[2048,128]{1,0:T(8,128)(2,1)S(1)}, bf16[2048,128]{1,0:T(8,128)(2,1)S(1)}, u32[]{:S(2)}, u32[]{:S(2)}) collective-permute-start(bf16[2048,128]{1,0:T(8,128)(2,1)S(1)} %get-tuple-element.19), channel_id=1, source_target_pairs={{0,16},{8,24},{16,0},{24,8},{1,17},{9,25},{17,1},{25,9},{2,18},{10... | collective-permute-start | bytes 1572872 | tf_op jit(solution)/shard_map/ppermute | solution.py:223
  35.3 23.0 %copy-start = (bf16[2048,256]{1,0:T(8,128)(2,1)S(1)}, bf16[2048,256]{1,0:T(8,128)(2,1)}, u32[]{:S(2)}) copy-start(bf16[2048,256]{1,0:T(8,128)(2,1)} %refs_0_.3) | copy-start | bytes 3145732
  35.3 41.0 %collective-permute-start.10 = (bf16[2048,128]{1,0:T(8,128)(2,1)}, bf16[2048,128]{1,0:T(8,128)(2,1)}, u32[]{:S(2)}, u32[]{:S(2)}) collective-permute-start(bf16[2048,128]{1,0:T(8,128)(2,1)} %get-tuple-element.27), channel_id=1, source_target_pairs={{0,16},{8,24},{16,0},{24,8},{1,17},{9,25},{17,1},{25,9},{2,18},{10... | collective-permute-start | bytes 1572872 | tf_op jit(solution)/shard_map/ppermute | solution.py:223
  36.3 20.0 %collective-permute-start.8 = (bf16[2048,128]{1,0:T(8,128)(2,1)}, bf16[2048,128]{1,0:T(8,128)(2,1)}, u32[]{:S(2)}, u32[]{:S(2)}) collective-permute-start(bf16[2048,128]{1,0:T(8,128)(2,1)} %get-tuple-element.20), channel_id=1, source_target_pairs={{0,8},{8,0},{16,24},{24,16},{1,9},{9,1},{17,25},{25,17},{2,10},{10... | collective-permute-start | bytes 1572872 | tf_op jit(solution)/shard_map/ppermute | solution.py:223
  55.2 0.8 copy-start.6
  56.0 20.4 %collective-permute-start.12 = (bf16[2048,128]{1,0:T(8,128)(2,1)}, bf16[2048,128]{1,0:T(8,128)(2,1)}, u32[]{:S(2)}, u32[]{:S(2)}) collective-permute-start(bf16[2048,128]{1,0:T(8,128)(2,1)} %get-tuple-element.23), channel_id=1, source_target_pairs={{0,8},{8,0},{16,24},{24,16},{1,9},{9,1},{17,25},{25,17},{2,10},{10... | collective-permute-start | bytes 1572872 | tf_op jit(solution)/shard_map/ppermute | solution.py:223
  56.3 36.9 %collective-permute-start.4 = (bf16[2048,128]{1,0:T(8,128)(2,1)}, bf16[2048,128]{1,0:T(8,128)(2,1)S(1)}, u32[]{:S(2)}, u32[]{:S(2)}) collective-permute-start(bf16[2048,128]{1,0:T(8,128)(2,1)} %get-tuple-element.28), channel_id=1, source_target_pairs={{0,16},{8,24},{16,0},{24,8},{1,17},{9,25},{17,1},{25,9},{2,18},{10... | collective-permute-start | bytes 1572872 | tf_op jit(solution)/shard_map/ppermute | solution.py:223
  58.4 1.2 %copy-start.3 = (bf16[2048,256]{1,0:T(8,128)(2,1)S(1)}, bf16[2048,256]{1,0:T(8,128)(2,1)}, u32[]{:S(2)}) copy-start(bf16[2048,256]{1,0:T(8,128)(2,1)} %copy-done.2) | copy-start | bytes 3145732
  59.6 1.2 %copy-start.5 = (bf16[2048,256]{1,0:T(8,128)(2,1)S(1)}, bf16[2048,256]{1,0:T(8,128)(2,1)}, u32[]{:S(2)}) copy-start(bf16[2048,256]{1,0:T(8,128)(2,1)} %q_ref.5) | copy-start | bytes 3145732
  60.8 1.0 %copy-start.7 = (bf16[2048,128]{1,0:T(8,128)(2,1)S(1)}, bf16[2048,128]{1,0:T(8,128)(2,1)}, u32[]{:S(2)}) copy-start(bf16[2048,128]{1,0:T(8,128)(2,1)} %copy-done.6) | copy-start | bytes 1572868
  61.9 13.0 %copy-start.8 = (bf16[2048,128]{1,0:T(8,128)(2,1)S(1)}, bf16[2048,128]{1,0:T(8,128)(2,1)}, u32[]{:S(2)}) copy-start(bf16[2048,128]{1,0:T(8,128)(2,1)} %get-tuple-element.24) | copy-start | bytes 1572868
  61.9 14.5 %copy-start.4 = (bf16[2048,256]{1,0:T(8,128)(2,1)S(1)}, bf16[2048,256]{1,0:T(8,128)(2,1)}, u32[]{:S(2)}) copy-start(bf16[2048,256]{1,0:T(8,128)(2,1)} %copy-done.2) | copy-start | bytes 3145732
  74.8 18.4 %collective-permute-start.6 = (bf16[2048,128]{1,0:T(8,128)(2,1)S(1)}, bf16[2048,128]{1,0:T(8,128)(2,1)S(1)}, u32[]{:S(2)}, u32[]{:S(2)}) collective-permute-start(bf16[2048,128]{1,0:T(8,128)(2,1)S(1)} %copy-done.8), channel_id=1, source_target_pairs={{0,8},{8,0},{16,24},{24,16},{1,9},{9,1},{17,25},{25,17},{2,10},{10... | collective-permute-start | bytes 1572872 | tf_op jit(solution)/shard_map/ppermute | solution.py:223

commit v4 on v3

--- a/solution.py
+++ b/solution.py
@@ -13,6 +13,7 @@
 LANES = 2 * DH
 ROWS = 8
 CHUNK = 2048
+SUBS = 2
 VMEM_BYTES = 16 * 1024 * 1024
 EXP2_SCALE = 0.125 * 1.4426950408889634
 
@@ -97,42 +98,38 @@
 
     slots = shared + 2 * RAND
 
+    glob_ones = jnp.ones((globs * BLK, LANES), jnp.bfloat16)
+
+    def scores(row):
+        at = row * slots
+        q_bd = jnp.concatenate(split_heads(block(q_ref, row)), axis=0)
+        k_list, v_list, one_list = [], [], []
+        for j in range(shared + RAND):
+            a, b = (at + j, at + j) if j < shared else (at + j, at + RAND + j)
+            k, v = block(k_all, lists_ref[a]), block(v_all, lists_ref[a])
+            if j >= shared:
+                k = jnp.where(first, k, block(k_all, lists_ref[b]))
+                v = jnp.where(first, v, block(v_all, lists_ref[b]))
+            if kind == "full" or (kind == "early" and j == 1):
+                ones = block_ones
+            else:
+                ones = listed(flags_ref[a], flags_ref[b])
+                v = v * ones
+            k_list.append(k)
+            v_list.append(v)
+            one_list.append(ones)
+        s = qk(q_bd, jnp.concatenate(k_list + [k_glob[...]], axis=0))
+        v = jnp.concatenate(v_list + [v_glob[...]], axis=0)
+        return s, v, jnp.concatenate(one_list + [glob_ones], axis=0)
+
     def rows_step(step, carry):
         base = step * ROWS
-        q_bd, k_lists, v_lists = [], [], []
+        ahead = scores(base)
         for u in range(ROWS):
-            at = (base + u) * slots
-            q_bd += split_heads(block(q_ref, base + u))
-            k_list, v_list, one_list = [], [], []
-            for j in range(shared + RAND):
-                a, b = (at + j, at + j) if j < shared else (at + j, at + RAND + j)
-                k, v = block(k_all, lists_ref[a]), block(v_all, lists_ref[a])
-                if j >= shared:
-                    k = jnp.where(first, k, block(k_all, lists_ref[b]))
-                    v = jnp.where(first, v, block(v_all, lists_ref[b]))
-                if kind == "full" or (kind == "early" and j == 1):
-                    ones = block_ones
-                else:
-                    ones = listed(flags_ref[a], flags_ref[b])
-                    v = v * ones
-                k_list.append(k)
-                v_list.append(v)
-                one_list.append(ones)
-            k_lists.append(jnp.concatenate(k_list, axis=0))
-            v_lists.append((jnp.concatenate(v_list, axis=0), jnp.concatenate(one_list, axis=0)))
-        q_bd = jnp.concatenate(q_bd, axis=0)
-        parts = [slice(2 * BLK * u, 2 * BLK * (u + 1)) for u in range(ROWS)]
-        s_own = jnp.concatenate([qk(q_bd[parts[u]], k_lists[u]) for u in range(ROWS)], axis=0)
-        s_glob = qk(q_bd, k_glob[...])
-        peak = jnp.maximum(
-            jnp.max(s_own, axis=1, keepdims=True), jnp.max(s_glob, axis=1, keepdims=True)
-        )
-        w_own = jnp.exp2((s_own - peak) * EXP2_SCALE)
-        w_glob = jnp.exp2((s_glob - peak) * EXP2_SCALE)
-        sums_glob = weighted(w_glob, v_glob[...], jnp.ones((globs * BLK, LANES), jnp.bfloat16))
-        for u in range(ROWS):
-            sums = sums_glob[parts[u]] + weighted(w_own[parts[u]], *v_lists[u])
-            finish(base + u, base + u, peak[parts[u]], sums)
+            (s, v, ones), ahead = ahead, scores(base + u + 1) if u + 1 < ROWS else None
+            peak = jnp.max(s, axis=1, keepdims=True)
+            w = jnp.exp2((s - peak) * EXP2_SCALE)
+            finish(base + u, base + u, peak, weighted(w, v, ones))
         return carry
 
     lax.fori_loop(0, blocks // ROWS, rows_step, 0)
@@ -141,16 +138,21 @@
     for g in range(gpd):
         q_glob += split_heads(block(q_ref, own_ref[g]))
     q_glob = jnp.concatenate(q_glob, axis=0)
-    chunk_ones = jnp.ones((CHUNK, LANES), jnp.bfloat16)
+    chunk_ones = jnp.ones((CHUNK // SUBS, LANES), jnp.bfloat16)
 
     def chunk_step(c, carry):
         peak, sums = carry
-        span = pl.ds(pl.multiple_of(c * CHUNK, CHUNK), CHUNK)
-        s = qk(q_glob, k_all[span, :])
-        top = jnp.maximum(peak, jnp.max(s, axis=1, keepdims=True))
-        w = jnp.exp2((s - top) * EXP2_SCALE)
-        sums = sums * jnp.exp2((peak - top) * EXP2_SCALE) + weighted(w, v_all[span, :], chunk_ones)
-        return top, sums
+        size = CHUNK // SUBS
+        spans = [pl.ds(pl.multiple_of(c * CHUNK + i * size, size), size) for i in range(SUBS)]
+        ahead = qk(q_glob, k_all[spans[0], :])
+        for i in range(SUBS):
+            s, ahead = ahead, qk(q_glob, k_all[spans[i + 1], :]) if i + 1 < SUBS else None
+            top = jnp.maximum(peak, jnp.max(s, axis=1, keepdims=True))
+            w = jnp.exp2((s - top) * EXP2_SCALE)
+            factor = jnp.exp2((peak - top) * EXP2_SCALE)
+            sums = sums * factor + weighted(w, v_all[spans[i], :], chunk_ones)
+            peak = top
+        return peak, sums
 
     height = 2 * gpd * BLK
     initial = (
@@ -254,14 +256,16 @@
         for k_step, v_step in zip(steps[1:], back[1:]):
             for k_at, v_at in list(zip(k_parts, v_parts)):
                 outgoing = (k_parts[k_at], v_parts[v_at])
-                if pair > 0 and not done:
-                    outgoing = lax.optimization_barrier(outgoing + (k_first, v_first))[:2]
+                if pair > 0:
+                    gate = before[len(done)] if done else (k_first, v_first)
+                    outgoing = lax.optimization_barrier(outgoing + gate)[:2]
                 done.append((exchange(outgoing[0], k_step), exchange(outgoing[1], v_step)))
                 k_parts[k_at ^ k_step], v_parts[v_at ^ v_step] = done[-1]
         k_parts.update({0: keys, steps[0]: k_first})
         v_parts.update({0: values, back[0]: v_first})
         k_sent.append([k_parts[at] for at in range(count)])
         v_sent.append([v_parts[at] for at in range(count)])
+        before = done
 
     own = global_blocks - rank * blocks
 
@@ -279,6 +283,7 @@
     out = None
     for pair in range(pairs - 1):
         out = call("full", pair, 3, window, row, 0, count, so_far=out)
+    window = lax.optimization_barrier((window, out))[0]
     state = call("early", pairs - 1, 3, window, row, 0, last)
     halo = jnp.where(row == 0, window[:, :1], window[:, 2:])
     spare = glob[gpd * last] - last * blocks

time: 101 us -> 92.8 us (0.919)
  Pallas kernels: 37 us -> 31.8 us
  local copies, waits for them, and re-layouts: 12.3 us -> 10.5 us
    pallas_call x3, Pallas kernels: 37 us -> 31.8 us  [part_call(): pl.pallas_call(functools.partial(part_kernel, pair, kind, wide, gpd, toke...]
    unnamed x18 -> x8, local copies, waits for them, and re-layouts: 4.32 us -> 2.45 us
  transfers between devices with their start and end apart: 13 -> 13, of which waited for: 3 -> 3; matrix products, arithmetic and copies ran while one was open for 10% -> 11% of each run, Pallas kernels for 30% -> 26%
where the time goes in v4:
time: 92.8 us; the launch traced here: 92.4 us
  waiting for transfers between devices  32 us (34%)
  Pallas kernels  31.8 us (34%)
  starting transfers between devices  14.8 us (16%)
  local copies, waits for them, and re-layouts  10.5 us (11%)
  other arithmetic  2.35 us (3%)
    ppermute x13, waiting for transfers between devices, exchange(): return lax.ppermute(array, 'seq', [(i, i ^ step) for i in range(count)])  32 us
    pallas_call x3, Pallas kernels, part_call(): pl.pallas_call(functools.partial(part_kernel, pair, kind, wide, gpd, toke...  31.8 us
    ppermute x13, starting transfers between devices, exchange(): return lax.ppermute(array, 'seq', [(i, i ^ step) for i in range(count)])  14.8 us
    slice x2, local copies, waits for them, and re-layouts, shards(): v_parts = {0: v_held[:, lanes], back[0]: v_first[:, lanes]}  3.28 us
    slice x2, local copies, waits for them, and re-layouts, shards(): k_parts = {0: k_held[:, lanes], steps[0]: k_first[:, lanes]}  3.28 us
    unnamed x8, local copies, waits for them, and re-layouts  2.45 us
  transfers between devices with their start and end apart: 13, of which 3 were waited for; matrix products, arithmetic and copies ran while one was open for 11% of the time, Pallas kernels for 26%

profile of v4, /device:TPU:0, one launch (start us, length us, event | category | flops | bytes accessed | tf_op | source)
XLA Modules:
  0.0 92.4 jit_solution(4172430870527379727)
XLA Ops:
  0.0 3.9 %collective-permute-start.2 = (s32[2]{0:T(128)}, s32[2]{0:T(128)S(1)}, u32[]{:S(2)}, u32[]{:S(2)}) collective-permute-start(s32[2]{0:T(128)} %param.9), channel_id=1, source_target_pairs={{0,24},{8,16},{16,8},{24,0},{1,25},{9,17},{17,9},{25,1},{2,26},{10... | collective-permute-start | bytes 32 | tf_op jit(solution)/shard_map/ppermute | solution.py:225
  4.5 1.9 %collective-permute-start.3 = (bf16[2048,256]{1,0:T(8,128)(2,1)}, bf16[2048,256]{1,0:T(8,128)(2,1)S(1)}, u32[]{:S(2)}, u32[]{:S(2)}) collective-permute-start(bf16[2048,256]{1,0:T(8,128)(2,1)} %refs_0_.3), channel_id=1, source_target_pairs={{0,8},{8,0},{16,24},{24,16},{1,9},{9,1},{17,25},{25,17},{2,10},{10... | collective-permute-start | bytes 3145736 | tf_op jit(solution)/shard_map/ppermute | solution.py:225
  6.4 1.5 %collective-permute-start.7 = (bf16[2048,256]{1,0:T(8,128)(2,1)}, bf16[2048,256]{1,0:T(8,128)(2,1)}, u32[]{:S(2)}, u32[]{:S(2)}) collective-permute-start(bf16[2048,256]{1,0:T(8,128)(2,1)} %refs_3_.1), channel_id=1, source_target_pairs={{0,16},{8,24},{16,0},{24,8},{1,17},{9,25},{17,1},{25,9},{2,18},{10... | collective-permute-start | bytes 3145736 | tf_op jit(solution)/shard_map/ppermute | solution.py:225
  8.0 0.7 broadcast_subtract_fusion.own_ref
  8.6 0.7 fusion.2
  9.6 0.7 fusion.12.glob_ref
  10.4 2.2 %fusion.18 = (bf16[2048,128]{1,0:T(8,128)(2,1)}, bf16[2048,128]{1,0:T(8,128)(2,1)}) fusion(bf16[2048,256]{1,0:T(8,128)(2,1)} %refs_0_.3), kind=kLoop, calls=%fused_computation.53 | loop fusion | bytes 2097152 | tf_op jit(solution)/shard_map/slice | solution.py:253
  13.1 1.1 %fusion.17 = (bf16[2048,128]{1,0:T(8,128)(2,1)}, bf16[2048,128]{1,0:T(8,128)(2,1)}) fusion(bf16[2048,256]{1,0:T(8,128)(2,1)S(1)} %copy-done.1), kind=kLoop, calls=%fused_computation.52 | loop fusion | bytes 2097152 | tf_op jit(solution)/shard_map/slice | solution.py:254
  14.3 0.6 slice.54
  15.0 15.8 %collective-permute-done.3.refs_1_ = bf16[2048,256]{1,0:T(8,128)(2,1)S(1)} collective-permute-done((bf16[2048,256]{1,0:T(8,128)(2,1)}, bf16[2048,256]{1,0:T(8,128)(2,1)S(1)}, u32[]{:S(2)}, u32[]{:S(2)}) %collective-permute-start.3) | collective-permute-done | bytes 1048608 | tf_op jit(solution)/shard_map/ppermute | solution.py:225
  30.8 1.0 %fusion.20 = (bf16[2048,128]{1,0:T(8,128)(2,1)}, bf16[2048,128]{1,0:T(8,128)(2,1)}) fusion(bf16[2048,256]{1,0:T(8,128)(2,1)S(1)} %collective-permute-done.3.refs_1_), kind=kLoop, calls=%fused_computation.55 | loop fusion | bytes 2097152 | tf_op jit(solution)/shard_map/slice | solution.py:253
  31.9 1.9 %collective-permute-start.5 = (bf16[2048,128]{1,0:T(8,128)(2,1)}, bf16[2048,128]{1,0:T(8,128)(2,1)}, u32[]{:S(2)}, u32[]{:S(2)}) collective-permute-start(bf16[2048,128]{1,0:T(8,128)(2,1)} %get-tuple-element.36), channel_id=1, source_target_pairs={{0,16},{8,24},{16,0},{24,8},{1,17},{9,25},{17,1},{25,9},{2,18},{10... | collective-permute-start | bytes 1572872 | tf_op jit(solution)/shard_map/ppermute | solution.py:225
  33.8 2.2 %fusion.19 = (bf16[2048,128]{1,0:T(8,128)(2,1)}, bf16[2048,128]{1,0:T(8,128)(2,1)}) fusion(bf16[2048,256]{1,0:T(8,128)(2,1)} %collective-permute-done.7.refs_6_.refs_5_), kind=kLoop, calls=%fused_computation.54 | loop fusion | bytes 2097152 | tf_op jit(solution)/shard_map/slice | solution.py:254
  36.0 1.5 %collective-permute-start.8 = (bf16[2048,128]{1,0:T(8,128)(2,1)}, bf16[2048,128]{1,0:T(8,128)(2,1)}, u32[]{:S(2)}, u32[]{:S(2)}) collective-permute-start(bf16[2048,128]{1,0:T(8,128)(2,1)} %get-tuple-element.34), channel_id=1, source_target_pairs={{0,8},{8,0},{16,24},{24,16},{1,9},{9,1},{17,25},{25,17},{2,10},{10... | collective-permute-start | bytes 1572872 | tf_op jit(solution)/shard_map/ppermute | solution.py:225
  38.4 0.6 collective-permute-start.11
  39.0 5.1 %collective-permute-done.4.refs_2_ = bf16[2048,128]{1,0:T(8,128)(2,1)} collective-permute-done((bf16[2048,128]{1,0:T(8,128)(2,1)}, bf16[2048,128]{1,0:T(8,128)(2,1)}, u32[]{:S(2)}, u32[]{:S(2)}) %collective-permute-start.4) | collective-permute-done | bytes 524320 | tf_op jit(solution)/shard_map/ppermute | solution.py:225
  44.2 11.1 %collective-permute-done.5.refs_3_ = bf16[2048,128]{1,0:T(8,128)(2,1)} collective-permute-done((bf16[2048,128]{1,0:T(8,128)(2,1)}, bf16[2048,128]{1,0:T(8,128)(2,1)}, u32[]{:S(2)}, u32[]{:S(2)}) %collective-permute-start.5) | collective-permute-done | bytes 524320 | tf_op jit(solution)/shard_map/ppermute | solution.py:225
  55.3 1.2 %copy-done.2 = bf16[2048,256]{1,0:T(8,128)(2,1)S(1)} copy-done((bf16[2048,256]{1,0:T(8,128)(2,1)S(1)}, bf16[2048,256]{1,0:T(8,128)(2,1)}, u32[]{:S(2)}) %copy-start.2) | copy-done | bytes 1048600
  56.6 13.7 %full.1.refs_4_ = bf16[2048,256]{1,0:T(8,128)(2,1)} custom-call(s32[288]{0:T(512)S(1)} %fusion.14.lists_ref, f32[288]{0:T(512)S(1)} %fusion.13.flags_ref, s32[8]{0:T(128)S(1)} %fusion.12.glob_ref, s32[2]{0:T(128)S(1)} %broadcast_subtract_fusion.own_ref, bf16[2048,256]{1,0:T(8,128)(2,1)S(1)} %copy-done.2, bf16[2048,256]{1,0:T(8,128)(2,1)S(1)} %copy-done, ...), custom_call_target="tpu_custom_call" | custom-call | flops 5905580032 | bytes 4194304 | tf_op jit(solution)/shard_map/full/pallas_call | solution.py:205
  70.5 1.6 %collective-permute-start.9 = (bf16[2048,128]{1,0:T(8,128)(2,1)}, bf16[2048,128]{1,0:T(8,128)(2,1)}, u32[]{:S(2)}, u32[]{:S(2)}) collective-permute-start(bf16[2048,128]{1,0:T(8,128)(2,1)} %get-tuple-element.23), channel_id=1, source_target_pairs={{0,16},{8,24},{16,0},{24,8},{1,17},{9,25},{17,1},{25,9},{2,18},{10... | collective-permute-start | bytes 1572872 | tf_op jit(solution)/shard_map/ppermute | solution.py:225
  72.1 0.5 collective-permute-start.10
  73.1 1.2 %copy-done.3 = bf16[2048,256]{1,0:T(8,128)(2,1)S(1)} copy-done((bf16[2048,256]{1,0:T(8,128)(2,1)S(1)}, bf16[2048,256]{1,0:T(8,128)(2,1)}, u32[]{:S(2)}) %copy-start.3) | copy-done | bytes 1048600
  74.3 10.7 %early.1 = (f32[2176,128]{1,0:T(8,128)S(1)}, f32[2176,128]{1,0:T(8,128)S(1)}) custom-call(s32[288]{0:T(512)S(1)} %fusion.16.lists_ref, f32[288]{0:T(512)S(1)} %fusion.15.flags_ref, s32[6]{0:T(128)S(1)} %bitcast.6, s32[2]{0:T(128)S(1)} %broadcast_subtract_fusion.own_ref, bf16[2048,256]{1,0:T(8,128)(2,1)S(1)} %copy-done.3, bf16[2048,256]{1,0:T(8,128)(2,1)S(1)} %copy-done, ...), custom_call_target="tpu_custom_call" | custom-call | flops 4831838208 | bytes 3145728 | tf_op jit(solution)/shard_map/early/pallas_call | solution.py:205
  85.1 7.3 %late.1 = bf16[2048,256]{1,0:T(8,128)(2,1)} custom-call(s32[224]{0:T(256)S(1)} %select_n.69.lists_ref, f32[224]{0:T(256)S(1)} %reshape.53.flags_ref, s32[2]{0:T(128)S(1)} %slice_add_fusion.glob_ref, s32[2]{0:T(128)S(1)} %broadcast_subtract_fusion.own_ref, bf16[2048,256]{1,0:T(8,128)(2,1)S(1)} %copy-done.3, ...), custom_call_target="tpu_custom_call", output_to_operand_aliasing={{}: (9, {})} | custom-call | flops 2147483648 | bytes 1048576 | tf_op jit(solution)/shard_map/late/pallas_call | solution.py:205
  (49 shorter events, 2.5 us)
Async XLA Ops:
  0.0 13.1 %copy-start.1 = (bf16[2048,256]{1,0:T(8,128)(2,1)S(1)}, bf16[2048,256]{1,0:T(8,128)(2,1)}, u32[]{:S(2)}) copy-start(bf16[2048,256]{1,0:T(8,128)(2,1)} %refs_3_.1) | copy-start | bytes 3145732
  0.0 9.5 %collective-permute-start.2 = (s32[2]{0:T(128)}, s32[2]{0:T(128)S(1)}, u32[]{:S(2)}, u32[]{:S(2)}) collective-permute-start(s32[2]{0:T(128)} %param.9), channel_id=1, source_target_pairs={{0,24},{8,16},{16,8},{24,0},{1,25},{9,17},{17,9},{25,1},{2,26},{10... | collective-permute-start | bytes 32 | tf_op jit(solution)/shard_map/ppermute | solution.py:225
  3.9 5.6 %collective-permute-start.1 = (s32[2]{0:T(128)}, s32[2]{0:T(128)S(1)}, u32[]{:S(2)}, u32[]{:S(2)}) collective-permute-start(s32[2]{0:T(128)} %param.9), channel_id=1, source_target_pairs={{0,16},{8,24},{16,0},{24,8},{1,17},{9,25},{17,1},{25,9},{2,18},{10... | collective-permute-start | bytes 32 | tf_op jit(solution)/shard_map/ppermute | solution.py:225
  4.4 5.2 %collective-permute-start = (s32[2]{0:T(128)}, s32[2]{0:T(128)S(1)}, u32[]{:S(2)}, u32[]{:S(2)}) collective-permute-start(s32[2]{0:T(128)} %param.9), channel_id=1, source_target_pairs={{0,8},{8,0},{16,24},{24,16},{1,9},{9,1},{17,25},{25,17},{2,10},{10... | collective-permute-start | bytes 32 | tf_op jit(solution)/shard_map/ppermute | solution.py:225
  4.5 26.3 %collective-permute-start.3 = (bf16[2048,256]{1,0:T(8,128)(2,1)}, bf16[2048,256]{1,0:T(8,128)(2,1)S(1)}, u32[]{:S(2)}, u32[]{:S(2)}) collective-permute-start(bf16[2048,256]{1,0:T(8,128)(2,1)} %refs_0_.3), channel_id=1, source_target_pairs={{0,8},{8,0},{16,24},{24,16},{1,9},{9,1},{17,25},{25,17},{2,10},{10... | collective-permute-start | bytes 3145736 | tf_op jit(solution)/shard_map/ppermute | solution.py:225
  6.4 27.4 %collective-permute-start.7 = (bf16[2048,256]{1,0:T(8,128)(2,1)}, bf16[2048,256]{1,0:T(8,128)(2,1)}, u32[]{:S(2)}, u32[]{:S(2)}) collective-permute-start(bf16[2048,256]{1,0:T(8,128)(2,1)} %refs_3_.1), channel_id=1, source_target_pairs={{0,16},{8,24},{16,0},{24,8},{1,17},{9,25},{17,1},{25,9},{2,18},{10... | collective-permute-start | bytes 3145736 | tf_op jit(solution)/shard_map/ppermute | solution.py:225
  12.6 31.5 %collective-permute-start.4 = (bf16[2048,128]{1,0:T(8,128)(2,1)}, bf16[2048,128]{1,0:T(8,128)(2,1)}, u32[]{:S(2)}, u32[]{:S(2)}) collective-permute-start(bf16[2048,128]{1,0:T(8,128)(2,1)} %get-tuple-element.32), channel_id=1, source_target_pairs={{0,16},{8,24},{16,0},{24,8},{1,17},{9,25},{17,1},{25,9},{2,18},{10... | collective-permute-start | bytes 1572872 | tf_op jit(solution)/shard_map/ppermute | solution.py:225
  14.2 30.0 %collective-permute-start.6 = (bf16[2048,128]{1,0:T(8,128)(2,1)}, bf16[2048,128]{1,0:T(8,128)(2,1)}, u32[]{:S(2)}, u32[]{:S(2)}) collective-permute-start(bf16[2048,128]{1,0:T(8,128)(2,1)} %get-tuple-element.30), channel_id=1, source_target_pairs={{0,8},{8,0},{16,24},{24,16},{1,9},{9,1},{17,25},{25,17},{2,10},{10... | collective-permute-start | bytes 1572872 | tf_op jit(solution)/shard_map/ppermute | solution.py:225
  31.9 23.5 %copy-start = (bf16[2048,256]{1,0:T(8,128)(2,1)S(1)}, bf16[2048,256]{1,0:T(8,128)(2,1)}, u32[]{:S(2)}) copy-start(bf16[2048,256]{1,0:T(8,128)(2,1)} %refs_0_.3) | copy-start | bytes 3145732
  31.9 23.4 %collective-permute-start.5 = (bf16[2048,128]{1,0:T(8,128)(2,1)}, bf16[2048,128]{1,0:T(8,128)(2,1)}, u32[]{:S(2)}, u32[]{:S(2)}) collective-permute-start(bf16[2048,128]{1,0:T(8,128)(2,1)} %get-tuple-element.36), channel_id=1, source_target_pairs={{0,16},{8,24},{16,0},{24,8},{1,17},{9,25},{17,1},{25,9},{2,18},{10... | collective-permute-start | bytes 1572872 | tf_op jit(solution)/shard_map/ppermute | solution.py:225
  36.0 19.3 %collective-permute-start.8 = (bf16[2048,128]{1,0:T(8,128)(2,1)}, bf16[2048,128]{1,0:T(8,128)(2,1)}, u32[]{:S(2)}, u32[]{:S(2)}) collective-permute-start(bf16[2048,128]{1,0:T(8,128)(2,1)} %get-tuple-element.34), channel_id=1, source_target_pairs={{0,8},{8,0},{16,24},{24,16},{1,9},{9,1},{17,25},{25,17},{2,10},{10... | collective-permute-start | bytes 1572872 | tf_op jit(solution)/shard_map/ppermute | solution.py:225
  38.4 34.6 %collective-permute-start.11 = (bf16[2048,128]{1,0:T(8,128)(2,1)}, bf16[2048,128]{1,0:T(8,128)(2,1)}, u32[]{:S(2)}, u32[]{:S(2)}) collective-permute-start(bf16[2048,128]{1,0:T(8,128)(2,1)} %get-tuple-element.25), channel_id=1, source_target_pairs={{0,16},{8,24},{16,0},{24,8},{1,17},{9,25},{17,1},{25,9},{2,18},{10... | collective-permute-start | bytes 1572872 | tf_op jit(solution)/shard_map/ppermute | solution.py:225
  44.1 29.0 %collective-permute-start.12 = (bf16[2048,128]{1,0:T(8,128)(2,1)}, bf16[2048,128]{1,0:T(8,128)(2,1)}, u32[]{:S(2)}, u32[]{:S(2)}) collective-permute-start(bf16[2048,128]{1,0:T(8,128)(2,1)} %get-tuple-element.26), channel_id=1, source_target_pairs={{0,8},{8,0},{16,24},{24,16},{1,9},{9,1},{17,25},{25,17},{2,10},{10... | collective-permute-start | bytes 1572872 | tf_op jit(solution)/shard_map/ppermute | solution.py:225
  55.3 1.2 %copy-start.2 = (bf16[2048,256]{1,0:T(8,128)(2,1)S(1)}, bf16[2048,256]{1,0:T(8,128)(2,1)}, u32[]{:S(2)}) copy-start(bf16[2048,256]{1,0:T(8,128)(2,1)} %q_ref.5) | copy-start | bytes 3145732
  70.5 14.5 %collective-permute-start.9 = (bf16[2048,128]{1,0:T(8,128)(2,1)}, bf16[2048,128]{1,0:T(8,128)(2,1)}, u32[]{:S(2)}, u32[]{:S(2)}) collective-permute-start(bf16[2048,128]{1,0:T(8,128)(2,1)} %get-tuple-element.23), channel_id=1, source_target_pairs={{0,16},{8,24},{16,0},{24,8},{1,17},{9,25},{17,1},{25,9},{2,18},{10... | collective-permute-start | bytes 1572872 | tf_op jit(solution)/shard_map/ppermute | solution.py:225
  72.1 13.0 %collective-permute-start.10 = (bf16[2048,128]{1,0:T(8,128)(2,1)}, bf16[2048,128]{1,0:T(8,128)(2,1)}, u32[]{:S(2)}, u32[]{:S(2)}) collective-permute-start(bf16[2048,128]{1,0:T(8,128)(2,1)} %get-tuple-element.24), channel_id=1, source_target_pairs={{0,8},{8,0},{16,24},{24,16},{1,9},{9,1},{17,25},{25,17},{2,10},{10... | collective-permute-start | bytes 1572872 | tf_op jit(solution)/shard_map/ppermute | solution.py:225
  73.1 1.2 %copy-start.3 = (bf16[2048,256]{1,0:T(8,128)(2,1)S(1)}, bf16[2048,256]{1,0:T(8,128)(2,1)}, u32[]{:S(2)}) copy-start(bf16[2048,256]{1,0:T(8,128)(2,1)} %q_ref.5) | copy-start | bytes 3145732

commit v5 on v4

--- a/solution.py
+++ b/solution.py
@@ -241,35 +241,17 @@
     row = jnp.arange(blocks)[:, None]
     window = place((rank * blocks + row + jnp.arange(-1, 2)) % (count * blocks))
     rand = place(rand_blocks)
-    glob = jnp.concatenate([global_blocks] + [exchange(global_blocks, j) for j in range(1, count)])
-    glob = place(glob)
 
     back = steps[::-1]
     k_first, v_first = exchange(keys, steps[0]), exchange(values, back[0])
-    k_held, v_held, rand, window, glob = lax.optimization_barrier((keys, values, rand, window, glob))
-    k_sent, v_sent = [], []
-    for pair in range(pairs):
-        lanes = slice(pair * LANES, (pair + 1) * LANES)
-        k_parts = {0: k_held[:, lanes], steps[0]: k_first[:, lanes]}
-        v_parts = {0: v_held[:, lanes], back[0]: v_first[:, lanes]}
-        done = []
-        for k_step, v_step in zip(steps[1:], back[1:]):
-            for k_at, v_at in list(zip(k_parts, v_parts)):
-                outgoing = (k_parts[k_at], v_parts[v_at])
-                if pair > 0:
-                    gate = before[len(done)] if done else (k_first, v_first)
-                    outgoing = lax.optimization_barrier(outgoing + gate)[:2]
-                done.append((exchange(outgoing[0], k_step), exchange(outgoing[1], v_step)))
-                k_parts[k_at ^ k_step], v_parts[v_at ^ v_step] = done[-1]
-        k_parts.update({0: keys, steps[0]: k_first})
-        v_parts.update({0: values, back[0]: v_first})
-        k_sent.append([k_parts[at] for at in range(count)])
-        v_sent.append([v_parts[at] for at in range(count)])
-        before = done
-
+    glob = [global_blocks] + [exchange(global_blocks, j) for j in range(1, count)]
+    glob = place(jnp.concatenate(glob))
+    k_held, v_held, glob, rand, window = lax.optimization_barrier((keys, values, glob, rand, window))
     own = global_blocks - rank * blocks
-
-    def call(kind, pair, shared, listed, spare, start, stop, state=(), so_far=None):
+    halo = jnp.where(row == 0, window[:, :1], window[:, 2:])
+
+    def call(kind, pair, k_parts, v_parts, shared, listed, spare, state=(), so_far=None):
+        start, stop = (last, count) if kind == "late" else (0, last)
         mine = rand[:, 2 * pair : 2 * pair + 2].reshape(blocks, 2 * RAND)
         lists = jnp.concatenate([listed, mine], axis=1)
         inside = (lists >= start * blocks) & (lists < stop * blocks)
@@ -277,17 +259,33 @@
         return part_call(
             pair, kind, shared, lists.reshape(-1), inside.astype(jnp.float32).reshape(-1),
             glob[gpd * start : gpd * stop] - start * blocks, own, queries,
-            k_sent[pair][start:stop], v_sent[pair][start:stop], state, so_far,
+            [k_parts[at] for at in range(start, stop)], [v_parts[at] for at in range(start, stop)],
+            state, so_far,
         )
 
-    out = None
-    for pair in range(pairs - 1):
-        out = call("full", pair, 3, window, row, 0, count, so_far=out)
-    window = lax.optimization_barrier((window, out))[0]
-    state = call("early", pairs - 1, 3, window, row, 0, last)
-    halo = jnp.where(row == 0, window[:, :1], window[:, 2:])
-    spare = glob[gpd * last] - last * blocks
-    return call("late", pairs - 1, 1, halo, spare, last, count, state=state, so_far=out)
+    out, state = None, None
+    for pair in range(pairs):
+        lanes = slice(pair * LANES, (pair + 1) * LANES)
+        k_parts = {0: k_held[:, lanes], steps[0]: k_first[:, lanes]}
+        v_parts = {0: v_held[:, lanes], back[0]: v_first[:, lanes]}
+        done = 0
+        for k_step, v_step in zip(steps[1:], back[1:]):
+            for k_at, v_at in list(zip(k_parts, v_parts)):
+                outgoing = (k_parts[k_at], v_parts[v_at])
+                if pair > 0:
+                    gate = state if done else (k_first, v_first)
+                    outgoing = lax.optimization_barrier((*outgoing, *gate))[:2]
+                k_parts[k_at ^ k_step] = exchange(outgoing[0], k_step)
+                v_parts[v_at ^ v_step] = exchange(outgoing[1], v_step)
+                done += 1
+        k_parts.update({0: keys, steps[0]: k_first})
+        v_parts.update({0: values, back[0]: v_first})
+        if pair > 0:
+            window = lax.optimization_barrier((window, out))[0]
+        state = call("early", pair, k_parts, v_parts, 3, window, row)
+        spare = glob[gpd * last] - last * blocks
+        out = call("late", pair, k_parts, v_parts, 1, halo, spare, state, out)
+    return out
 
 
 def solution(mesh):

time: 92.8 us -> 87.1 us (0.939)
  waiting for transfers between devices: 32 us -> 20.1 us
  Pallas kernels: 31.8 us -> 36.2 us
  starting transfers between devices: 14.8 us -> 16.2 us
    ppermute x13, waiting for transfers between devices: 32 us -> 20.1 us  [exchange(): return lax.ppermute(array, 'seq', [(i, i ^ step) for i in range(count)])]
    pallas_call x3 -> x4, Pallas kernels: 31.8 us -> 36.2 us  [part_call(): pl.pallas_call(functools.partial(part_kernel, pair, kind, wide, gpd, toke...]
    ppermute x13, starting transfers between devices: 14.8 us -> 16.2 us  [exchange(): return lax.ppermute(array, 'seq', [(i, i ^ step) for i in range(count)])]
    unnamed x8 -> x10, local copies, waits for them, and re-layouts: 2.45 us -> 2.46 us
  transfers between devices with their start and end apart: 13 -> 13, of which waited for: 3 -> 2; matrix products, arithmetic and copies ran while one was open for 11% -> 12% of each run, Pallas kernels for 26% -> 33%
where the time goes in v5:
time: 87.1 us; the launch traced here: 86.7 us
  Pallas kernels  36.2 us (42%)
  waiting for transfers between devices  20.1 us (23%)
  starting transfers between devices  16.2 us (19%)
  local copies, waits for them, and re-layouts  11 us (13%)
  other arithmetic  2.34 us (3%)
    pallas_call x4, Pallas kernels, part_call(): pl.pallas_call(functools.partial(part_kernel, pair, kind, wide, gpd, toke...  36.2 us
    ppermute x13, waiting for transfers between devices, exchange(): return lax.ppermute(array, 'seq', [(i, i ^ step) for i in range(count)])  20.1 us
    ppermute x13, starting transfers between devices, exchange(): return lax.ppermute(array, 'seq', [(i, i ^ step) for i in range(count)])  16.2 us
    slice x2, local copies, waits for them, and re-layouts, shards(): v_parts = {0: v_held[:, lanes], back[0]: v_first[:, lanes]}  3.34 us
    slice x2, local copies, waits for them, and re-layouts, shards(): k_parts = {0: k_held[:, lanes], steps[0]: k_first[:, lanes]}  3.29 us
    unnamed x10, local copies, waits for them, and re-layouts  2.46 us
  transfers between devices with their start and end apart: 13, of which 2 were waited for; matrix products, arithmetic and copies ran while one was open for 12% of the time, Pallas kernels for 33%

profile of v5, /device:TPU:0, one launch (start us, length us, event | category | flops | bytes accessed | tf_op | source)
XLA Modules:
  0.0 86.7 jit_solution(18435134530242189175)
XLA Ops:
  0.0 3.9 %collective-permute-start.2 = (s32[2]{0:T(128)}, s32[2]{0:T(128)S(1)}, u32[]{:S(2)}, u32[]{:S(2)}) collective-permute-start(s32[2]{0:T(128)} %param.9), channel_id=1, source_target_pairs={{0,24},{8,16},{16,8},{24,0},{1,25},{9,17},{17,9},{25,1},{2,26},{10... | collective-permute-start | bytes 32 | tf_op jit(solution)/shard_map/ppermute | solution.py:225
  4.5 2.0 %collective-permute-start.3 = (bf16[2048,256]{1,0:T(8,128)(2,1)}, bf16[2048,256]{1,0:T(8,128)(2,1)S(1)}, u32[]{:S(2)}, u32[]{:S(2)}) collective-permute-start(bf16[2048,256]{1,0:T(8,128)(2,1)} %refs_0_.3), channel_id=1, source_target_pairs={{0,8},{8,0},{16,24},{24,16},{1,9},{9,1},{17,25},{25,17},{2,10},{10... | collective-permute-start | bytes 3145736 | tf_op jit(solution)/shard_map/ppermute | solution.py:225
  6.4 1.5 %collective-permute-start.4 = (bf16[2048,256]{1,0:T(8,128)(2,1)}, bf16[2048,256]{1,0:T(8,128)(2,1)}, u32[]{:S(2)}, u32[]{:S(2)}) collective-permute-start(bf16[2048,256]{1,0:T(8,128)(2,1)} %refs_3_.3), channel_id=1, source_target_pairs={{0,16},{8,24},{16,0},{24,8},{1,17},{9,25},{17,1},{25,9},{2,18},{10... | collective-permute-start | bytes 3145736 | tf_op jit(solution)/shard_map/ppermute | solution.py:225
  7.9 0.7 broadcast_subtract_fusion.own_ref
  8.6 0.7 fusion.2
  9.6 0.7 fusion.13
  10.3 0.6 slice.53
  11.4 2.3 %fusion.19 = (bf16[2048,128]{1,0:T(8,128)(2,1)}, bf16[2048,128]{1,0:T(8,128)(2,1)}) fusion(bf16[2048,256]{1,0:T(8,128)(2,1)} %refs_0_.3), kind=kLoop, calls=%fused_computation.57 | loop fusion | bytes 2097152 | tf_op jit(solution)/shard_map/slice | solution.py:269
  14.2 1.1 %fusion.18 = (bf16[2048,128]{1,0:T(8,128)(2,1)}, bf16[2048,128]{1,0:T(8,128)(2,1)}) fusion(bf16[2048,256]{1,0:T(8,128)(2,1)S(1)} %copy-done.1), kind=kLoop, calls=%fused_computation.56 | loop fusion | bytes 2097152 | tf_op jit(solution)/shard_map/slice | solution.py:270
  16.0 14.8 %collective-permute-done.3.refs_1_ = bf16[2048,256]{1,0:T(8,128)(2,1)S(1)} collective-permute-done((bf16[2048,256]{1,0:T(8,128)(2,1)}, bf16[2048,256]{1,0:T(8,128)(2,1)S(1)}, u32[]{:S(2)}, u32[]{:S(2)}) %collective-permute-start.3) | collective-permute-done | bytes 1048608 | tf_op jit(solution)/shard_map/ppermute | solution.py:225
  30.8 1.0 %fusion.21 = (bf16[2048,128]{1,0:T(8,128)(2,1)}, bf16[2048,128]{1,0:T(8,128)(2,1)}) fusion(bf16[2048,256]{1,0:T(8,128)(2,1)S(1)} %collective-permute-done.3.refs_1_), kind=kLoop, calls=%fused_computation.59 | loop fusion | bytes 2097152 | tf_op jit(solution)/shard_map/slice | solution.py:269
  31.8 2.0 %collective-permute-start.9 = (bf16[2048,128]{1,0:T(8,128)(2,1)}, bf16[2048,128]{1,0:T(8,128)(2,1)}, u32[]{:S(2)}, u32[]{:S(2)}) collective-permute-start(bf16[2048,128]{1,0:T(8,128)(2,1)} %get-tuple-element.39), channel_id=1, source_target_pairs={{0,16},{8,24},{16,0},{24,8},{1,17},{9,25},{17,1},{25,9},{2,18},{10... | collective-permute-start | bytes 1572872 | tf_op jit(solution)/shard_map/ppermute | solution.py:225
  33.8 2.3 %fusion.20 = (bf16[2048,128]{1,0:T(8,128)(2,1)}, bf16[2048,128]{1,0:T(8,128)(2,1)}) fusion(bf16[2048,256]{1,0:T(8,128)(2,1)} %collective-permute-done.4.refs_5_), kind=kLoop, calls=%fused_computation.58 | loop fusion | bytes 2097152 | tf_op jit(solution)/shard_map/slice | solution.py:270
  36.1 1.5 %collective-permute-start.10 = (bf16[2048,128]{1,0:T(8,128)(2,1)}, bf16[2048,128]{1,0:T(8,128)(2,1)}, u32[]{:S(2)}, u32[]{:S(2)}) collective-permute-start(bf16[2048,128]{1,0:T(8,128)(2,1)} %get-tuple-element.37), channel_id=1, source_target_pairs={{0,8},{8,0},{16,24},{24,16},{1,9},{9,1},{17,25},{25,17},{2,10},{10... | collective-permute-start | bytes 1572872 | tf_op jit(solution)/shard_map/ppermute | solution.py:225
  38.2 0.6 collective-permute-start.11
  38.7 5.3 %collective-permute-done.5.refs_2_ = bf16[2048,128]{1,0:T(8,128)(2,1)} collective-permute-done((bf16[2048,128]{1,0:T(8,128)(2,1)}, bf16[2048,128]{1,0:T(8,128)(2,1)}, u32[]{:S(2)}, u32[]{:S(2)}) %collective-permute-start.5) | collective-permute-done | bytes 524320 | tf_op jit(solution)/shard_map/ppermute | solution.py:225
  44.1 1.2 %copy-done.2 = bf16[2048,256]{1,0:T(8,128)(2,1)S(1)} copy-done((bf16[2048,256]{1,0:T(8,128)(2,1)S(1)}, bf16[2048,256]{1,0:T(8,128)(2,1)}, u32[]{:S(2)}) %copy-start.2) | copy-done | bytes 1048600
  45.4 10.8 %early.2 = (f32[2176,128]{1,0:T(8,128)S(1)}, f32[2176,128]{1,0:T(8,128)S(1)}) custom-call(s32[288]{0:T(512)S(1)} %fusion.15.lists_ref, f32[288]{0:T(512)S(1)} %fusion.14.flags_ref, s32[6]{0:T(128)S(1)} %bitcast.6, s32[2]{0:T(128)S(1)} %broadcast_subtract_fusion.own_ref, bf16[2048,256]{1,0:T(8,128)(2,1)S(1)} %copy-done.2, bf16[2048,256]{1,0:T(8,128)(2,1)S(1)} %copy-done, ...), custom_call_target="tpu_custom_call" | custom-call | flops 4831838208 | bytes 3145728 | tf_op jit(solution)/shard_map/early/pallas_call | solution.py:205
  56.1 2.1 %collective-permute-start.7 = (bf16[2048,128]{1,0:T(8,128)(2,1)}, bf16[2048,128]{1,0:T(8,128)(2,1)}, u32[]{:S(2)}, u32[]{:S(2)}) collective-permute-start(bf16[2048,128]{1,0:T(8,128)(2,1)} %get-tuple-element.26), channel_id=1, source_target_pairs={{0,16},{8,24},{16,0},{24,8},{1,17},{9,25},{17,1},{25,9},{2,18},{10... | collective-permute-start | bytes 1572872 | tf_op jit(solution)/shard_map/ppermute | solution.py:225
  58.2 1.5 %collective-permute-start.8 = (bf16[2048,128]{1,0:T(8,128)(2,1)}, bf16[2048,128]{1,0:T(8,128)(2,1)}, u32[]{:S(2)}, u32[]{:S(2)}) collective-permute-start(bf16[2048,128]{1,0:T(8,128)(2,1)} %get-tuple-element.27), channel_id=1, source_target_pairs={{0,8},{8,0},{16,24},{24,16},{1,9},{9,1},{17,25},{25,17},{2,10},{10... | collective-permute-start | bytes 1572872 | tf_op jit(solution)/shard_map/ppermute | solution.py:225
  59.7 7.3 %late.2.refs_4_ = bf16[2048,256]{1,0:T(8,128)(2,1)} custom-call(s32[224]{0:T(256)S(1)} %select_n.78.lists_ref, f32[224]{0:T(256)S(1)} %reshape.70.flags_ref, s32[2]{0:T(128)S(1)} %slice_add_fusion.glob_ref, s32[2]{0:T(128)S(1)} %broadcast_subtract_fusion.own_ref, bf16[2048,256]{1,0:T(8,128)(2,1)S(1)} %copy-done.3, ...), custom_call_target="tpu_custom_call" | custom-call | flops 2147483648 | bytes 1048576 | tf_op jit(solution)/shard_map/late/pallas_call | solution.py:205
  67.3 1.2 %copy-done.4 = bf16[2048,256]{1,0:T(8,128)(2,1)S(1)} copy-done((bf16[2048,256]{1,0:T(8,128)(2,1)S(1)}, bf16[2048,256]{1,0:T(8,128)(2,1)}, u32[]{:S(2)}) %copy-start.4) | copy-done | bytes 1048600
  68.5 10.8 %early.3 = (f32[2176,128]{1,0:T(8,128)S(1)}, f32[2176,128]{1,0:T(8,128)S(1)}) custom-call(s32[288]{0:T(512)S(1)} %fusion.17.lists_ref, f32[288]{0:T(512)S(1)} %fusion.16.flags_ref, s32[6]{0:T(128)S(1)} %bitcast.7, s32[2]{0:T(128)S(1)} %broadcast_subtract_fusion.own_ref, bf16[2048,256]{1,0:T(8,128)(2,1)S(1)} %copy-done.4, bf16[2048,256]{1,0:T(8,128)(2,1)S(1)} %copy-done, ...), custom_call_target="tpu_custom_call" | custom-call | flops 4831838208 | bytes 3145728 | tf_op jit(solution)/shard_map/early/pallas_call | solution.py:205
  79.3 7.3 %late.3 = bf16[2048,256]{1,0:T(8,128)(2,1)} custom-call(s32[224]{0:T(256)S(1)} %select_n.75.lists_ref, f32[224]{0:T(256)S(1)} %reshape.69.flags_ref, s32[2]{0:T(128)S(1)} %slice_add_fusion.glob_ref, s32[2]{0:T(128)S(1)} %broadcast_subtract_fusion.own_ref, bf16[2048,256]{1,0:T(8,128)(2,1)S(1)} %copy-done.4, ...), custom_call_target="tpu_custom_call", output_to_operand_aliasing={{}: (9, {})} | custom-call | flops 2147483648 | bytes 1048576 | tf_op jit(solution)/shard_map/late/pallas_call | solution.py:205
  (56 shorter events, 2.8 us)
Async XLA Ops:
  0.0 9.5 %collective-permute-start.2 = (s32[2]{0:T(128)}, s32[2]{0:T(128)S(1)}, u32[]{:S(2)}, u32[]{:S(2)}) collective-permute-start(s32[2]{0:T(128)} %param.9), channel_id=1, source_target_pairs={{0,24},{8,16},{16,8},{24,0},{1,25},{9,17},{17,9},{25,1},{2,26},{10... | collective-permute-start | bytes 32 | tf_op jit(solution)/shard_map/ppermute | solution.py:225
  3.9 5.6 %collective-permute-start.1 = (s32[2]{0:T(128)}, s32[2]{0:T(128)S(1)}, u32[]{:S(2)}, u32[]{:S(2)}) collective-permute-start(s32[2]{0:T(128)} %param.9), channel_id=1, source_target_pairs={{0,16},{8,24},{16,0},{24,8},{1,17},{9,25},{17,1},{25,9},{2,18},{10... | collective-permute-start | bytes 32 | tf_op jit(solution)/shard_map/ppermute | solution.py:225
  4.4 5.2 %collective-permute-start = (s32[2]{0:T(128)}, s32[2]{0:T(128)S(1)}, u32[]{:S(2)}, u32[]{:S(2)}) collective-permute-start(s32[2]{0:T(128)} %param.9), channel_id=1, source_target_pairs={{0,8},{8,0},{16,24},{24,16},{1,9},{9,1},{17,25},{25,17},{2,10},{10... | collective-permute-start | bytes 32 | tf_op jit(solution)/shard_map/ppermute | solution.py:225
  4.5 26.3 %collective-permute-start.3 = (bf16[2048,256]{1,0:T(8,128)(2,1)}, bf16[2048,256]{1,0:T(8,128)(2,1)S(1)}, u32[]{:S(2)}, u32[]{:S(2)}) collective-permute-start(bf16[2048,256]{1,0:T(8,128)(2,1)} %refs_0_.3), channel_id=1, source_target_pairs={{0,8},{8,0},{16,24},{24,16},{1,9},{9,1},{17,25},{25,17},{2,10},{10... | collective-permute-start | bytes 3145736 | tf_op jit(solution)/shard_map/ppermute | solution.py:225
  6.4 27.4 %collective-permute-start.4 = (bf16[2048,256]{1,0:T(8,128)(2,1)}, bf16[2048,256]{1,0:T(8,128)(2,1)}, u32[]{:S(2)}, u32[]{:S(2)}) collective-permute-start(bf16[2048,256]{1,0:T(8,128)(2,1)} %refs_3_.3), channel_id=1, source_target_pairs={{0,16},{8,24},{16,0},{24,8},{1,17},{9,25},{17,1},{25,9},{2,18},{10... | collective-permute-start | bytes 3145736 | tf_op jit(solution)/shard_map/ppermute | solution.py:225
  10.9 3.2 %copy-start.1 = (bf16[2048,256]{1,0:T(8,128)(2,1)S(1)}, bf16[2048,256]{1,0:T(8,128)(2,1)}, u32[]{:S(2)}) copy-start(bf16[2048,256]{1,0:T(8,128)(2,1)} %refs_3_.3) | copy-start | bytes 3145732
  13.6 30.4 %collective-permute-start.5 = (bf16[2048,128]{1,0:T(8,128)(2,1)}, bf16[2048,128]{1,0:T(8,128)(2,1)}, u32[]{:S(2)}, u32[]{:S(2)}) collective-permute-start(bf16[2048,128]{1,0:T(8,128)(2,1)} %get-tuple-element.36), channel_id=1, source_target_pairs={{0,16},{8,24},{16,0},{24,8},{1,17},{9,25},{17,1},{25,9},{2,18},{10... | collective-permute-start | bytes 1572872 | tf_op jit(solution)/shard_map/ppermute | solution.py:225
  15.2 28.9 %collective-permute-start.6 = (bf16[2048,128]{1,0:T(8,128)(2,1)}, bf16[2048,128]{1,0:T(8,128)(2,1)}, u32[]{:S(2)}, u32[]{:S(2)}) collective-permute-start(bf16[2048,128]{1,0:T(8,128)(2,1)} %get-tuple-element.34), channel_id=1, source_target_pairs={{0,8},{8,0},{16,24},{24,16},{1,9},{9,1},{17,25},{25,17},{2,10},{10... | collective-permute-start | bytes 1572872 | tf_op jit(solution)/shard_map/ppermute | solution.py:225
  31.8 12.3 %copy-start = (bf16[2048,256]{1,0:T(8,128)(2,1)S(1)}, bf16[2048,256]{1,0:T(8,128)(2,1)}, u32[]{:S(2)}) copy-start(bf16[2048,256]{1,0:T(8,128)(2,1)} %refs_0_.3) | copy-start | bytes 3145732
  31.8 26.4 %collective-permute-start.9 = (bf16[2048,128]{1,0:T(8,128)(2,1)}, bf16[2048,128]{1,0:T(8,128)(2,1)}, u32[]{:S(2)}, u32[]{:S(2)}) collective-permute-start(bf16[2048,128]{1,0:T(8,128)(2,1)} %get-tuple-element.39), channel_id=1, source_target_pairs={{0,16},{8,24},{16,0},{24,8},{1,17},{9,25},{17,1},{25,9},{2,18},{10... | collective-permute-start | bytes 1572872 | tf_op jit(solution)/shard_map/ppermute | solution.py:225
  36.1 23.6 %collective-permute-start.10 = (bf16[2048,128]{1,0:T(8,128)(2,1)}, bf16[2048,128]{1,0:T(8,128)(2,1)}, u32[]{:S(2)}, u32[]{:S(2)}) collective-permute-start(bf16[2048,128]{1,0:T(8,128)(2,1)} %get-tuple-element.37), channel_id=1, source_target_pairs={{0,8},{8,0},{16,24},{24,16},{1,9},{9,1},{17,25},{25,17},{2,10},{10... | collective-permute-start | bytes 1572872 | tf_op jit(solution)/shard_map/ppermute | solution.py:225
  38.2 29.1 %collective-permute-start.11 = (bf16[2048,128]{1,0:T(8,128)(2,1)}, bf16[2048,128]{1,0:T(8,128)(2,1)}, u32[]{:S(2)}, u32[]{:S(2)}) collective-permute-start(bf16[2048,128]{1,0:T(8,128)(2,1)} %get-tuple-element.29), channel_id=1, source_target_pairs={{0,16},{8,24},{16,0},{24,8},{1,17},{9,25},{17,1},{25,9},{2,18},{10... | collective-permute-start | bytes 1572872 | tf_op jit(solution)/shard_map/ppermute | solution.py:225
  44.1 23.2 %collective-permute-start.12 = (bf16[2048,128]{1,0:T(8,128)(2,1)}, bf16[2048,128]{1,0:T(8,128)(2,1)}, u32[]{:S(2)}, u32[]{:S(2)}) collective-permute-start(bf16[2048,128]{1,0:T(8,128)(2,1)} %get-tuple-element.30), channel_id=1, source_target_pairs={{0,8},{8,0},{16,24},{24,16},{1,9},{9,1},{17,25},{25,17},{2,10},{10... | collective-permute-start | bytes 1572872 | tf_op jit(solution)/shard_map/ppermute | solution.py:225
  44.1 1.2 %copy-start.2 = (bf16[2048,256]{1,0:T(8,128)(2,1)S(1)}, bf16[2048,256]{1,0:T(8,128)(2,1)}, u32[]{:S(2)}) copy-start(bf16[2048,256]{1,0:T(8,128)(2,1)} %q_ref.7) | copy-start | bytes 3145732
  45.4 14.3 %copy-start.3 = (bf16[2048,256]{1,0:T(8,128)(2,1)S(1)}, bf16[2048,256]{1,0:T(8,128)(2,1)}, u32[]{:S(2)}) copy-start(bf16[2048,256]{1,0:T(8,128)(2,1)} %q_ref.7) | copy-start | bytes 3145732
  56.1 23.2 %collective-permute-start.7 = (bf16[2048,128]{1,0:T(8,128)(2,1)}, bf16[2048,128]{1,0:T(8,128)(2,1)}, u32[]{:S(2)}, u32[]{:S(2)}) collective-permute-start(bf16[2048,128]{1,0:T(8,128)(2,1)} %get-tuple-element.26), channel_id=1, source_target_pairs={{0,16},{8,24},{16,0},{24,8},{1,17},{9,25},{17,1},{25,9},{2,18},{10... | collective-permute-start | bytes 1572872 | tf_op jit(solution)/shard_map/ppermute | solution.py:225
  58.2 21.1 %collective-permute-start.8 = (bf16[2048,128]{1,0:T(8,128)(2,1)}, bf16[2048,128]{1,0:T(8,128)(2,1)}, u32[]{:S(2)}, u32[]{:S(2)}) collective-permute-start(bf16[2048,128]{1,0:T(8,128)(2,1)} %get-tuple-element.27), channel_id=1, source_target_pairs={{0,8},{8,0},{16,24},{24,16},{1,9},{9,1},{17,25},{25,17},{2,10},{10... | collective-permute-start | bytes 1572872 | tf_op jit(solution)/shard_map/ppermute | solution.py:225
  67.3 1.2 %copy-start.4 = (bf16[2048,256]{1,0:T(8,128)(2,1)S(1)}, bf16[2048,256]{1,0:T(8,128)(2,1)}, u32[]{:S(2)}) copy-start(bf16[2048,256]{1,0:T(8,128)(2,1)} %q_ref.7) | copy-start | bytes 3145732

commit v6 on v5

--- a/solution.py
+++ b/solution.py
@@ -11,7 +11,8 @@
 BLK = 64
 RAND = 3
 LANES = 2 * DH
-ROWS = 8
+ROWS = 16
+ID_ROWS = 16
 CHUNK = 2048
 SUBS = 2
 VMEM_BYTES = 16 * 1024 * 1024
@@ -44,7 +45,7 @@
             span = pl.ds(j * tokens, tokens)
             lanes = pl.ds(pair * LANES, LANES)
             for side, (source, target) in enumerate(((k_parts[j], k_all), (v_parts[j], v_all))):
-                source = source.at[:, lanes] if wide[j][side] else source
+                source = source.at[:tokens, lanes] if wide[j][side] else source.at[:tokens]
                 copies.append(pltpu.make_async_copy(source, target.at[span], sems.at[2 * j + side]))
         for copy in copies:
             copy.start()
@@ -78,9 +79,6 @@
     def finish(b, target, peak, sums):
         o, total = fold(sums[:, :LANES]), fold(sums[:, LANES:])
         where = pl.ds(pl.multiple_of(target * BLK, BLK), BLK)
-        if kind == "full":
-            out_ref[where, :] = (o / total).astype(jnp.bfloat16)
-            return
         top = fold(jnp.broadcast_to(peak, (2 * BLK, LANES))) * EXP2_SCALE
         if kind == "late":
             old_o, old_l = block(state_o_ref, b), block(state_l_ref, b)
@@ -110,7 +108,7 @@
             if j >= shared:
                 k = jnp.where(first, k, block(k_all, lists_ref[b]))
                 v = jnp.where(first, v, block(v_all, lists_ref[b]))
-            if kind == "full" or (kind == "early" and j == 1):
+            if kind == "early" and j == 1:
                 ones = block_ones
             else:
                 ones = listed(flags_ref[a], flags_ref[b])
@@ -244,10 +242,12 @@
 
     back = steps[::-1]
     k_first, v_first = exchange(keys, steps[0]), exchange(values, back[0])
-    glob = [global_blocks] + [exchange(global_blocks, j) for j in range(1, count)]
-    glob = place(jnp.concatenate(glob))
-    k_held, v_held, glob, rand, window = lax.optimization_barrier((keys, values, glob, rand, window))
-    own = global_blocks - rank * blocks
+    k_held, v_held, own, rand, window = lax.optimization_barrier(
+        (keys, values, global_blocks - rank * blocks, rand, window)
+    )
+    id_rows = jnp.pad(own[None].astype(keys.dtype), ((0, ID_ROWS - 1), (0, LANES - gpd)))
+    direct = [at for at in range(count) if at & steps[0] and at & back[0]]
+    glob = {at: exchange(own, at) for at in direct}
     halo = jnp.where(row == 0, window[:, :1], window[:, 2:])
 
     def call(kind, pair, k_parts, v_parts, shared, listed, spare, state=(), so_far=None):
@@ -268,19 +268,30 @@
         lanes = slice(pair * LANES, (pair + 1) * LANES)
         k_parts = {0: k_held[:, lanes], steps[0]: k_first[:, lanes]}
         v_parts = {0: v_held[:, lanes], back[0]: v_first[:, lanes]}
-        done = 0
+        if pair == 0:
+            k_parts[0] = jnp.concatenate([k_parts[0], id_rows])
+            v_parts[0] = jnp.concatenate([v_parts[0], id_rows])
+        done, sent = 0, []
         for k_step, v_step in zip(steps[1:], back[1:]):
             for k_at, v_at in list(zip(k_parts, v_parts)):
                 outgoing = (k_parts[k_at], v_parts[v_at])
                 if pair > 0:
                     gate = state if done else (k_first, v_first)
                     outgoing = lax.optimization_barrier((*outgoing, *gate))[:2]
+                sent += outgoing
                 k_parts[k_at ^ k_step] = exchange(outgoing[0], k_step)
                 v_parts[v_at ^ v_step] = exchange(outgoing[1], v_step)
                 done += 1
         k_parts.update({0: keys, steps[0]: k_first})
         v_parts.update({0: values, back[0]: v_first})
-        if pair > 0:
+        if pair == 0:
+            glob[0] = own
+            for at in range(1, count):
+                carrier = glob[at] if at in direct else v_parts[at] if at & steps[0] else k_parts[at]
+                carrier = lax.optimization_barrier((carrier, *sent))[0]
+                glob[at] = carrier if at in direct else carrier[tokens, :gpd].astype(jnp.int32)
+            glob = jnp.concatenate([glob[at] + at * blocks for at in range(count)])
+        else:
             window = lax.optimization_barrier((window, out))[0]
         state = call("early", pair, k_parts, v_parts, 3, window, row)
         spare = glob[gpd * last] - last * blocks

time: 87.1 us -> 84.2 us (0.967)
  waiting for transfers between devices: 20.1 us -> 17.9 us
  Pallas kernels: 36.2 us -> 34.3 us
  other arithmetic: 2.34 us -> 4 us
    unnamed x10 -> x12, local copies, waits for them, and re-layouts: 2.46 us -> 4.9 us
    slice x2 -> x1, local copies, waits for them, and re-layouts: 3.29 us -> 1.05 us  [shards(): k_parts = {0: k_held[:, lanes], steps[0]: k_first[:, lanes]}]
    ppermute x13 -> x11, waiting for transfers between devices: 20.1 us -> 17.9 us  [exchange(): return lax.ppermute(array, 'seq', [(i, i ^ step) for i in range(count)])]
    pallas_call x4, Pallas kernels: 36.2 us -> 34.3 us  [part_call(): pl.pallas_call(functools.partial(part_kernel, pair, kind, wide, gpd, toke...]
    add x0 -> x3, other arithmetic: none -> 1.35 us  [shards(): glob = jnp.concatenate([glob[at] + at * blocks for at in range(count)])]
    concatenate x0 -> x2, other arithmetic: none -> 1.12 us  [the longest x1 1.05 us: shards(): v_parts[0] = jnp.concatenate([v_parts[0], id_rows])]
    ppermute x13 -> x11, starting transfers between devices: 16.2 us -> 16.3 us  [exchange(): return lax.ppermute(array, 'seq', [(i, i ^ step) for i in range(count)])]
  transfers between devices with their start and end apart: 13 -> 11, of which waited for: 2 -> 2; matrix products, arithmetic and copies ran while one was open for 12% -> 12% of each run, Pallas kernels for 33% -> 33%
where the time goes in v6:
time: 84.2 us; the launch traced here: 83.7 us
  Pallas kernels  34.3 us (41%)
  waiting for transfers between devices  17.9 us (21%)
  starting transfers between devices  16.3 us (19%)
  local copies, waits for them, and re-layouts  10.9 us (13%)
  other arithmetic  4 us (5%)
    pallas_call x4, Pallas kernels, part_call(): pl.pallas_call(functools.partial(part_kernel, pair, kind, wide, gpd, toke...  34.3 us
    ppermute x11, waiting for transfers between devices, exchange(): return lax.ppermute(array, 'seq', [(i, i ^ step) for i in range(count)])  17.9 us
    ppermute x11, starting transfers between devices, exchange(): return lax.ppermute(array, 'seq', [(i, i ^ step) for i in range(count)])  16.3 us
    unnamed x12, local copies, waits for them, and re-layouts  4.9 us
    slice x2, local copies, waits for them, and re-layouts, shards(): v_parts = {0: v_held[:, lanes], back[0]: v_first[:, lanes]}  3.7 us
  transfers between devices with their start and end apart: 11, of which 2 were waited for; matrix products, arithmetic and copies ran while one was open for 12% of the time, Pallas kernels for 33%

profile of v6, /device:TPU:0, one launch (start us, length us, event | category | flops | bytes accessed | tf_op | source)
XLA Modules:
  0.0 83.7 jit_solution(12088124494112253381)
XLA Ops:
  0.0 2.9 %collective-permute-start.1 = (bf16[2048,256]{1,0:T(8,128)(2,1)}, bf16[2048,256]{1,0:T(8,128)(2,1)S(1)}, u32[]{:S(2)}, u32[]{:S(2)}) collective-permute-start(bf16[2048,256]{1,0:T(8,128)(2,1)} %refs_0_.3), channel_id=1, source_target_pairs={{0,8},{8,0},{16,24},{24,16},{1,9},{9,1},{17,25},{25,17},{2,10},{10... | collective-permute-start | bytes 3145736 | tf_op jit(solution)/shard_map/ppermute | solution.py:223
  2.9 1.5 %collective-permute-start.2 = (bf16[2048,256]{1,0:T(8,128)(2,1)}, bf16[2048,256]{1,0:T(8,128)(2,1)S(1)}, u32[]{:S(2)}, u32[]{:S(2)}) collective-permute-start(bf16[2048,256]{1,0:T(8,128)(2,1)} %refs_3_.3), channel_id=1, source_target_pairs={{0,16},{8,24},{16,0},{24,8},{1,17},{9,25},{17,1},{25,9},{2,18},{10... | collective-permute-start | bytes 3145736 | tf_op jit(solution)/shard_map/ppermute | solution.py:223
  5.1 0.7 fusion.5
  6.0 2.6 %fusion.20 = (bf16[2048,128]{1,0:T(8,128)(2,1)}, bf16[2048,128]{1,0:T(8,128)(2,1)S(1)}, bf16[2048,128]{1,0:T(8,128)(2,1)S(1)}, bf16[2048,128]{1,0:T(8,128)(2,1)}) fusion(bf16[2048,256]{1,0:T(8,128)(2,1)} %refs_3_.3, bf16[2048,256]{1,0:T(8,128)(2,1)} %refs_0_.3), kind=kLoop, calls=%fused_computation.57 | loop fusion | bytes 4194304 | tf_op jit(solution)/shard_map/slice | solution.py:270
  8.7 1.0 %fusion.2 = (bf16[2064,128]{1,0:T(8,128)(2,1)}, bf16[2064,128]{1,0:T(8,128)(2,1)}) fusion(bf16[1,2]{1,0:T(2,128)(2,1)S(1)} %convert_bitcast_fusion, bf16[2048,128]{1,0:T(8,128)(2,1)S(1)} %get-tuple-element.40, bf16[2048,128]{1,0:T(8,128)(2,1)S(1)} %get-tuple-element.55), kind=kLoop, calls=%fused_computation.3 | loop fusion | flops 2377728 | bytes 2105348 | tf_op jit(solution)/shard_map/concatenate | solution.py:273
  9.7 1.9 %collective-permute-start.3 = (bf16[2064,128]{1,0:T(8,128)(2,1)}, bf16[2064,128]{1,0:T(8,128)(2,1)}, u32[]{:S(2)}, u32[]{:S(2)}) collective-permute-start(bf16[2064,128]{1,0:T(8,128)(2,1)} %get-tuple-element.53), channel_id=1, source_target_pairs={{0,8},{8,0},{16,24},{24,16},{1,9},{9,1},{17,25},{25,17},{2,10},{10... | collective-permute-start | bytes 1585160 | tf_op jit(solution)/shard_map/ppermute | solution.py:223
  11.6 1.5 %collective-permute-start.4 = (bf16[2064,128]{1,0:T(8,128)(2,1)}, bf16[2064,128]{1,0:T(8,128)(2,1)}, u32[]{:S(2)}, u32[]{:S(2)}) collective-permute-start(bf16[2064,128]{1,0:T(8,128)(2,1)} %get-tuple-element.54), channel_id=1, source_target_pairs={{0,16},{8,24},{16,0},{24,8},{1,17},{9,25},{17,1},{25,9},{2,18},{10... | collective-permute-start | bytes 1585160 | tf_op jit(solution)/shard_map/ppermute | solution.py:223
  14.0 13.2 %collective-permute-done.1.refs_1_ = bf16[2048,256]{1,0:T(8,128)(2,1)S(1)} collective-permute-done((bf16[2048,256]{1,0:T(8,128)(2,1)}, bf16[2048,256]{1,0:T(8,128)(2,1)S(1)}, u32[]{:S(2)}, u32[]{:S(2)}) %collective-permute-start.1) | collective-permute-done | bytes 1048608 | tf_op jit(solution)/shard_map/ppermute | solution.py:223
  27.1 1.1 %fusion.23 = (bf16[2048,128]{1,0:T(8,128)(2,1)}, bf16[2048,128]{1,0:T(8,128)(2,1)}) fusion(bf16[2048,256]{1,0:T(8,128)(2,1)S(1)} %collective-permute-done.1.refs_1_), kind=kLoop, calls=%fused_computation.60 | loop fusion | bytes 2097152 | tf_op jit(solution)/shard_map/slice | solution.py:269
  28.2 2.1 %collective-permute-start.7 = (bf16[2048,128]{1,0:T(8,128)(2,1)}, bf16[2048,128]{1,0:T(8,128)(2,1)}, u32[]{:S(2)}, u32[]{:S(2)}) collective-permute-start(bf16[2048,128]{1,0:T(8,128)(2,1)} %get-tuple-element.46), channel_id=1, source_target_pairs={{0,16},{8,24},{16,0},{24,8},{1,17},{9,25},{17,1},{25,9},{2,18},{10... | collective-permute-start | bytes 1572872 | tf_op jit(solution)/shard_map/ppermute | solution.py:223
  30.3 1.1 %fusion.22 = (bf16[2048,128]{1,0:T(8,128)(2,1)}, bf16[2048,128]{1,0:T(8,128)(2,1)}) fusion(bf16[2048,256]{1,0:T(8,128)(2,1)S(1)} %collective-permute-done.2.refs_5_), kind=kLoop, calls=%fused_computation.59 | loop fusion | bytes 2097152 | tf_op jit(solution)/shard_map/slice | solution.py:270
  31.3 1.5 %collective-permute-start.8 = (bf16[2048,128]{1,0:T(8,128)(2,1)}, bf16[2048,128]{1,0:T(8,128)(2,1)}, u32[]{:S(2)}, u32[]{:S(2)}) collective-permute-start(bf16[2048,128]{1,0:T(8,128)(2,1)} %get-tuple-element.44), channel_id=1, source_target_pairs={{0,8},{8,0},{16,24},{24,16},{1,9},{9,1},{17,25},{25,17},{2,10},{10... | collective-permute-start | bytes 1572872 | tf_op jit(solution)/shard_map/ppermute | solution.py:223
  33.8 4.8 %collective-permute-done.3.refs_4_ = bf16[2064,128]{1,0:T(8,128)(2,1)} collective-permute-done((bf16[2064,128]{1,0:T(8,128)(2,1)}, bf16[2064,128]{1,0:T(8,128)(2,1)}, u32[]{:S(2)}, u32[]{:S(2)}) %collective-permute-start.3) | collective-permute-done | bytes 528416 | tf_op jit(solution)/shard_map/ppermute | solution.py:223
  38.6 2.1 %collective-permute-start.10 = (bf16[2048,128]{1,0:T(8,128)(2,1)}, bf16[2048,128]{1,0:T(8,128)(2,1)}, u32[]{:S(2)}, u32[]{:S(2)}) collective-permute-start(bf16[2048,128]{1,0:T(8,128)(2,1)} %get-tuple-element.36), channel_id=1, source_target_pairs={{0,8},{8,0},{16,24},{24,16},{1,9},{9,1},{17,25},{25,17},{2,10},{10... | collective-permute-start | bytes 1572872 | tf_op jit(solution)/shard_map/ppermute | solution.py:223
  40.6 0.7 add_bitcast_fusion.1
  42.1 1.2 %copy-done.1 = bf16[2048,256]{1,0:T(8,128)(2,1)S(1)} copy-done((bf16[2048,256]{1,0:T(8,128)(2,1)S(1)}, bf16[2048,256]{1,0:T(8,128)(2,1)}, u32[]{:S(2)}) %copy-start.1) | copy-done | bytes 1048600
  43.3 1.2 %copy-done.3 = bf16[2048,256]{1,0:T(8,128)(2,1)S(1)} copy-done((bf16[2048,256]{1,0:T(8,128)(2,1)S(1)}, bf16[2048,256]{1,0:T(8,128)(2,1)}, u32[]{:S(2)}) %copy-start.3) | copy-done | bytes 1048600
  44.5 10.3 %early.2 = (f32[2176,128]{1,0:T(8,128)S(1)}, f32[2176,128]{1,0:T(8,128)S(1)}) custom-call(s32[288]{0:T(512)S(1)} %fusion.17.lists_ref, f32[288]{0:T(512)S(1)} %fusion.16.flags_ref, s32[6]{0:T(128)S(1)} %pad_add_fusion.4.glob_ref, s32[2]{0:T(128)S(1)} %broadcast_subtract_fusion.own_ref, bf16[2048,256]{1,0:T(8,128)(2,1)S(1)} %copy-done.3, ...), custom_call_target="tpu_custom_call" | custom-call | flops 4831838208 | bytes 3145728 | tf_op jit(solution)/shard_map/early/pallas_call | solution.py:203
  54.8 1.6 %collective-permute-start.5 = (bf16[2048,128]{1,0:T(8,128)(2,1)}, bf16[2048,128]{1,0:T(8,128)(2,1)}, u32[]{:S(2)}, u32[]{:S(2)}) collective-permute-start(bf16[2048,128]{1,0:T(8,128)(2,1)} %get-tuple-element.32), channel_id=1, source_target_pairs={{0,16},{8,24},{16,0},{24,8},{1,17},{9,25},{17,1},{25,9},{2,18},{10... | collective-permute-start | bytes 1572872 | tf_op jit(solution)/shard_map/ppermute | solution.py:223
  56.9 7.0 %late.2.refs_4_ = bf16[2048,256]{1,0:T(8,128)(2,1)} custom-call(s32[224]{0:T(256)S(1)} %select_n.65.lists_ref, f32[224]{0:T(256)S(1)} %reshape.77.flags_ref, s32[2]{0:T(128)S(1)} %collective-permute-done.glob_ref, s32[2]{0:T(128)S(1)} %broadcast_subtract_fusion.own_ref, bf16[2048,256]{1,0:T(8,128)(2,1)S(1)} %copy-done.4, ...), custom_call_target="tpu_custom_call" | custom-call | flops 2147483648 | bytes 1048576 | tf_op jit(solution)/shard_map/late/pallas_call | solution.py:203
  64.2 1.2 %copy-done.2 = bf16[2048,256]{1,0:T(8,128)(2,1)S(1)} copy-done((bf16[2048,256]{1,0:T(8,128)(2,1)S(1)}, bf16[2048,256]{1,0:T(8,128)(2,1)}, u32[]{:S(2)}) %copy-start.2) | copy-done | bytes 1048600
  65.4 1.2 %copy-done.5 = bf16[2048,256]{1,0:T(8,128)(2,1)S(1)} copy-done((bf16[2048,256]{1,0:T(8,128)(2,1)S(1)}, bf16[2048,256]{1,0:T(8,128)(2,1)}, u32[]{:S(2)}) %copy-start.5) | copy-done | bytes 1048600
  66.6 10.1 %early.3 = (f32[2176,128]{1,0:T(8,128)S(1)}, f32[2176,128]{1,0:T(8,128)S(1)}) custom-call(s32[288]{0:T(512)S(1)} %fusion.19.lists_ref, f32[288]{0:T(512)S(1)} %fusion.18.flags_ref, s32[6]{0:T(128)S(1)} %pad_add_fusion.4.glob_ref, s32[2]{0:T(128)S(1)} %broadcast_subtract_fusion.own_ref, bf16[2048,256]{1,0:T(8,128)(2,1)S(1)} %copy-done.5, ...), custom_call_target="tpu_custom_call" | custom-call | flops 4831838208 | bytes 3145728 | tf_op jit(solution)/shard_map/early/pallas_call | solution.py:203
  76.7 7.0 %late.3 = bf16[2048,256]{1,0:T(8,128)(2,1)} custom-call(s32[224]{0:T(256)S(1)} %select_n.62.lists_ref, f32[224]{0:T(256)S(1)} %reshape.76.flags_ref, s32[2]{0:T(128)S(1)} %collective-permute-done.glob_ref, s32[2]{0:T(128)S(1)} %broadcast_subtract_fusion.own_ref, bf16[2048,256]{1,0:T(8,128)(2,1)S(1)} %copy-done.5, ...), custom_call_target="tpu_custom_call", output_to_operand_aliasing={{}: (9, {})} | custom-call | flops 2147483648 | bytes 1048576 | tf_op jit(solution)/shard_map/late/pallas_call | solution.py:203
  (56 shorter events, 4.0 us)
Async XLA Ops:
  0.0 27.1 %collective-permute-start.1 = (bf16[2048,256]{1,0:T(8,128)(2,1)}, bf16[2048,256]{1,0:T(8,128)(2,1)S(1)}, u32[]{:S(2)}, u32[]{:S(2)}) collective-permute-start(bf16[2048,256]{1,0:T(8,128)(2,1)} %refs_0_.3), channel_id=1, source_target_pairs={{0,8},{8,0},{16,24},{24,16},{1,9},{9,1},{17,25},{25,17},{2,10},{10... | collective-permute-start | bytes 3145736 | tf_op jit(solution)/shard_map/ppermute | solution.py:223
  2.9 27.3 %collective-permute-start.2 = (bf16[2048,256]{1,0:T(8,128)(2,1)}, bf16[2048,256]{1,0:T(8,128)(2,1)S(1)}, u32[]{:S(2)}, u32[]{:S(2)}) collective-permute-start(bf16[2048,256]{1,0:T(8,128)(2,1)} %refs_3_.3), channel_id=1, source_target_pairs={{0,16},{8,24},{16,0},{24,8},{1,17},{9,25},{17,1},{25,9},{2,18},{10... | collective-permute-start | bytes 3145736 | tf_op jit(solution)/shard_map/ppermute | solution.py:223
  5.9 26.9 %collective-permute-start = (s32[2]{0:T(128)S(1)}, s32[2]{0:T(128)S(1)}, u32[]{:S(2)}, u32[]{:S(2)}) collective-permute-start(s32[2]{0:T(128)S(1)} %broadcast_subtract_fusion.own_ref), channel_id=1, source_target_pairs={{0,24},{8,16},{16,8},{24,0},{1,25},{9,17},{17,9},{25,1},{2,26},{10... | collective-permute-start | bytes 32 | tf_op jit(solution)/shard_map/ppermute | solution.py:223
  9.7 28.9 %collective-permute-start.3 = (bf16[2064,128]{1,0:T(8,128)(2,1)}, bf16[2064,128]{1,0:T(8,128)(2,1)}, u32[]{:S(2)}, u32[]{:S(2)}) collective-permute-start(bf16[2064,128]{1,0:T(8,128)(2,1)} %get-tuple-element.53), channel_id=1, source_target_pairs={{0,8},{8,0},{16,24},{24,16},{1,9},{9,1},{17,25},{25,17},{2,10},{10... | collective-permute-start | bytes 1585160 | tf_op jit(solution)/shard_map/ppermute | solution.py:223
  11.6 29.7 %collective-permute-start.4 = (bf16[2064,128]{1,0:T(8,128)(2,1)}, bf16[2064,128]{1,0:T(8,128)(2,1)}, u32[]{:S(2)}, u32[]{:S(2)}) collective-permute-start(bf16[2064,128]{1,0:T(8,128)(2,1)} %get-tuple-element.54), channel_id=1, source_target_pairs={{0,16},{8,24},{16,0},{24,8},{1,17},{9,25},{17,1},{25,9},{2,18},{10... | collective-permute-start | bytes 1585160 | tf_op jit(solution)/shard_map/ppermute | solution.py:223
  28.2 13.9 %copy-start = (bf16[2048,256]{1,0:T(8,128)(2,1)S(1)}, bf16[2048,256]{1,0:T(8,128)(2,1)}, u32[]{:S(2)}) copy-start(bf16[2048,256]{1,0:T(8,128)(2,1)} %refs_0_.3) | copy-start | bytes 3145732
  28.2 28.2 %collective-permute-start.7 = (bf16[2048,128]{1,0:T(8,128)(2,1)}, bf16[2048,128]{1,0:T(8,128)(2,1)}, u32[]{:S(2)}, u32[]{:S(2)}) collective-permute-start(bf16[2048,128]{1,0:T(8,128)(2,1)} %get-tuple-element.46), channel_id=1, source_target_pairs={{0,16},{8,24},{16,0},{24,8},{1,17},{9,25},{17,1},{25,9},{2,18},{10... | collective-permute-start | bytes 1572872 | tf_op jit(solution)/shard_map/ppermute | solution.py:223
  31.3 25.6 %collective-permute-start.8 = (bf16[2048,128]{1,0:T(8,128)(2,1)}, bf16[2048,128]{1,0:T(8,128)(2,1)}, u32[]{:S(2)}, u32[]{:S(2)}) collective-permute-start(bf16[2048,128]{1,0:T(8,128)(2,1)} %get-tuple-element.44), channel_id=1, source_target_pairs={{0,8},{8,0},{16,24},{24,16},{1,9},{9,1},{17,25},{25,17},{2,10},{10... | collective-permute-start | bytes 1572872 | tf_op jit(solution)/shard_map/ppermute | solution.py:223
  32.8 31.3 %collective-permute-start.9 = (bf16[2048,128]{1,0:T(8,128)(2,1)}, bf16[2048,128]{1,0:T(8,128)(2,1)}, u32[]{:S(2)}, u32[]{:S(2)}) collective-permute-start(bf16[2048,128]{1,0:T(8,128)(2,1)} %get-tuple-element.35), channel_id=1, source_target_pairs={{0,16},{8,24},{16,0},{24,8},{1,17},{9,25},{17,1},{25,9},{2,18},{10... | collective-permute-start | bytes 1572872 | tf_op jit(solution)/shard_map/ppermute | solution.py:223
  38.6 25.6 %collective-permute-start.10 = (bf16[2048,128]{1,0:T(8,128)(2,1)}, bf16[2048,128]{1,0:T(8,128)(2,1)}, u32[]{:S(2)}, u32[]{:S(2)}) collective-permute-start(bf16[2048,128]{1,0:T(8,128)(2,1)} %get-tuple-element.36), channel_id=1, source_target_pairs={{0,8},{8,0},{16,24},{24,16},{1,9},{9,1},{17,25},{25,17},{2,10},{10... | collective-permute-start | bytes 1572872 | tf_op jit(solution)/shard_map/ppermute | solution.py:223
  42.1 1.2 %copy-start.1 = (bf16[2048,256]{1,0:T(8,128)(2,1)S(1)}, bf16[2048,256]{1,0:T(8,128)(2,1)}, u32[]{:S(2)}) copy-start(bf16[2048,256]{1,0:T(8,128)(2,1)} %refs_3_.3) | copy-start | bytes 3145732
  43.3 1.2 %copy-start.3 = (bf16[2048,256]{1,0:T(8,128)(2,1)S(1)}, bf16[2048,256]{1,0:T(8,128)(2,1)}, u32[]{:S(2)}) copy-start(bf16[2048,256]{1,0:T(8,128)(2,1)} %q_ref.7) | copy-start | bytes 3145732
  44.5 12.4 %copy-start.4 = (bf16[2048,256]{1,0:T(8,128)(2,1)S(1)}, bf16[2048,256]{1,0:T(8,128)(2,1)}, u32[]{:S(2)}) copy-start(bf16[2048,256]{1,0:T(8,128)(2,1)} %q_ref.7) | copy-start | bytes 3145732
  54.8 21.9 %collective-permute-start.5 = (bf16[2048,128]{1,0:T(8,128)(2,1)}, bf16[2048,128]{1,0:T(8,128)(2,1)}, u32[]{:S(2)}, u32[]{:S(2)}) collective-permute-start(bf16[2048,128]{1,0:T(8,128)(2,1)} %get-tuple-element.32), channel_id=1, source_target_pairs={{0,16},{8,24},{16,0},{24,8},{1,17},{9,25},{17,1},{25,9},{2,18},{10... | collective-permute-start | bytes 1572872 | tf_op jit(solution)/shard_map/ppermute | solution.py:223
  56.4 20.3 %collective-permute-start.6 = (bf16[2048,128]{1,0:T(8,128)(2,1)}, bf16[2048,128]{1,0:T(8,128)(2,1)}, u32[]{:S(2)}, u32[]{:S(2)}) collective-permute-start(bf16[2048,128]{1,0:T(8,128)(2,1)} %get-tuple-element.33), channel_id=1, source_target_pairs={{0,8},{8,0},{16,24},{24,16},{1,9},{9,1},{17,25},{25,17},{2,10},{10... | collective-permute-start | bytes 1572872 | tf_op jit(solution)/shard_map/ppermute | solution.py:223
  64.1 1.2 %copy-start.2 = (bf16[2048,256]{1,0:T(8,128)(2,1)S(1)}, bf16[2048,256]{1,0:T(8,128)(2,1)}, u32[]{:S(2)}) copy-start(bf16[2048,256]{1,0:T(8,128)(2,1)} %refs_3_.3) | copy-start | bytes 3145732
  65.4 1.2 %copy-start.5 = (bf16[2048,256]{1,0:T(8,128)(2,1)S(1)}, bf16[2048,256]{1,0:T(8,128)(2,1)}, u32[]{:S(2)}) copy-start(bf16[2048,256]{1,0:T(8,128)(2,1)} %q_ref.7) | copy-start | bytes 3145732

commit v7 on v6

--- a/solution.py
+++ b/solution.py
@@ -120,17 +120,19 @@
         v = jnp.concatenate(v_list + [v_glob[...]], axis=0)
         return s, v, jnp.concatenate(one_list + [glob_ones], axis=0)
 
+    size = blocks if kind == "late" else ROWS
+
     def rows_step(step, carry):
-        base = step * ROWS
+        base = step * size
         ahead = scores(base)
-        for u in range(ROWS):
-            (s, v, ones), ahead = ahead, scores(base + u + 1) if u + 1 < ROWS else None
+        for u in range(size):
+            (s, v, ones), ahead = ahead, scores(base + u + 1) if u + 1 < size else None
             peak = jnp.max(s, axis=1, keepdims=True)
             w = jnp.exp2((s - peak) * EXP2_SCALE)
             finish(base + u, base + u, peak, weighted(w, v, ones))
         return carry
 
-    lax.fori_loop(0, blocks // ROWS, rows_step, 0)
+    rows_step(0, 0) if kind == "late" else lax.fori_loop(0, blocks // ROWS, rows_step, 0)
 
     q_glob = []
     for g in range(gpd):

time: 84.2 us -> 83.2 us (0.988)
  Pallas kernels: 34.3 us -> 33.4 us
    pallas_call x4, Pallas kernels: 34.3 us -> 33.4 us  [part_call(): pl.pallas_call(functools.partial(part_kernel, pair, kind, wide, gpd, toke...]
where the time goes in v7:
time: 83.2 us; the launch traced here: 82.7 us
  Pallas kernels  33.4 us (40%)
  waiting for transfers between devices  17.9 us (22%)
  starting transfers between devices  16.3 us (20%)
  local copies, waits for them, and re-layouts  10.9 us (13%)
  other arithmetic  4 us (5%)
    pallas_call x4, Pallas kernels, part_call(): pl.pallas_call(functools.partial(part_kernel, pair, kind, wide, gpd, toke...  33.4 us
    ppermute x11, waiting for transfers between devices, exchange(): return lax.ppermute(array, 'seq', [(i, i ^ step) for i in range(count)])  17.9 us
    ppermute x11, starting transfers between devices, exchange(): return lax.ppermute(array, 'seq', [(i, i ^ step) for i in range(count)])  16.3 us
    unnamed x12, local copies, waits for them, and re-layouts  4.9 us
    slice x2, local copies, waits for them, and re-layouts, shards(): v_parts = {0: v_held[:, lanes], back[0]: v_first[:, lanes]}  3.7 us
  transfers between devices with their start and end apart: 11, of which 2 were waited for; matrix products, arithmetic and copies ran while one was open for 12% of the time, Pallas kernels for 33%

profile of v7, /device:TPU:0, one launch (start us, length us, event | category | flops | bytes accessed | tf_op | source)
XLA Modules:
  0.0 82.7 jit_solution(6696410781024149169)
XLA Ops:
  0.0 2.9 %collective-permute-start.1 = (bf16[2048,256]{1,0:T(8,128)(2,1)}, bf16[2048,256]{1,0:T(8,128)(2,1)S(1)}, u32[]{:S(2)}, u32[]{:S(2)}) collective-permute-start(bf16[2048,256]{1,0:T(8,128)(2,1)} %refs_0_.3), channel_id=1, source_target_pairs={{0,8},{8,0},{16,24},{24,16},{1,9},{9,1},{17,25},{25,17},{2,10},{10... | collective-permute-start | bytes 3145736 | tf_op jit(solution)/shard_map/ppermute | solution.py:225
  2.9 1.5 %collective-permute-start.2 = (bf16[2048,256]{1,0:T(8,128)(2,1)}, bf16[2048,256]{1,0:T(8,128)(2,1)S(1)}, u32[]{:S(2)}, u32[]{:S(2)}) collective-permute-start(bf16[2048,256]{1,0:T(8,128)(2,1)} %refs_3_.3), channel_id=1, source_target_pairs={{0,16},{8,24},{16,0},{24,8},{1,17},{9,25},{17,1},{25,9},{2,18},{10... | collective-permute-start | bytes 3145736 | tf_op jit(solution)/shard_map/ppermute | solution.py:225
  5.1 0.7 fusion.5
  6.0 2.6 %fusion.20 = (bf16[2048,128]{1,0:T(8,128)(2,1)}, bf16[2048,128]{1,0:T(8,128)(2,1)S(1)}, bf16[2048,128]{1,0:T(8,128)(2,1)S(1)}, bf16[2048,128]{1,0:T(8,128)(2,1)}) fusion(bf16[2048,256]{1,0:T(8,128)(2,1)} %refs_3_.3, bf16[2048,256]{1,0:T(8,128)(2,1)} %refs_0_.3), kind=kLoop, calls=%fused_computation.57 | loop fusion | bytes 4194304 | tf_op jit(solution)/shard_map/slice | solution.py:272
  8.7 1.0 %fusion.2 = (bf16[2064,128]{1,0:T(8,128)(2,1)}, bf16[2064,128]{1,0:T(8,128)(2,1)}) fusion(bf16[1,2]{1,0:T(2,128)(2,1)S(1)} %convert_bitcast_fusion, bf16[2048,128]{1,0:T(8,128)(2,1)S(1)} %get-tuple-element.40, bf16[2048,128]{1,0:T(8,128)(2,1)S(1)} %get-tuple-element.55), kind=kLoop, calls=%fused_computation.3 | loop fusion | flops 2377728 | bytes 2105348 | tf_op jit(solution)/shard_map/concatenate | solution.py:275
  9.7 1.9 %collective-permute-start.3 = (bf16[2064,128]{1,0:T(8,128)(2,1)}, bf16[2064,128]{1,0:T(8,128)(2,1)}, u32[]{:S(2)}, u32[]{:S(2)}) collective-permute-start(bf16[2064,128]{1,0:T(8,128)(2,1)} %get-tuple-element.53), channel_id=1, source_target_pairs={{0,8},{8,0},{16,24},{24,16},{1,9},{9,1},{17,25},{25,17},{2,10},{10... | collective-permute-start | bytes 1585160 | tf_op jit(solution)/shard_map/ppermute | solution.py:225
  11.6 1.5 %collective-permute-start.4 = (bf16[2064,128]{1,0:T(8,128)(2,1)}, bf16[2064,128]{1,0:T(8,128)(2,1)}, u32[]{:S(2)}, u32[]{:S(2)}) collective-permute-start(bf16[2064,128]{1,0:T(8,128)(2,1)} %get-tuple-element.54), channel_id=1, source_target_pairs={{0,16},{8,24},{16,0},{24,8},{1,17},{9,25},{17,1},{25,9},{2,18},{10... | collective-permute-start | bytes 1585160 | tf_op jit(solution)/shard_map/ppermute | solution.py:225
  14.0 13.2 %collective-permute-done.1.refs_1_ = bf16[2048,256]{1,0:T(8,128)(2,1)S(1)} collective-permute-done((bf16[2048,256]{1,0:T(8,128)(2,1)}, bf16[2048,256]{1,0:T(8,128)(2,1)S(1)}, u32[]{:S(2)}, u32[]{:S(2)}) %collective-permute-start.1) | collective-permute-done | bytes 1048608 | tf_op jit(solution)/shard_map/ppermute | solution.py:225
  27.1 1.1 %fusion.23 = (bf16[2048,128]{1,0:T(8,128)(2,1)}, bf16[2048,128]{1,0:T(8,128)(2,1)}) fusion(bf16[2048,256]{1,0:T(8,128)(2,1)S(1)} %collective-permute-done.1.refs_1_), kind=kLoop, calls=%fused_computation.60 | loop fusion | bytes 2097152 | tf_op jit(solution)/shard_map/slice | solution.py:271
  28.2 2.1 %collective-permute-start.7 = (bf16[2048,128]{1,0:T(8,128)(2,1)}, bf16[2048,128]{1,0:T(8,128)(2,1)}, u32[]{:S(2)}, u32[]{:S(2)}) collective-permute-start(bf16[2048,128]{1,0:T(8,128)(2,1)} %get-tuple-element.46), channel_id=1, source_target_pairs={{0,16},{8,24},{16,0},{24,8},{1,17},{9,25},{17,1},{25,9},{2,18},{10... | collective-permute-start | bytes 1572872 | tf_op jit(solution)/shard_map/ppermute | solution.py:225
  30.3 1.1 %fusion.22 = (bf16[2048,128]{1,0:T(8,128)(2,1)}, bf16[2048,128]{1,0:T(8,128)(2,1)}) fusion(bf16[2048,256]{1,0:T(8,128)(2,1)S(1)} %collective-permute-done.2.refs_5_), kind=kLoop, calls=%fused_computation.59 | loop fusion | bytes 2097152 | tf_op jit(solution)/shard_map/slice | solution.py:272
  31.3 1.5 %collective-permute-start.8 = (bf16[2048,128]{1,0:T(8,128)(2,1)}, bf16[2048,128]{1,0:T(8,128)(2,1)}, u32[]{:S(2)}, u32[]{:S(2)}) collective-permute-start(bf16[2048,128]{1,0:T(8,128)(2,1)} %get-tuple-element.44), channel_id=1, source_target_pairs={{0,8},{8,0},{16,24},{24,16},{1,9},{9,1},{17,25},{25,17},{2,10},{10... | collective-permute-start | bytes 1572872 | tf_op jit(solution)/shard_map/ppermute | solution.py:225
  33.8 4.8 %collective-permute-done.3.refs_4_ = bf16[2064,128]{1,0:T(8,128)(2,1)} collective-permute-done((bf16[2064,128]{1,0:T(8,128)(2,1)}, bf16[2064,128]{1,0:T(8,128)(2,1)}, u32[]{:S(2)}, u32[]{:S(2)}) %collective-permute-start.3) | collective-permute-done | bytes 528416 | tf_op jit(solution)/shard_map/ppermute | solution.py:225
  38.6 2.1 %collective-permute-start.10 = (bf16[2048,128]{1,0:T(8,128)(2,1)}, bf16[2048,128]{1,0:T(8,128)(2,1)}, u32[]{:S(2)}, u32[]{:S(2)}) collective-permute-start(bf16[2048,128]{1,0:T(8,128)(2,1)} %get-tuple-element.36), channel_id=1, source_target_pairs={{0,8},{8,0},{16,24},{24,16},{1,9},{9,1},{17,25},{25,17},{2,10},{10... | collective-permute-start | bytes 1572872 | tf_op jit(solution)/shard_map/ppermute | solution.py:225
  40.6 0.7 add_bitcast_fusion.1
  42.1 1.2 %copy-done.1 = bf16[2048,256]{1,0:T(8,128)(2,1)S(1)} copy-done((bf16[2048,256]{1,0:T(8,128)(2,1)S(1)}, bf16[2048,256]{1,0:T(8,128)(2,1)}, u32[]{:S(2)}) %copy-start.1) | copy-done | bytes 1048600
  43.3 1.2 %copy-done.3 = bf16[2048,256]{1,0:T(8,128)(2,1)S(1)} copy-done((bf16[2048,256]{1,0:T(8,128)(2,1)S(1)}, bf16[2048,256]{1,0:T(8,128)(2,1)}, u32[]{:S(2)}) %copy-start.3) | copy-done | bytes 1048600
  44.5 10.3 %early.2 = (f32[2176,128]{1,0:T(8,128)S(1)}, f32[2176,128]{1,0:T(8,128)S(1)}) custom-call(s32[288]{0:T(512)S(1)} %fusion.17.lists_ref, f32[288]{0:T(512)S(1)} %fusion.16.flags_ref, s32[6]{0:T(128)S(1)} %pad_add_fusion.4.glob_ref, s32[2]{0:T(128)S(1)} %broadcast_subtract_fusion.own_ref, bf16[2048,256]{1,0:T(8,128)(2,1)S(1)} %copy-done.3, ...), custom_call_target="tpu_custom_call" | custom-call | flops 4831838208 | bytes 3145728 | tf_op jit(solution)/shard_map/early/pallas_call | solution.py:205
  54.8 1.6 %collective-permute-start.5 = (bf16[2048,128]{1,0:T(8,128)(2,1)}, bf16[2048,128]{1,0:T(8,128)(2,1)}, u32[]{:S(2)}, u32[]{:S(2)}) collective-permute-start(bf16[2048,128]{1,0:T(8,128)(2,1)} %get-tuple-element.32), channel_id=1, source_target_pairs={{0,16},{8,24},{16,0},{24,8},{1,17},{9,25},{17,1},{25,9},{2,18},{10... | collective-permute-start | bytes 1572872 | tf_op jit(solution)/shard_map/ppermute | solution.py:225
  56.9 6.4 %late.2.refs_4_ = bf16[2048,256]{1,0:T(8,128)(2,1)} custom-call(s32[224]{0:T(256)S(1)} %select_n.65.lists_ref, f32[224]{0:T(256)S(1)} %reshape.77.flags_ref, s32[2]{0:T(128)S(1)} %collective-permute-done.glob_ref, s32[2]{0:T(128)S(1)} %broadcast_subtract_fusion.own_ref, bf16[2048,256]{1,0:T(8,128)(2,1)S(1)} %copy-done.4, ...), custom_call_target="tpu_custom_call" | custom-call | flops 2147483648 | bytes 1048576 | tf_op jit(solution)/shard_map/late/pallas_call | solution.py:205
  63.6 1.2 %copy-done.2 = bf16[2048,256]{1,0:T(8,128)(2,1)S(1)} copy-done((bf16[2048,256]{1,0:T(8,128)(2,1)S(1)}, bf16[2048,256]{1,0:T(8,128)(2,1)}, u32[]{:S(2)}) %copy-start.2) | copy-done | bytes 1048600
  64.8 1.2 %copy-done.5 = bf16[2048,256]{1,0:T(8,128)(2,1)S(1)} copy-done((bf16[2048,256]{1,0:T(8,128)(2,1)S(1)}, bf16[2048,256]{1,0:T(8,128)(2,1)}, u32[]{:S(2)}) %copy-start.5) | copy-done | bytes 1048600
  66.0 10.3 %early.3 = (f32[2176,128]{1,0:T(8,128)S(1)}, f32[2176,128]{1,0:T(8,128)S(1)}) custom-call(s32[288]{0:T(512)S(1)} %fusion.19.lists_ref, f32[288]{0:T(512)S(1)} %fusion.18.flags_ref, s32[6]{0:T(128)S(1)} %pad_add_fusion.4.glob_ref, s32[2]{0:T(128)S(1)} %broadcast_subtract_fusion.own_ref, bf16[2048,256]{1,0:T(8,128)(2,1)S(1)} %copy-done.5, ...), custom_call_target="tpu_custom_call" | custom-call | flops 4831838208 | bytes 3145728 | tf_op jit(solution)/shard_map/early/pallas_call | solution.py:205
  76.4 6.4 %late.3 = bf16[2048,256]{1,0:T(8,128)(2,1)} custom-call(s32[224]{0:T(256)S(1)} %select_n.62.lists_ref, f32[224]{0:T(256)S(1)} %reshape.76.flags_ref, s32[2]{0:T(128)S(1)} %collective-permute-done.glob_ref, s32[2]{0:T(128)S(1)} %broadcast_subtract_fusion.own_ref, bf16[2048,256]{1,0:T(8,128)(2,1)S(1)} %copy-done.5, ...), custom_call_target="tpu_custom_call", output_to_operand_aliasing={{}: (9, {})} | custom-call | flops 2147483648 | bytes 1048576 | tf_op jit(solution)/shard_map/late/pallas_call | solution.py:205
  (56 shorter events, 4.0 us)
Async XLA Ops:
  0.0 27.1 %collective-permute-start.1 = (bf16[2048,256]{1,0:T(8,128)(2,1)}, bf16[2048,256]{1,0:T(8,128)(2,1)S(1)}, u32[]{:S(2)}, u32[]{:S(2)}) collective-permute-start(bf16[2048,256]{1,0:T(8,128)(2,1)} %refs_0_.3), channel_id=1, source_target_pairs={{0,8},{8,0},{16,24},{24,16},{1,9},{9,1},{17,25},{25,17},{2,10},{10... | collective-permute-start | bytes 3145736 | tf_op jit(solution)/shard_map/ppermute | solution.py:225
  2.9 27.3 %collective-permute-start.2 = (bf16[2048,256]{1,0:T(8,128)(2,1)}, bf16[2048,256]{1,0:T(8,128)(2,1)S(1)}, u32[]{:S(2)}, u32[]{:S(2)}) collective-permute-start(bf16[2048,256]{1,0:T(8,128)(2,1)} %refs_3_.3), channel_id=1, source_target_pairs={{0,16},{8,24},{16,0},{24,8},{1,17},{9,25},{17,1},{25,9},{2,18},{10... | collective-permute-start | bytes 3145736 | tf_op jit(solution)/shard_map/ppermute | solution.py:225
  5.9 26.9 %collective-permute-start = (s32[2]{0:T(128)S(1)}, s32[2]{0:T(128)S(1)}, u32[]{:S(2)}, u32[]{:S(2)}) collective-permute-start(s32[2]{0:T(128)S(1)} %broadcast_subtract_fusion.own_ref), channel_id=1, source_target_pairs={{0,24},{8,16},{16,8},{24,0},{1,25},{9,17},{17,9},{25,1},{2,26},{10... | collective-permute-start | bytes 32 | tf_op jit(solution)/shard_map/ppermute | solution.py:225
  9.7 28.9 %collective-permute-start.3 = (bf16[2064,128]{1,0:T(8,128)(2,1)}, bf16[2064,128]{1,0:T(8,128)(2,1)}, u32[]{:S(2)}, u32[]{:S(2)}) collective-permute-start(bf16[2064,128]{1,0:T(8,128)(2,1)} %get-tuple-element.53), channel_id=1, source_target_pairs={{0,8},{8,0},{16,24},{24,16},{1,9},{9,1},{17,25},{25,17},{2,10},{10... | collective-permute-start | bytes 1585160 | tf_op jit(solution)/shard_map/ppermute | solution.py:225
  11.6 29.7 %collective-permute-start.4 = (bf16[2064,128]{1,0:T(8,128)(2,1)}, bf16[2064,128]{1,0:T(8,128)(2,1)}, u32[]{:S(2)}, u32[]{:S(2)}) collective-permute-start(bf16[2064,128]{1,0:T(8,128)(2,1)} %get-tuple-element.54), channel_id=1, source_target_pairs={{0,16},{8,24},{16,0},{24,8},{1,17},{9,25},{17,1},{25,9},{2,18},{10... | collective-permute-start | bytes 1585160 | tf_op jit(solution)/shard_map/ppermute | solution.py:225
  28.2 13.9 %copy-start = (bf16[2048,256]{1,0:T(8,128)(2,1)S(1)}, bf16[2048,256]{1,0:T(8,128)(2,1)}, u32[]{:S(2)}) copy-start(bf16[2048,256]{1,0:T(8,128)(2,1)} %refs_0_.3) | copy-start | bytes 3145732
  28.2 28.2 %collective-permute-start.7 = (bf16[2048,128]{1,0:T(8,128)(2,1)}, bf16[2048,128]{1,0:T(8,128)(2,1)}, u32[]{:S(2)}, u32[]{:S(2)}) collective-permute-start(bf16[2048,128]{1,0:T(8,128)(2,1)} %get-tuple-element.46), channel_id=1, source_target_pairs={{0,16},{8,24},{16,0},{24,8},{1,17},{9,25},{17,1},{25,9},{2,18},{10... | collective-permute-start | bytes 1572872 | tf_op jit(solution)/shard_map/ppermute | solution.py:225
  31.3 25.6 %collective-permute-start.8 = (bf16[2048,128]{1,0:T(8,128)(2,1)}, bf16[2048,128]{1,0:T(8,128)(2,1)}, u32[]{:S(2)}, u32[]{:S(2)}) collective-permute-start(bf16[2048,128]{1,0:T(8,128)(2,1)} %get-tuple-element.44), channel_id=1, source_target_pairs={{0,8},{8,0},{16,24},{24,16},{1,9},{9,1},{17,25},{25,17},{2,10},{10... | collective-permute-start | bytes 1572872 | tf_op jit(solution)/shard_map/ppermute | solution.py:225
  32.8 30.7 %collective-permute-start.9 = (bf16[2048,128]{1,0:T(8,128)(2,1)}, bf16[2048,128]{1,0:T(8,128)(2,1)}, u32[]{:S(2)}, u32[]{:S(2)}) collective-permute-start(bf16[2048,128]{1,0:T(8,128)(2,1)} %get-tuple-element.35), channel_id=1, source_target_pairs={{0,16},{8,24},{16,0},{24,8},{1,17},{9,25},{17,1},{25,9},{2,18},{10... | collective-permute-start | bytes 1572872 | tf_op jit(solution)/shard_map/ppermute | solution.py:225
  38.6 25.0 %collective-permute-start.10 = (bf16[2048,128]{1,0:T(8,128)(2,1)}, bf16[2048,128]{1,0:T(8,128)(2,1)}, u32[]{:S(2)}, u32[]{:S(2)}) collective-permute-start(bf16[2048,128]{1,0:T(8,128)(2,1)} %get-tuple-element.36), channel_id=1, source_target_pairs={{0,8},{8,0},{16,24},{24,16},{1,9},{9,1},{17,25},{25,17},{2,10},{10... | collective-permute-start | bytes 1572872 | tf_op jit(solution)/shard_map/ppermute | solution.py:225
  42.1 1.2 %copy-start.1 = (bf16[2048,256]{1,0:T(8,128)(2,1)S(1)}, bf16[2048,256]{1,0:T(8,128)(2,1)}, u32[]{:S(2)}) copy-start(bf16[2048,256]{1,0:T(8,128)(2,1)} %refs_3_.3) | copy-start | bytes 3145732
  43.3 1.2 %copy-start.3 = (bf16[2048,256]{1,0:T(8,128)(2,1)S(1)}, bf16[2048,256]{1,0:T(8,128)(2,1)}, u32[]{:S(2)}) copy-start(bf16[2048,256]{1,0:T(8,128)(2,1)} %q_ref.7) | copy-start | bytes 3145732
  44.5 12.4 %copy-start.4 = (bf16[2048,256]{1,0:T(8,128)(2,1)S(1)}, bf16[2048,256]{1,0:T(8,128)(2,1)}, u32[]{:S(2)}) copy-start(bf16[2048,256]{1,0:T(8,128)(2,1)} %q_ref.7) | copy-start | bytes 3145732
  54.8 21.5 %collective-permute-start.5 = (bf16[2048,128]{1,0:T(8,128)(2,1)}, bf16[2048,128]{1,0:T(8,128)(2,1)}, u32[]{:S(2)}, u32[]{:S(2)}) collective-permute-start(bf16[2048,128]{1,0:T(8,128)(2,1)} %get-tuple-element.32), channel_id=1, source_target_pairs={{0,16},{8,24},{16,0},{24,8},{1,17},{9,25},{17,1},{25,9},{2,18},{10... | collective-permute-start | bytes 1572872 | tf_op jit(solution)/shard_map/ppermute | solution.py:225
  56.4 19.9 %collective-permute-start.6 = (bf16[2048,128]{1,0:T(8,128)(2,1)}, bf16[2048,128]{1,0:T(8,128)(2,1)}, u32[]{:S(2)}, u32[]{:S(2)}) collective-permute-start(bf16[2048,128]{1,0:T(8,128)(2,1)} %get-tuple-element.33), channel_id=1, source_target_pairs={{0,8},{8,0},{16,24},{24,16},{1,9},{9,1},{17,25},{25,17},{2,10},{10... | collective-permute-start | bytes 1572872 | tf_op jit(solution)/shard_map/ppermute | solution.py:225
  63.6 1.2 %copy-start.2 = (bf16[2048,256]{1,0:T(8,128)(2,1)S(1)}, bf16[2048,256]{1,0:T(8,128)(2,1)}, u32[]{:S(2)}) copy-start(bf16[2048,256]{1,0:T(8,128)(2,1)} %refs_3_.3) | copy-start | bytes 3145732
  64.8 1.2 %copy-start.5 = (bf16[2048,256]{1,0:T(8,128)(2,1)S(1)}, bf16[2048,256]{1,0:T(8,128)(2,1)}, u32[]{:S(2)}) copy-start(bf16[2048,256]{1,0:T(8,128)(2,1)} %q_ref.7) | copy-start | bytes 3145732

commit v8 on v6

--- a/solution.py
+++ b/solution.py
@@ -12,7 +12,9 @@
 RAND = 3
 LANES = 2 * DH
 ROWS = 16
+TOGETHER = 8
 ID_ROWS = 16
+TOGETHER = 8
 CHUNK = 2048
 SUBS = 2
 VMEM_BYTES = 16 * 1024 * 1024
@@ -31,19 +33,15 @@
     globs = gpd * ranges
     k_parts, v_parts, refs = refs[:ranges], refs[ranges : 2 * ranges], refs[2 * ranges :]
     if kind == "late":
-        state_o_ref, state_l_ref = refs[:2]
+        q_all, state_o_ref, state_l_ref = q_ref, *refs[:2]
         out_ref, k_glob, v_glob = refs[3:] if pair > 0 else refs[2:]
         k_all, v_all = k_parts[0], v_parts[0]
     else:
-        if kind == "early":
-            out_l_ref, refs = refs[1], refs[:1] + refs[2:]
-        elif pair > 0:
-            refs = refs[1:]
-        out_ref, k_glob, v_glob, k_all, v_all, sems = refs
-        copies = []
+        out_ref, out_l_ref, q_all, k_glob, v_glob, k_all, v_all, sems = refs
+        lanes = pl.ds(pair * LANES, LANES)
+        copies = [pltpu.make_async_copy(q_ref.at[:, lanes], q_all, sems.at[2 * ranges])]
         for j in range(ranges):
             span = pl.ds(j * tokens, tokens)
-            lanes = pl.ds(pair * LANES, LANES)
             for side, (source, target) in enumerate(((k_parts[j], k_all), (v_parts[j], v_all))):
                 source = source.at[:tokens, lanes] if wide[j][side] else source.at[:tokens]
                 copies.append(pltpu.make_async_copy(source, target.at[span], sems.at[2 * j + side]))
@@ -98,9 +96,9 @@
 
     glob_ones = jnp.ones((globs * BLK, LANES), jnp.bfloat16)
 
-    def scores(row):
+    def parts_of(row):
         at = row * slots
-        q_bd = jnp.concatenate(split_heads(block(q_ref, row)), axis=0)
+        q_bd = jnp.concatenate(split_heads(block(q_all, row)), axis=0)
         k_list, v_list, one_list = [], [], []
         for j in range(shared + RAND):
             a, b = (at + j, at + j) if j < shared else (at + j, at + RAND + j)
@@ -116,11 +114,17 @@
             k_list.append(k)
             v_list.append(v)
             one_list.append(ones)
-        s = qk(q_bd, jnp.concatenate(k_list + [k_glob[...]], axis=0))
-        v = jnp.concatenate(v_list + [v_glob[...]], axis=0)
-        return s, v, jnp.concatenate(one_list + [glob_ones], axis=0)
-
-    def rows_step(step, carry):
+        return q_bd, k_list, v_list, one_list
+
+    def joined(arrays):
+        return jnp.concatenate(arrays, axis=0)
+
+    def scores(row):
+        q_bd, k_list, v_list, one_list = parts_of(row)
+        s = qk(q_bd, joined(k_list + [k_glob[...]]))
+        return s, joined(v_list + [v_glob[...]]), joined(one_list + [glob_ones])
+
+    def early_rows(step, carry):
         base = step * ROWS
         ahead = scores(base)
         for u in range(ROWS):
@@ -130,11 +134,34 @@
             finish(base + u, base + u, peak, weighted(w, v, ones))
         return carry
 
-    lax.fori_loop(0, blocks // ROWS, rows_step, 0)
+    def late_rows(base):
+        rows = [parts_of(base + u) for u in range(TOGETHER)]
+        s_own = [qk(q_bd, joined(k_list)) for q_bd, k_list, _, _ in rows]
+        s_glob = qk(joined([q_bd for q_bd, _, _, _ in rows]), k_glob[...])
+        sums, w_glob, peaks = [], [], []
+        for u, (_, _, v_list, one_list) in enumerate(rows):
+            s_here = s_glob[2 * BLK * u : 2 * BLK * (u + 1)]
+            peak = jnp.maximum(
+                jnp.max(s_own[u], axis=1, keepdims=True), jnp.max(s_here, axis=1, keepdims=True)
+            )
+            w = jnp.exp2((s_own[u] - peak) * EXP2_SCALE)
+            sums.append(weighted(w, joined(v_list), joined(one_list)))
+            w_glob.append(jnp.exp2((s_here - peak) * EXP2_SCALE).astype(jnp.bfloat16))
+            peaks.append(peak)
+        sums_glob = weighted(joined(w_glob), v_glob[...], glob_ones)
+        for u in range(TOGETHER):
+            here = sums_glob[2 * BLK * u : 2 * BLK * (u + 1)]
+            finish(base + u, base + u, peaks[u], sums[u] + here)
+
+    if kind == "late":
+        for base in range(0, blocks, TOGETHER):
+            late_rows(base)
+    else:
+        lax.fori_loop(0, blocks // ROWS, early_rows, 0)
 
     q_glob = []
     for g in range(gpd):
-        q_glob += split_heads(block(q_ref, own_ref[g]))
+        q_glob += split_heads(block(q_all, own_ref[g]))
     q_glob = jnp.concatenate(q_glob, axis=0)
     chunk_ones = jnp.ones((CHUNK // SUBS, LANES), jnp.bfloat16)
 
@@ -168,10 +195,12 @@
     pair, kind, shared, lists, flags, glob, own, queries, k_parts, v_parts, state=(), so_far=None
 ):
     tokens, columns = queries.shape
+    if kind == "late":
+        *state, queries = state
     ranges = len(k_parts)
     gpd = own.shape[0]
     smem = pl.BlockSpec(memory_space=pltpu.SMEM)
-    hbm = pl.BlockSpec(memory_space=pl.ANY)
+    hbm = pl.BlockSpec(memory_space=pltpu.HBM)
     half = pl.BlockSpec((tokens, LANES), lambda i: (0, pair))
     state_rows = tokens + gpd * BLK
 
@@ -179,7 +208,7 @@
         return pl.BlockSpec((rows, LANES), lambda i: (0, 0))
 
     operands = [lists, flags, glob, own, queries, *k_parts, *v_parts, *state]
-    in_specs = [smem] * 4 + [half] + [full(tokens) if kind == "late" else hbm] * (2 * ranges)
+    in_specs = [smem] * 4 + [full(tokens) if kind == "late" else hbm] * (1 + 2 * ranges)
     in_specs += [full(state_rows)] * len(state)
     aliases = {}
     if so_far is not None:
@@ -187,8 +216,9 @@
         operands.append(so_far)
         in_specs.append(hbm)
     if kind == "early":
-        out_specs = [full(state_rows)] * 2
+        out_specs = [full(state_rows)] * 2 + [full(tokens)]
         out_shape = [jax.ShapeDtypeStruct((state_rows, LANES), jnp.float32)] * 2
+        out_shape.append(jax.ShapeDtypeStruct((tokens, LANES), queries.dtype))
     else:
         out_specs = half
         out_shape = jax.ShapeDtypeStruct((tokens, columns), jnp.bfloat16)
@@ -199,7 +229,7 @@
     scratch = [pltpu.VMEM((globs, LANES), jnp.bfloat16)] * 2
     if kind != "late":
         scratch += [pltpu.VMEM((keys_all, LANES), jnp.bfloat16)] * 2
-        scratch.append(pltpu.SemaphoreType.DMA((2 * ranges,)))
+        scratch.append(pltpu.SemaphoreType.DMA((2 * ranges + 1,)))
     return pl.pallas_call(
         functools.partial(part_kernel, pair, kind, wide, gpd, tokens, shared),
         grid=(1,),

time: 84.2 us -> 82.6 us (0.981)
  Pallas kernels: 34.3 us -> 32.8 us
    pallas_call x4, Pallas kernels: 34.3 us -> 32.8 us  [part_call(): pl.pallas_call(functools.partial(part_kernel, pair, kind, wide, gpd, toke...]
    unnamed x12 -> x10, local copies, waits for them, and re-layouts: 4.9 us -> 4.9 us
where the time goes in v8:
time: 82.6 us; the launch traced here: 82.2 us
  Pallas kernels  32.8 us (40%)
  waiting for transfers between devices  18 us (22%)
  starting transfers between devices  16.3 us (20%)
  local copies, waits for them, and re-layouts  10.9 us (13%)
  other arithmetic  4.01 us (5%)
    pallas_call x4, Pallas kernels, part_call(): pl.pallas_call(functools.partial(part_kernel, pair, kind, wide, gpd, toke...  32.8 us
    ppermute x11, waiting for transfers between devices, exchange(): return lax.ppermute(array, 'seq', [(i, i ^ step) for i in range(count)])  18 us
    ppermute x11, starting transfers between devices, exchange(): return lax.ppermute(array, 'seq', [(i, i ^ step) for i in range(count)])  16.3 us
    unnamed x10, local copies, waits for them, and re-layouts  4.9 us
    slice x2, local copies, waits for them, and re-layouts, shards(): v_parts = {0: v_held[:, lanes], back[0]: v_first[:, lanes]}  3.67 us
  transfers between devices with their start and end apart: 11, of which 2 were waited for; matrix products, arithmetic and copies ran while one was open for 12% of the time, Pallas kernels for 33%

profile of v8, /device:TPU:0, one launch (start us, length us, event | category | flops | bytes accessed | tf_op | source)
XLA Modules:
  0.0 82.2 jit_solution(18435649762471855944)
XLA Ops:
  0.0 2.9 %collective-permute-start.1 = (bf16[2048,256]{1,0:T(8,128)(2,1)}, bf16[2048,256]{1,0:T(8,128)(2,1)S(1)}, u32[]{:S(2)}, u32[]{:S(2)}) collective-permute-start(bf16[2048,256]{1,0:T(8,128)(2,1)} %refs_0_.3), channel_id=1, source_target_pairs={{0,8},{8,0},{16,24},{24,16},{1,9},{9,1},{17,25},{25,17},{2,10},{10... | collective-permute-start | bytes 3145736 | tf_op jit(solution)/shard_map/ppermute | solution.py:253
  2.9 1.5 %collective-permute-start.2 = (bf16[2048,256]{1,0:T(8,128)(2,1)}, bf16[2048,256]{1,0:T(8,128)(2,1)S(1)}, u32[]{:S(2)}, u32[]{:S(2)}) collective-permute-start(bf16[2048,256]{1,0:T(8,128)(2,1)} %refs_3_.3), channel_id=1, source_target_pairs={{0,16},{8,24},{16,0},{24,8},{1,17},{9,25},{17,1},{25,9},{2,18},{10... | collective-permute-start | bytes 3145736 | tf_op jit(solution)/shard_map/ppermute | solution.py:253
  5.1 0.7 fusion.5
  6.0 2.6 %fusion.22 = (bf16[2048,128]{1,0:T(8,128)(2,1)}, bf16[2048,128]{1,0:T(8,128)(2,1)S(1)}, bf16[2048,128]{1,0:T(8,128)(2,1)S(1)}, bf16[2048,128]{1,0:T(8,128)(2,1)}) fusion(bf16[2048,256]{1,0:T(8,128)(2,1)} %refs_3_.3, bf16[2048,256]{1,0:T(8,128)(2,1)} %refs_0_.3), kind=kLoop, calls=%fused_computation.59 | loop fusion | bytes 4194304 | tf_op jit(solution)/shard_map/slice | solution.py:300
  8.7 1.1 %fusion.2 = (bf16[2064,128]{1,0:T(8,128)(2,1)}, bf16[2064,128]{1,0:T(8,128)(2,1)}) fusion(bf16[1,2]{1,0:T(2,128)(2,1)S(1)} %convert_bitcast_fusion, bf16[2048,128]{1,0:T(8,128)(2,1)S(1)} %get-tuple-element.48, bf16[2048,128]{1,0:T(8,128)(2,1)S(1)} %get-tuple-element.59), kind=kLoop, calls=%fused_computation.3 | loop fusion | flops 2377728 | bytes 2105348 | tf_op jit(solution)/shard_map/concatenate | solution.py:303
  9.7 1.9 %collective-permute-start.3 = (bf16[2064,128]{1,0:T(8,128)(2,1)}, bf16[2064,128]{1,0:T(8,128)(2,1)}, u32[]{:S(2)}, u32[]{:S(2)}) collective-permute-start(bf16[2064,128]{1,0:T(8,128)(2,1)} %get-tuple-element.57), channel_id=1, source_target_pairs={{0,8},{8,0},{16,24},{24,16},{1,9},{9,1},{17,25},{25,17},{2,10},{10... | collective-permute-start | bytes 1585160 | tf_op jit(solution)/shard_map/ppermute | solution.py:253
  11.7 1.5 %collective-permute-start.4 = (bf16[2064,128]{1,0:T(8,128)(2,1)}, bf16[2064,128]{1,0:T(8,128)(2,1)}, u32[]{:S(2)}, u32[]{:S(2)}) collective-permute-start(bf16[2064,128]{1,0:T(8,128)(2,1)} %get-tuple-element.58), channel_id=1, source_target_pairs={{0,16},{8,24},{16,0},{24,8},{1,17},{9,25},{17,1},{25,9},{2,18},{10... | collective-permute-start | bytes 1585160 | tf_op jit(solution)/shard_map/ppermute | solution.py:253
  14.0 13.2 %collective-permute-done.1.refs_1_ = bf16[2048,256]{1,0:T(8,128)(2,1)S(1)} collective-permute-done((bf16[2048,256]{1,0:T(8,128)(2,1)}, bf16[2048,256]{1,0:T(8,128)(2,1)S(1)}, u32[]{:S(2)}, u32[]{:S(2)}) %collective-permute-start.1) | collective-permute-done | bytes 1048608 | tf_op jit(solution)/shard_map/ppermute | solution.py:253
  27.1 1.1 %fusion.21 = (bf16[2048,128]{1,0:T(8,128)(2,1)}, bf16[2048,128]{1,0:T(8,128)(2,1)}) fusion(bf16[2048,256]{1,0:T(8,128)(2,1)S(1)} %collective-permute-done.1.refs_1_), kind=kLoop, calls=%fused_computation.58 | loop fusion | bytes 2097152 | tf_op jit(solution)/shard_map/slice | solution.py:299
  28.2 2.1 %collective-permute-start.5 = (bf16[2048,128]{1,0:T(8,128)(2,1)}, bf16[2048,128]{1,0:T(8,128)(2,1)}, u32[]{:S(2)}, u32[]{:S(2)}) collective-permute-start(bf16[2048,128]{1,0:T(8,128)(2,1)} %get-tuple-element.46), channel_id=1, source_target_pairs={{0,16},{8,24},{16,0},{24,8},{1,17},{9,25},{17,1},{25,9},{2,18},{10... | collective-permute-start | bytes 1572872 | tf_op jit(solution)/shard_map/ppermute | solution.py:253
  30.3 1.0 %fusion.20 = (bf16[2048,128]{1,0:T(8,128)(2,1)}, bf16[2048,128]{1,0:T(8,128)(2,1)}) fusion(bf16[2048,256]{1,0:T(8,128)(2,1)S(1)} %collective-permute-done.2.refs_5_), kind=kLoop, calls=%fused_computation.57 | loop fusion | bytes 2097152 | tf_op jit(solution)/shard_map/slice | solution.py:300
  31.3 1.5 %collective-permute-start.6 = (bf16[2048,128]{1,0:T(8,128)(2,1)}, bf16[2048,128]{1,0:T(8,128)(2,1)}, u32[]{:S(2)}, u32[]{:S(2)}) collective-permute-start(bf16[2048,128]{1,0:T(8,128)(2,1)} %get-tuple-element.44), channel_id=1, source_target_pairs={{0,8},{8,0},{16,24},{24,16},{1,9},{9,1},{17,25},{25,17},{2,10},{10... | collective-permute-start | bytes 1572872 | tf_op jit(solution)/shard_map/ppermute | solution.py:253
  33.8 4.8 %collective-permute-done.3.refs_4_ = bf16[2064,128]{1,0:T(8,128)(2,1)} collective-permute-done((bf16[2064,128]{1,0:T(8,128)(2,1)}, bf16[2064,128]{1,0:T(8,128)(2,1)}, u32[]{:S(2)}, u32[]{:S(2)}) %collective-permute-start.3) | collective-permute-done | bytes 528416 | tf_op jit(solution)/shard_map/ppermute | solution.py:253
  38.6 2.1 %collective-permute-start.8 = (bf16[2048,128]{1,0:T(8,128)(2,1)}, bf16[2048,128]{1,0:T(8,128)(2,1)}, u32[]{:S(2)}, u32[]{:S(2)}) collective-permute-start(bf16[2048,128]{1,0:T(8,128)(2,1)} %get-tuple-element.37), channel_id=1, source_target_pairs={{0,8},{8,0},{16,24},{24,16},{1,9},{9,1},{17,25},{25,17},{2,10},{10... | collective-permute-start | bytes 1572872 | tf_op jit(solution)/shard_map/ppermute | solution.py:253
  41.3 0.7 add_bitcast_fusion
  42.1 1.2 %copy-done.1 = bf16[2048,256]{1,0:T(8,128)(2,1)S(1)} copy-done((bf16[2048,256]{1,0:T(8,128)(2,1)S(1)}, bf16[2048,256]{1,0:T(8,128)(2,1)}, u32[]{:S(2)}) %copy-start.1) | copy-done | bytes 1048600
  43.3 1.2 %copy-done.3 = bf16[2048,256]{1,0:T(8,128)(2,1)S(1)} copy-done((bf16[2048,256]{1,0:T(8,128)(2,1)S(1)}, bf16[2048,256]{1,0:T(8,128)(2,1)}, u32[]{:S(2)}) %copy-start.3) | copy-done | bytes 1048600
  44.5 10.3 %early.2 = (f32[2176,128]{1,0:T(8,128)S(1)}, f32[2176,128]{1,0:T(8,128)S(1)}, bf16[2048,128]{1,0:T(8,128)(2,1)S(1)}) custom-call(s32[288]{0:T(512)S(1)} %fusion.17.lists_ref, f32[288]{0:T(512)S(1)} %fusion.16.flags_ref, s32[6]{0:T(128)S(1)} %pad_add_fusion.4.glob_ref, s32[2]{0:T(128)S(1)} %broadcast_subtract_fusion.own_ref, bf16[2048,256]{1,0:T(8,128)(2,1)S(1)} %copy-done.3, ...), custom_call_target="tpu_custom_call" | custom-call | flops 4831838208 | bytes 3145728 | tf_op jit(solution)/shard_map/early/pallas_call | solution.py:233
  54.9 1.6 %collective-permute-start.9 = (bf16[2048,128]{1,0:T(8,128)(2,1)}, bf16[2048,128]{1,0:T(8,128)(2,1)}, u32[]{:S(2)}, u32[]{:S(2)}) collective-permute-start(bf16[2048,128]{1,0:T(8,128)(2,1)} %get-tuple-element.39), channel_id=1, source_target_pairs={{0,16},{8,24},{16,0},{24,8},{1,17},{9,25},{17,1},{25,9},{2,18},{10... | collective-permute-start | bytes 1572872 | tf_op jit(solution)/shard_map/ppermute | solution.py:253
  57.0 6.0 %late.2.refs_4_ = bf16[2048,256]{1,0:T(8,128)(2,1)} custom-call(s32[224]{0:T(256)S(1)} %select_n.64.lists_ref, f32[224]{0:T(256)S(1)} %reshape.77.flags_ref, s32[2]{0:T(128)S(1)} %collective-permute-done.glob_ref, s32[2]{0:T(128)S(1)} %broadcast_subtract_fusion.own_ref, bf16[2048,128]{1,0:T(8,128)(2,1)S(1)} %get-tuple-element.32.q_ref, ...), custom_call_target="tpu_custom_call" | custom-call | flops 2147483648 | bytes 1048576 | tf_op jit(solution)/shard_map/late/pallas_call | solution.py:233
  63.3 1.2 %copy-done.2 = bf16[2048,256]{1,0:T(8,128)(2,1)S(1)} copy-done((bf16[2048,256]{1,0:T(8,128)(2,1)S(1)}, bf16[2048,256]{1,0:T(8,128)(2,1)}, u32[]{:S(2)}) %copy-start.2) | copy-done | bytes 1048600
  64.5 1.2 %copy-done.4 = bf16[2048,256]{1,0:T(8,128)(2,1)S(1)} copy-done((bf16[2048,256]{1,0:T(8,128)(2,1)S(1)}, bf16[2048,256]{1,0:T(8,128)(2,1)}, u32[]{:S(2)}) %copy-start.4) | copy-done | bytes 1048600
  65.7 10.4 %early.3 = (f32[2176,128]{1,0:T(8,128)S(1)}, f32[2176,128]{1,0:T(8,128)S(1)}, bf16[2048,128]{1,0:T(8,128)(2,1)S(1)}) custom-call(s32[288]{0:T(512)S(1)} %fusion.19.lists_ref, f32[288]{0:T(512)S(1)} %fusion.18.flags_ref, s32[6]{0:T(128)S(1)} %pad_add_fusion.4.glob_ref, s32[2]{0:T(128)S(1)} %broadcast_subtract_fusion.own_ref, bf16[2048,256]{1,0:T(8,128)(2,1)S(1)} %copy-done.4, ...), custom_call_target="tpu_custom_call" | custom-call | flops 4831838208 | bytes 3145728 | tf_op jit(solution)/shard_map/early/pallas_call | solution.py:233
  76.1 6.0 %late.3 = bf16[2048,256]{1,0:T(8,128)(2,1)} custom-call(s32[224]{0:T(256)S(1)} %select_n.62.lists_ref, f32[224]{0:T(256)S(1)} %reshape.76.flags_ref, s32[2]{0:T(128)S(1)} %collective-permute-done.glob_ref, s32[2]{0:T(128)S(1)} %broadcast_subtract_fusion.own_ref, bf16[2048,128]{1,0:T(8,128)(2,1)S(1)} %get-tuple-element.38.q_ref, ...), custom_call_target="tpu_custom_call", output_to_operand_aliasing={{}: (9, {})} | custom-call | flops 2147483648 | bytes 1048576 | tf_op jit(solution)/shard_map/late/pallas_call | solution.py:233
  (54 shorter events, 4.0 us)
Async XLA Ops:
  0.0 27.1 %collective-permute-start.1 = (bf16[2048,256]{1,0:T(8,128)(2,1)}, bf16[2048,256]{1,0:T(8,128)(2,1)S(1)}, u32[]{:S(2)}, u32[]{:S(2)}) collective-permute-start(bf16[2048,256]{1,0:T(8,128)(2,1)} %refs_0_.3), channel_id=1, source_target_pairs={{0,8},{8,0},{16,24},{24,16},{1,9},{9,1},{17,25},{25,17},{2,10},{10... | collective-permute-start | bytes 3145736 | tf_op jit(solution)/shard_map/ppermute | solution.py:253
  2.9 27.3 %collective-permute-start.2 = (bf16[2048,256]{1,0:T(8,128)(2,1)}, bf16[2048,256]{1,0:T(8,128)(2,1)S(1)}, u32[]{:S(2)}, u32[]{:S(2)}) collective-permute-start(bf16[2048,256]{1,0:T(8,128)(2,1)} %refs_3_.3), channel_id=1, source_target_pairs={{0,16},{8,24},{16,0},{24,8},{1,17},{9,25},{17,1},{25,9},{2,18},{10... | collective-permute-start | bytes 3145736 | tf_op jit(solution)/shard_map/ppermute | solution.py:253
  5.9 26.9 %collective-permute-start = (s32[2]{0:T(128)S(1)}, s32[2]{0:T(128)S(1)}, u32[]{:S(2)}, u32[]{:S(2)}) collective-permute-start(s32[2]{0:T(128)S(1)} %broadcast_subtract_fusion.own_ref), channel_id=1, source_target_pairs={{0,24},{8,16},{16,8},{24,0},{1,25},{9,17},{17,9},{25,1},{2,26},{10... | collective-permute-start | bytes 32 | tf_op jit(solution)/shard_map/ppermute | solution.py:253
  9.7 28.9 %collective-permute-start.3 = (bf16[2064,128]{1,0:T(8,128)(2,1)}, bf16[2064,128]{1,0:T(8,128)(2,1)}, u32[]{:S(2)}, u32[]{:S(2)}) collective-permute-start(bf16[2064,128]{1,0:T(8,128)(2,1)} %get-tuple-element.57), channel_id=1, source_target_pairs={{0,8},{8,0},{16,24},{24,16},{1,9},{9,1},{17,25},{25,17},{2,10},{10... | collective-permute-start | bytes 1585160 | tf_op jit(solution)/shard_map/ppermute | solution.py:253
  11.7 29.7 %collective-permute-start.4 = (bf16[2064,128]{1,0:T(8,128)(2,1)}, bf16[2064,128]{1,0:T(8,128)(2,1)}, u32[]{:S(2)}, u32[]{:S(2)}) collective-permute-start(bf16[2064,128]{1,0:T(8,128)(2,1)} %get-tuple-element.58), channel_id=1, source_target_pairs={{0,16},{8,24},{16,0},{24,8},{1,17},{9,25},{17,1},{25,9},{2,18},{10... | collective-permute-start | bytes 1585160 | tf_op jit(solution)/shard_map/ppermute | solution.py:253
  28.2 13.9 %copy-start = (bf16[2048,256]{1,0:T(8,128)(2,1)S(1)}, bf16[2048,256]{1,0:T(8,128)(2,1)}, u32[]{:S(2)}) copy-start(bf16[2048,256]{1,0:T(8,128)(2,1)} %refs_3_.3) | copy-start | bytes 3145732
  28.2 28.3 %collective-permute-start.5 = (bf16[2048,128]{1,0:T(8,128)(2,1)}, bf16[2048,128]{1,0:T(8,128)(2,1)}, u32[]{:S(2)}, u32[]{:S(2)}) collective-permute-start(bf16[2048,128]{1,0:T(8,128)(2,1)} %get-tuple-element.46), channel_id=1, source_target_pairs={{0,16},{8,24},{16,0},{24,8},{1,17},{9,25},{17,1},{25,9},{2,18},{10... | collective-permute-start | bytes 1572872 | tf_op jit(solution)/shard_map/ppermute | solution.py:253
  31.3 25.7 %collective-permute-start.6 = (bf16[2048,128]{1,0:T(8,128)(2,1)}, bf16[2048,128]{1,0:T(8,128)(2,1)}, u32[]{:S(2)}, u32[]{:S(2)}) collective-permute-start(bf16[2048,128]{1,0:T(8,128)(2,1)} %get-tuple-element.44), channel_id=1, source_target_pairs={{0,8},{8,0},{16,24},{24,16},{1,9},{9,1},{17,25},{25,17},{2,10},{10... | collective-permute-start | bytes 1572872 | tf_op jit(solution)/shard_map/ppermute | solution.py:253
  32.8 30.4 %collective-permute-start.7 = (bf16[2048,128]{1,0:T(8,128)(2,1)}, bf16[2048,128]{1,0:T(8,128)(2,1)}, u32[]{:S(2)}, u32[]{:S(2)}) collective-permute-start(bf16[2048,128]{1,0:T(8,128)(2,1)} %get-tuple-element.36), channel_id=1, source_target_pairs={{0,16},{8,24},{16,0},{24,8},{1,17},{9,25},{17,1},{25,9},{2,18},{10... | collective-permute-start | bytes 1572872 | tf_op jit(solution)/shard_map/ppermute | solution.py:253
  38.6 24.7 %collective-permute-start.8 = (bf16[2048,128]{1,0:T(8,128)(2,1)}, bf16[2048,128]{1,0:T(8,128)(2,1)}, u32[]{:S(2)}, u32[]{:S(2)}) collective-permute-start(bf16[2048,128]{1,0:T(8,128)(2,1)} %get-tuple-element.37), channel_id=1, source_target_pairs={{0,8},{8,0},{16,24},{24,16},{1,9},{9,1},{17,25},{25,17},{2,10},{10... | collective-permute-start | bytes 1572872 | tf_op jit(solution)/shard_map/ppermute | solution.py:253
  42.1 1.2 %copy-start.1 = (bf16[2048,256]{1,0:T(8,128)(2,1)S(1)}, bf16[2048,256]{1,0:T(8,128)(2,1)}, u32[]{:S(2)}) copy-start(bf16[2048,256]{1,0:T(8,128)(2,1)} %refs_0_.3) | copy-start | bytes 3145732
  43.3 1.2 %copy-start.3 = (bf16[2048,256]{1,0:T(8,128)(2,1)S(1)}, bf16[2048,256]{1,0:T(8,128)(2,1)}, u32[]{:S(2)}) copy-start(bf16[2048,256]{1,0:T(8,128)(2,1)} %q_ref.3) | copy-start | bytes 3145732
  54.9 21.2 %collective-permute-start.9 = (bf16[2048,128]{1,0:T(8,128)(2,1)}, bf16[2048,128]{1,0:T(8,128)(2,1)}, u32[]{:S(2)}, u32[]{:S(2)}) collective-permute-start(bf16[2048,128]{1,0:T(8,128)(2,1)} %get-tuple-element.39), channel_id=1, source_target_pairs={{0,16},{8,24},{16,0},{24,8},{1,17},{9,25},{17,1},{25,9},{2,18},{10... | collective-permute-start | bytes 1572872 | tf_op jit(solution)/shard_map/ppermute | solution.py:253
  56.5 19.7 %collective-permute-start.10 = (bf16[2048,128]{1,0:T(8,128)(2,1)}, bf16[2048,128]{1,0:T(8,128)(2,1)}, u32[]{:S(2)}, u32[]{:S(2)}) collective-permute-start(bf16[2048,128]{1,0:T(8,128)(2,1)} %get-tuple-element.40), channel_id=1, source_target_pairs={{0,8},{8,0},{16,24},{24,16},{1,9},{9,1},{17,25},{25,17},{2,10},{10... | collective-permute-start | bytes 1572872 | tf_op jit(solution)/shard_map/ppermute | solution.py:253
  63.3 1.2 %copy-start.2 = (bf16[2048,256]{1,0:T(8,128)(2,1)S(1)}, bf16[2048,256]{1,0:T(8,128)(2,1)}, u32[]{:S(2)}) copy-start(bf16[2048,256]{1,0:T(8,128)(2,1)} %refs_0_.3) | copy-start | bytes 3145732
  64.5 1.2 %copy-start.4 = (bf16[2048,256]{1,0:T(8,128)(2,1)S(1)}, bf16[2048,256]{1,0:T(8,128)(2,1)}, u32[]{:S(2)}) copy-start(bf16[2048,256]{1,0:T(8,128)(2,1)} %q_ref.3) | copy-start | bytes 3145732

commit v9 on v8

--- a/solution.py
+++ b/solution.py
@@ -312,8 +312,9 @@
                 k_parts[k_at ^ k_step] = exchange(outgoing[0], k_step)
                 v_parts[v_at ^ v_step] = exchange(outgoing[1], v_step)
                 done += 1
-        k_parts.update({0: keys, steps[0]: k_first})
-        v_parts.update({0: values, back[0]: v_first})
+        k_parts[steps[0]], v_parts[back[0]] = k_first, v_first
+        if pair == 0:
+            k_parts[0], v_parts[0] = keys, values
         if pair == 0:
             glob[0] = own
             for at in range(1, count):

time: 82.6 us -> 80.2 us (0.971)
  Pallas kernels: 32.8 us -> 30.9 us
  local copies, waits for them, and re-layouts: 10.9 us -> 9.74 us
    pallas_call x4, Pallas kernels: 32.8 us -> 30.9 us  [part_call(): pl.pallas_call(functools.partial(part_kernel, pair, kind, wide, gpd, toke...]
    unnamed x10 -> x12, local copies, waits for them, and re-layouts: 4.9 us -> 3.68 us
  transfers between devices with their start and end apart: 11 -> 11, of which waited for: 2 -> 3; matrix products, arithmetic and copies ran while one was open for 12% -> 13% of each run, Pallas kernels for 33% -> 32%
where the time goes in v9:
time: 80.2 us; the launch traced here: 79.8 us
  Pallas kernels  30.9 us (39%)
  waiting for transfers between devices  18.6 us (23%)
  starting transfers between devices  16.3 us (20%)
  local copies, waits for them, and re-layouts  9.74 us (12%)
  other arithmetic  4 us (5%)
    pallas_call x4, Pallas kernels, part_call(): pl.pallas_call(functools.partial(part_kernel, pair, kind, wide, gpd, toke...  30.9 us
    ppermute x11, waiting for transfers between devices, exchange(): return lax.ppermute(array, 'seq', [(i, i ^ step) for i in range(count)])  18.6 us
    ppermute x11, starting transfers between devices, exchange(): return lax.ppermute(array, 'seq', [(i, i ^ step) for i in range(count)])  16.3 us
    unnamed x12, local copies, waits for them, and re-layouts  3.68 us
    slice x2, local copies, waits for them, and re-layouts, shards(): v_parts = {0: v_held[:, lanes], back[0]: v_first[:, lanes]}  3.68 us
  transfers between devices with their start and end apart: 11, of which 3 were waited for; matrix products, arithmetic and copies ran while one was open for 13% of the time, Pallas kernels for 32%

profile of v9, /device:TPU:0, one launch (start us, length us, event | category | flops | bytes accessed | tf_op | source)
XLA Modules:
  0.0 79.8 jit_solution(14803426431709419231)
XLA Ops:
  0.0 2.9 %collective-permute-start.1 = (bf16[2048,256]{1,0:T(8,128)(2,1)}, bf16[2048,256]{1,0:T(8,128)(2,1)S(1)}, u32[]{:S(2)}, u32[]{:S(2)}) collective-permute-start(bf16[2048,256]{1,0:T(8,128)(2,1)} %refs_0_.1), channel_id=1, source_target_pairs={{0,8},{8,0},{16,24},{24,16},{1,9},{9,1},{17,25},{25,17},{2,10},{10... | collective-permute-start | bytes 3145736 | tf_op jit(solution)/shard_map/ppermute | solution.py:253
  2.9 1.5 %collective-permute-start.2 = (bf16[2048,256]{1,0:T(8,128)(2,1)}, bf16[2048,256]{1,0:T(8,128)(2,1)S(1)}, u32[]{:S(2)}, u32[]{:S(2)}) collective-permute-start(bf16[2048,256]{1,0:T(8,128)(2,1)} %refs_3_.1), channel_id=1, source_target_pairs={{0,16},{8,24},{16,0},{24,8},{1,17},{9,25},{17,1},{25,9},{2,18},{10... | collective-permute-start | bytes 3145736 | tf_op jit(solution)/shard_map/ppermute | solution.py:253
  5.1 0.7 fusion.5
  6.0 2.6 %fusion.22 = (bf16[2048,128]{1,0:T(8,128)(2,1)}, bf16[2048,128]{1,0:T(8,128)(2,1)S(1)}, bf16[2048,128]{1,0:T(8,128)(2,1)S(1)}, bf16[2048,128]{1,0:T(8,128)(2,1)}) fusion(bf16[2048,256]{1,0:T(8,128)(2,1)} %refs_3_.1, bf16[2048,256]{1,0:T(8,128)(2,1)} %refs_0_.1), kind=kLoop, calls=%fused_computation.59 | loop fusion | bytes 4194304 | tf_op jit(solution)/shard_map/slice | solution.py:300
  8.7 1.0 %fusion.2 = (bf16[2064,128]{1,0:T(8,128)(2,1)}, bf16[2064,128]{1,0:T(8,128)(2,1)}) fusion(bf16[1,2]{1,0:T(2,128)(2,1)S(1)} %convert_bitcast_fusion, bf16[2048,128]{1,0:T(8,128)(2,1)S(1)} %get-tuple-element.48, bf16[2048,128]{1,0:T(8,128)(2,1)S(1)} %get-tuple-element.59), kind=kLoop, calls=%fused_computation.3 | loop fusion | flops 2377728 | bytes 2105348 | tf_op jit(solution)/shard_map/concatenate | solution.py:303
  9.7 1.9 %collective-permute-start.3 = (bf16[2064,128]{1,0:T(8,128)(2,1)}, bf16[2064,128]{1,0:T(8,128)(2,1)}, u32[]{:S(2)}, u32[]{:S(2)}) collective-permute-start(bf16[2064,128]{1,0:T(8,128)(2,1)} %get-tuple-element.57), channel_id=1, source_target_pairs={{0,8},{8,0},{16,24},{24,16},{1,9},{9,1},{17,25},{25,17},{2,10},{10... | collective-permute-start | bytes 1585160 | tf_op jit(solution)/shard_map/ppermute | solution.py:253
  11.6 1.5 %collective-permute-start.4 = (bf16[2064,128]{1,0:T(8,128)(2,1)}, bf16[2064,128]{1,0:T(8,128)(2,1)}, u32[]{:S(2)}, u32[]{:S(2)}) collective-permute-start(bf16[2064,128]{1,0:T(8,128)(2,1)} %get-tuple-element.58), channel_id=1, source_target_pairs={{0,16},{8,24},{16,0},{24,8},{1,17},{9,25},{17,1},{25,9},{2,18},{10... | collective-permute-start | bytes 1585160 | tf_op jit(solution)/shard_map/ppermute | solution.py:253
  14.0 13.2 %collective-permute-done.1.refs_1_ = bf16[2048,256]{1,0:T(8,128)(2,1)S(1)} collective-permute-done((bf16[2048,256]{1,0:T(8,128)(2,1)}, bf16[2048,256]{1,0:T(8,128)(2,1)S(1)}, u32[]{:S(2)}, u32[]{:S(2)}) %collective-permute-start.1) | collective-permute-done | bytes 1048608 | tf_op jit(solution)/shard_map/ppermute | solution.py:253
  27.1 1.1 %fusion.21 = (bf16[2048,128]{1,0:T(8,128)(2,1)}, bf16[2048,128]{1,0:T(8,128)(2,1)}) fusion(bf16[2048,256]{1,0:T(8,128)(2,1)S(1)} %collective-permute-done.1.refs_1_), kind=kLoop, calls=%fused_computation.58 | loop fusion | bytes 2097152 | tf_op jit(solution)/shard_map/slice | solution.py:299
  28.2 2.1 %collective-permute-start.5 = (bf16[2048,128]{1,0:T(8,128)(2,1)}, bf16[2048,128]{1,0:T(8,128)(2,1)}, u32[]{:S(2)}, u32[]{:S(2)}) collective-permute-start(bf16[2048,128]{1,0:T(8,128)(2,1)} %get-tuple-element.46), channel_id=1, source_target_pairs={{0,16},{8,24},{16,0},{24,8},{1,17},{9,25},{17,1},{25,9},{2,18},{10... | collective-permute-start | bytes 1572872 | tf_op jit(solution)/shard_map/ppermute | solution.py:253
  30.3 1.0 %fusion.20 = (bf16[2048,128]{1,0:T(8,128)(2,1)}, bf16[2048,128]{1,0:T(8,128)(2,1)}) fusion(bf16[2048,256]{1,0:T(8,128)(2,1)S(1)} %collective-permute-done.2.refs_5_), kind=kLoop, calls=%fused_computation.57 | loop fusion | bytes 2097152 | tf_op jit(solution)/shard_map/slice | solution.py:300
  31.4 1.5 %collective-permute-start.6 = (bf16[2048,128]{1,0:T(8,128)(2,1)}, bf16[2048,128]{1,0:T(8,128)(2,1)}, u32[]{:S(2)}, u32[]{:S(2)}) collective-permute-start(bf16[2048,128]{1,0:T(8,128)(2,1)} %get-tuple-element.44), channel_id=1, source_target_pairs={{0,8},{8,0},{16,24},{24,16},{1,9},{9,1},{17,25},{25,17},{2,10},{10... | collective-permute-start | bytes 1572872 | tf_op jit(solution)/shard_map/ppermute | solution.py:253
  33.9 4.7 %collective-permute-done.3.refs_4_ = bf16[2064,128]{1,0:T(8,128)(2,1)} collective-permute-done((bf16[2064,128]{1,0:T(8,128)(2,1)}, bf16[2064,128]{1,0:T(8,128)(2,1)}, u32[]{:S(2)}, u32[]{:S(2)}) %collective-permute-start.3) | collective-permute-done | bytes 528416 | tf_op jit(solution)/shard_map/ppermute | solution.py:253
  38.6 2.1 %collective-permute-start.8 = (bf16[2048,128]{1,0:T(8,128)(2,1)}, bf16[2048,128]{1,0:T(8,128)(2,1)}, u32[]{:S(2)}, u32[]{:S(2)}) collective-permute-start(bf16[2048,128]{1,0:T(8,128)(2,1)} %get-tuple-element.37.refs_3_), channel_id=1, source_target_pairs={{0,8},{8,0},{16,24},{24,16},{1,9},{9,1},{17,25},{25,17},{2,10},{10... | collective-permute-start | bytes 1572872 | tf_op jit(solution)/shard_map/ppermute | solution.py:253
  40.6 0.7 add_bitcast_fusion.1
  42.1 1.2 %copy-done.1 = bf16[2048,256]{1,0:T(8,128)(2,1)S(1)} copy-done((bf16[2048,256]{1,0:T(8,128)(2,1)S(1)}, bf16[2048,256]{1,0:T(8,128)(2,1)}, u32[]{:S(2)}) %copy-start.1) | copy-done | bytes 1048600
  43.3 1.2 %copy-done.4 = bf16[2048,256]{1,0:T(8,128)(2,1)S(1)} copy-done((bf16[2048,256]{1,0:T(8,128)(2,1)S(1)}, bf16[2048,256]{1,0:T(8,128)(2,1)}, u32[]{:S(2)}) %copy-start.4) | copy-done | bytes 1048600
  44.5 9.9 %early.2 = (f32[2176,128]{1,0:T(8,128)S(1)}, f32[2176,128]{1,0:T(8,128)S(1)}, bf16[2048,128]{1,0:T(8,128)(2,1)S(1)}) custom-call(s32[288]{0:T(512)S(1)} %fusion.17.lists_ref, f32[288]{0:T(512)S(1)} %fusion.16.flags_ref, s32[6]{0:T(128)S(1)} %pad_add_fusion.4.glob_ref, s32[2]{0:T(128)S(1)} %broadcast_subtract_fusion.own_ref, bf16[2048,256]{1,0:T(8,128)(2,1)S(1)} %copy-done.4, ...), custom_call_target="tpu_custom_call" | custom-call | flops 4831838208 | bytes 3145728 | tf_op jit(solution)/shard_map/early/pallas_call | solution.py:233
  54.4 1.6 %collective-permute-start.9 = (bf16[2048,128]{1,0:T(8,128)(2,1)}, bf16[2048,128]{1,0:T(8,128)(2,1)}, u32[]{:S(2)}, u32[]{:S(2)}) collective-permute-start(bf16[2048,128]{1,0:T(8,128)(2,1)} %get-tuple-element.39), channel_id=1, source_target_pairs={{0,16},{8,24},{16,0},{24,8},{1,17},{9,25},{17,1},{25,9},{2,18},{10... | collective-permute-start | bytes 1572872 | tf_op jit(solution)/shard_map/ppermute | solution.py:253
  56.5 5.7 %late.2.refs_4_ = bf16[2048,256]{1,0:T(8,128)(2,1)} custom-call(s32[224]{0:T(256)S(1)} %select_n.64.lists_ref, f32[224]{0:T(256)S(1)} %reshape.77.flags_ref, s32[2]{0:T(128)S(1)} %collective-permute-done.glob_ref, s32[2]{0:T(128)S(1)} %broadcast_subtract_fusion.own_ref, bf16[2048,128]{1,0:T(8,128)(2,1)S(1)} %get-tuple-element.32.q_ref, ...), custom_call_target="tpu_custom_call" | custom-call | flops 2147483648 | bytes 1048576 | tf_op jit(solution)/shard_map/late/pallas_call | solution.py:233
  62.4 0.7 collective-permute-done.7.refs_2_
  63.2 1.2 %copy-done.5 = bf16[2048,256]{1,0:T(8,128)(2,1)S(1)} copy-done((bf16[2048,256]{1,0:T(8,128)(2,1)S(1)}, bf16[2048,256]{1,0:T(8,128)(2,1)}, u32[]{:S(2)}) %copy-start.5) | copy-done | bytes 1048600
  64.4 9.7 %early.3 = (f32[2176,128]{1,0:T(8,128)S(1)}, f32[2176,128]{1,0:T(8,128)S(1)}, bf16[2048,128]{1,0:T(8,128)(2,1)S(1)}) custom-call(s32[288]{0:T(512)S(1)} %fusion.19.lists_ref, f32[288]{0:T(512)S(1)} %fusion.18.flags_ref, s32[6]{0:T(128)S(1)} %pad_add_fusion.4.glob_ref, s32[2]{0:T(128)S(1)} %broadcast_subtract_fusion.own_ref, bf16[2048,256]{1,0:T(8,128)(2,1)S(1)} %copy-done.5, ...), custom_call_target="tpu_custom_call" | custom-call | flops 4831838208 | bytes 3145728 | tf_op jit(solution)/shard_map/early/pallas_call | solution.py:233
  74.1 5.6 %late.3 = bf16[2048,256]{1,0:T(8,128)(2,1)} custom-call(s32[224]{0:T(256)S(1)} %select_n.62.lists_ref, f32[224]{0:T(256)S(1)} %reshape.76.flags_ref, s32[2]{0:T(128)S(1)} %collective-permute-done.glob_ref, s32[2]{0:T(128)S(1)} %broadcast_subtract_fusion.own_ref, bf16[2048,128]{1,0:T(8,128)(2,1)S(1)} %get-tuple-element.38.q_ref, ...), custom_call_target="tpu_custom_call", output_to_operand_aliasing={{}: (9, {})} | custom-call | flops 2147483648 | bytes 1048576 | tf_op jit(solution)/shard_map/late/pallas_call | solution.py:233
  (56 shorter events, 4.1 us)
Async XLA Ops:
  0.0 27.1 %collective-permute-start.1 = (bf16[2048,256]{1,0:T(8,128)(2,1)}, bf16[2048,256]{1,0:T(8,128)(2,1)S(1)}, u32[]{:S(2)}, u32[]{:S(2)}) collective-permute-start(bf16[2048,256]{1,0:T(8,128)(2,1)} %refs_0_.1), channel_id=1, source_target_pairs={{0,8},{8,0},{16,24},{24,16},{1,9},{9,1},{17,25},{25,17},{2,10},{10... | collective-permute-start | bytes 3145736 | tf_op jit(solution)/shard_map/ppermute | solution.py:253
  2.9 27.4 %collective-permute-start.2 = (bf16[2048,256]{1,0:T(8,128)(2,1)}, bf16[2048,256]{1,0:T(8,128)(2,1)S(1)}, u32[]{:S(2)}, u32[]{:S(2)}) collective-permute-start(bf16[2048,256]{1,0:T(8,128)(2,1)} %refs_3_.1), channel_id=1, source_target_pairs={{0,16},{8,24},{16,0},{24,8},{1,17},{9,25},{17,1},{25,9},{2,18},{10... | collective-permute-start | bytes 3145736 | tf_op jit(solution)/shard_map/ppermute | solution.py:253
  5.9 26.9 %collective-permute-start = (s32[2]{0:T(128)S(1)}, s32[2]{0:T(128)S(1)}, u32[]{:S(2)}, u32[]{:S(2)}) collective-permute-start(s32[2]{0:T(128)S(1)} %broadcast_subtract_fusion.own_ref), channel_id=1, source_target_pairs={{0,24},{8,16},{16,8},{24,0},{1,25},{9,17},{17,9},{25,1},{2,26},{10... | collective-permute-start | bytes 32 | tf_op jit(solution)/shard_map/ppermute | solution.py:253
  9.7 28.9 %collective-permute-start.3 = (bf16[2064,128]{1,0:T(8,128)(2,1)}, bf16[2064,128]{1,0:T(8,128)(2,1)}, u32[]{:S(2)}, u32[]{:S(2)}) collective-permute-start(bf16[2064,128]{1,0:T(8,128)(2,1)} %get-tuple-element.57), channel_id=1, source_target_pairs={{0,8},{8,0},{16,24},{24,16},{1,9},{9,1},{17,25},{25,17},{2,10},{10... | collective-permute-start | bytes 1585160 | tf_op jit(solution)/shard_map/ppermute | solution.py:253
  11.6 29.7 %collective-permute-start.4 = (bf16[2064,128]{1,0:T(8,128)(2,1)}, bf16[2064,128]{1,0:T(8,128)(2,1)}, u32[]{:S(2)}, u32[]{:S(2)}) collective-permute-start(bf16[2064,128]{1,0:T(8,128)(2,1)} %get-tuple-element.58), channel_id=1, source_target_pairs={{0,16},{8,24},{16,0},{24,8},{1,17},{9,25},{17,1},{25,9},{2,18},{10... | collective-permute-start | bytes 1585160 | tf_op jit(solution)/shard_map/ppermute | solution.py:253
  28.2 13.8 %copy-start = (bf16[2048,256]{1,0:T(8,128)(2,1)S(1)}, bf16[2048,256]{1,0:T(8,128)(2,1)}, u32[]{:S(2)}) copy-start(bf16[2048,256]{1,0:T(8,128)(2,1)} %refs_3_.1) | copy-start | bytes 3145732
  28.2 27.8 %collective-permute-start.5 = (bf16[2048,128]{1,0:T(8,128)(2,1)}, bf16[2048,128]{1,0:T(8,128)(2,1)}, u32[]{:S(2)}, u32[]{:S(2)}) collective-permute-start(bf16[2048,128]{1,0:T(8,128)(2,1)} %get-tuple-element.46), channel_id=1, source_target_pairs={{0,16},{8,24},{16,0},{24,8},{1,17},{9,25},{17,1},{25,9},{2,18},{10... | collective-permute-start | bytes 1572872 | tf_op jit(solution)/shard_map/ppermute | solution.py:253
  31.4 25.2 %collective-permute-start.6 = (bf16[2048,128]{1,0:T(8,128)(2,1)}, bf16[2048,128]{1,0:T(8,128)(2,1)}, u32[]{:S(2)}, u32[]{:S(2)}) collective-permute-start(bf16[2048,128]{1,0:T(8,128)(2,1)} %get-tuple-element.44), channel_id=1, source_target_pairs={{0,8},{8,0},{16,24},{24,16},{1,9},{9,1},{17,25},{25,17},{2,10},{10... | collective-permute-start | bytes 1572872 | tf_op jit(solution)/shard_map/ppermute | solution.py:253
  33.3 29.8 %collective-permute-start.7 = (bf16[2048,128]{1,0:T(8,128)(2,1)}, bf16[2048,128]{1,0:T(8,128)(2,1)}, u32[]{:S(2)}, u32[]{:S(2)}) collective-permute-start(bf16[2048,128]{1,0:T(8,128)(2,1)} %get-tuple-element.36.refs_0_), channel_id=1, source_target_pairs={{0,16},{8,24},{16,0},{24,8},{1,17},{9,25},{17,1},{25,9},{2,18},{10... | collective-permute-start | bytes 1572872 | tf_op jit(solution)/shard_map/ppermute | solution.py:253
  38.6 24.6 %collective-permute-start.8 = (bf16[2048,128]{1,0:T(8,128)(2,1)}, bf16[2048,128]{1,0:T(8,128)(2,1)}, u32[]{:S(2)}, u32[]{:S(2)}) collective-permute-start(bf16[2048,128]{1,0:T(8,128)(2,1)} %get-tuple-element.37.refs_3_), channel_id=1, source_target_pairs={{0,8},{8,0},{16,24},{24,16},{1,9},{9,1},{17,25},{25,17},{2,10},{10... | collective-permute-start | bytes 1572872 | tf_op jit(solution)/shard_map/ppermute | solution.py:253
  42.1 1.2 %copy-start.1 = (bf16[2048,256]{1,0:T(8,128)(2,1)S(1)}, bf16[2048,256]{1,0:T(8,128)(2,1)}, u32[]{:S(2)}) copy-start(bf16[2048,256]{1,0:T(8,128)(2,1)} %refs_0_.1) | copy-start | bytes 3145732
  43.3 1.2 %copy-start.4 = (bf16[2048,256]{1,0:T(8,128)(2,1)S(1)}, bf16[2048,256]{1,0:T(8,128)(2,1)}, u32[]{:S(2)}) copy-start(bf16[2048,256]{1,0:T(8,128)(2,1)} %q_ref.3) | copy-start | bytes 3145732
  54.4 8.8 %copy-start.2 = (bf16[2048,128]{1,0:T(8,128)(2,1)S(1)}, bf16[2048,128]{1,0:T(8,128)(2,1)}, u32[]{:S(2)}) copy-start(bf16[2048,128]{1,0:T(8,128)(2,1)} %get-tuple-element.37.refs_3_) | copy-start | bytes 1572868
  54.4 8.8 %copy-start.3 = (bf16[2048,128]{1,0:T(8,128)(2,1)S(1)}, bf16[2048,128]{1,0:T(8,128)(2,1)}, u32[]{:S(2)}) copy-start(bf16[2048,128]{1,0:T(8,128)(2,1)} %get-tuple-element.36.refs_0_) | copy-start | bytes 1572868
  54.4 19.7 %collective-permute-start.9 = (bf16[2048,128]{1,0:T(8,128)(2,1)}, bf16[2048,128]{1,0:T(8,128)(2,1)}, u32[]{:S(2)}, u32[]{:S(2)}) collective-permute-start(bf16[2048,128]{1,0:T(8,128)(2,1)} %get-tuple-element.39), channel_id=1, source_target_pairs={{0,16},{8,24},{16,0},{24,8},{1,17},{9,25},{17,1},{25,9},{2,18},{10... | collective-permute-start | bytes 1572872 | tf_op jit(solution)/shard_map/ppermute | solution.py:253
  56.0 18.2 %collective-permute-start.10 = (bf16[2048,128]{1,0:T(8,128)(2,1)}, bf16[2048,128]{1,0:T(8,128)(2,1)}, u32[]{:S(2)}, u32[]{:S(2)}) collective-permute-start(bf16[2048,128]{1,0:T(8,128)(2,1)} %get-tuple-element.40), channel_id=1, source_target_pairs={{0,8},{8,0},{16,24},{24,16},{1,9},{9,1},{17,25},{25,17},{2,10},{10... | collective-permute-start | bytes 1572872 | tf_op jit(solution)/shard_map/ppermute | solution.py:253
  63.2 1.2 %copy-start.5 = (bf16[2048,256]{1,0:T(8,128)(2,1)S(1)}, bf16[2048,256]{1,0:T(8,128)(2,1)}, u32[]{:S(2)}) copy-start(bf16[2048,256]{1,0:T(8,128)(2,1)} %q_ref.3) | copy-start | bytes 3145732

commit v10 on v9

--- a/solution.py
+++ b/solution.py
@@ -37,9 +37,16 @@
         out_ref, k_glob, v_glob = refs[3:] if pair > 0 else refs[2:]
         k_all, v_all = k_parts[0], v_parts[0]
     else:
-        out_ref, out_l_ref, q_all, k_glob, v_glob, k_all, v_all, sems = refs
+        out_ref, out_l_ref, q_all, *q_next, k_glob, v_glob, k_all, v_all, sems = refs
         lanes = pl.ds(pair * LANES, LANES)
-        copies = [pltpu.make_async_copy(q_ref.at[:, lanes], q_all, sems.at[2 * ranges])]
+        if pair == 0:
+            q_halves = [q_ref.at[:, lanes], q_ref.at[:, pl.ds(LANES, LANES)]]
+        else:
+            q_halves = [q_ref]
+        copies = [
+            pltpu.make_async_copy(source, target, sems.at[2 * ranges + i])
+            for i, (source, target) in enumerate(zip(q_halves, [q_all, *q_next]))
+        ]
         for j in range(ranges):
             span = pl.ds(j * tokens, tokens)
             for side, (source, target) in enumerate(((k_parts[j], k_all), (v_parts[j], v_all))):
@@ -216,9 +223,10 @@
         operands.append(so_far)
         in_specs.append(hbm)
     if kind == "early":
-        out_specs = [full(state_rows)] * 2 + [full(tokens)]
+        handed = 2 if pair == 0 else 1
+        out_specs = [full(state_rows)] * 2 + [full(tokens)] * handed
         out_shape = [jax.ShapeDtypeStruct((state_rows, LANES), jnp.float32)] * 2
-        out_shape.append(jax.ShapeDtypeStruct((tokens, LANES), queries.dtype))
+        out_shape += [jax.ShapeDtypeStruct((tokens, LANES), queries.dtype)] * handed
     else:
         out_specs = half
         out_shape = jax.ShapeDtypeStruct((tokens, columns), jnp.bfloat16)
@@ -229,7 +237,7 @@
     scratch = [pltpu.VMEM((globs, LANES), jnp.bfloat16)] * 2
     if kind != "late":
         scratch += [pltpu.VMEM((keys_all, LANES), jnp.bfloat16)] * 2
-        scratch.append(pltpu.SemaphoreType.DMA((2 * ranges + 1,)))
+        scratch.append(pltpu.SemaphoreType.DMA((2 * ranges + 2,)))
     return pl.pallas_call(
         functools.partial(part_kernel, pair, kind, wide, gpd, tokens, shared),
         grid=(1,),
@@ -280,7 +288,7 @@
     glob = {at: exchange(own, at) for at in direct}
     halo = jnp.where(row == 0, window[:, :1], window[:, 2:])
 
-    def call(kind, pair, k_parts, v_parts, shared, listed, spare, state=(), so_far=None):
+    def call(kind, pair, queries, k_parts, v_parts, shared, listed, spare, state=(), so_far=None):
         start, stop = (last, count) if kind == "late" else (0, last)
         mine = rand[:, 2 * pair : 2 * pair + 2].reshape(blocks, 2 * RAND)
         lists = jnp.concatenate([listed, mine], axis=1)
@@ -293,7 +301,7 @@
             state, so_far,
         )
 
-    out, state = None, None
+    out, state, mine = None, None, queries
     for pair in range(pairs):
         lanes = slice(pair * LANES, (pair + 1) * LANES)
         k_parts = {0: k_held[:, lanes], steps[0]: k_first[:, lanes]}
@@ -324,9 +332,11 @@
             glob = jnp.concatenate([glob[at] + at * blocks for at in range(count)])
         else:
             window = lax.optimization_barrier((window, out))[0]
-        state = call("early", pair, k_parts, v_parts, 3, window, row)
+        *state, mine = call("early", pair, mine, k_parts, v_parts, 3, window, row)
+        if pair > 0:
+            state.append(mine)
         spare = glob[gpd * last] - last * blocks
-        out = call("late", pair, k_parts, v_parts, 1, halo, spare, state, out)
+        out = call("late", pair, queries, k_parts, v_parts, 1, halo, spare, state, out)
     return out
 
 

time: 80.2 us -> 80 us (level)
    unnamed x12 -> x14, local copies, waits for them, and re-layouts: 3.68 us -> 3.5 us
where the time goes in v10:
time: 80 us; the launch traced here: 79.5 us
  Pallas kernels  30.9 us (39%)
  waiting for transfers between devices  18.5 us (23%)
  starting transfers between devices  16.3 us (20%)
  local copies, waits for them, and re-layouts  9.57 us (12%)
  other arithmetic  4.01 us (5%)
    pallas_call x4, Pallas kernels, part_call(): pl.pallas_call(functools.partial(part_kernel, pair, kind, wide, gpd, toke...  30.9 us
    ppermute x11, waiting for transfers between devices, exchange(): return lax.ppermute(array, 'seq', [(i, i ^ step) for i in range(count)])  18.5 us
    ppermute x11, starting transfers between devices, exchange(): return lax.ppermute(array, 'seq', [(i, i ^ step) for i in range(count)])  16.3 us
    slice x2, local copies, waits for them, and re-layouts, shards(): v_parts = {0: v_held[:, lanes], back[0]: v_first[:, lanes]}  3.73 us
    unnamed x14, local copies, waits for them, and re-layouts  3.5 us
  transfers between devices with their start and end apart: 11, of which 3 were waited for; matrix products, arithmetic and copies ran while one was open for 13% of the time, Pallas kernels for 32%

profile of v10, /device:TPU:0, one launch (start us, length us, event | category | flops | bytes accessed | tf_op | source)
XLA Modules:
  0.0 79.5 jit_solution(4852998786042248074)
XLA Ops:
  0.0 2.9 %collective-permute-start.1 = (bf16[2048,256]{1,0:T(8,128)(2,1)}, bf16[2048,256]{1,0:T(8,128)(2,1)S(1)}, u32[]{:S(2)}, u32[]{:S(2)}) collective-permute-start(bf16[2048,256]{1,0:T(8,128)(2,1)} %refs_0_.1), channel_id=1, source_target_pairs={{0,8},{8,0},{16,24},{24,16},{1,9},{9,1},{17,25},{25,17},{2,10},{10... | collective-permute-start | bytes 3145736 | tf_op jit(solution)/shard_map/ppermute | solution.py:261
  2.9 1.5 %collective-permute-start.2 = (bf16[2048,256]{1,0:T(8,128)(2,1)}, bf16[2048,256]{1,0:T(8,128)(2,1)S(1)}, u32[]{:S(2)}, u32[]{:S(2)}) collective-permute-start(bf16[2048,256]{1,0:T(8,128)(2,1)} %refs_3_.1), channel_id=1, source_target_pairs={{0,16},{8,24},{16,0},{24,8},{1,17},{9,25},{17,1},{25,9},{2,18},{10... | collective-permute-start | bytes 3145736 | tf_op jit(solution)/shard_map/ppermute | solution.py:261
  5.1 0.7 fusion.5
  6.0 2.7 %fusion.22 = (bf16[2048,128]{1,0:T(8,128)(2,1)}, bf16[2048,128]{1,0:T(8,128)(2,1)S(1)}, bf16[2048,128]{1,0:T(8,128)(2,1)S(1)}, bf16[2048,128]{1,0:T(8,128)(2,1)}) fusion(bf16[2048,256]{1,0:T(8,128)(2,1)} %refs_3_.1, bf16[2048,256]{1,0:T(8,128)(2,1)} %refs_0_.1), kind=kLoop, calls=%fused_computation.59 | loop fusion | bytes 4194304 | tf_op jit(solution)/shard_map/slice | solution.py:308
  8.7 1.0 %fusion.2 = (bf16[2064,128]{1,0:T(8,128)(2,1)}, bf16[2064,128]{1,0:T(8,128)(2,1)}) fusion(bf16[1,2]{1,0:T(2,128)(2,1)S(1)} %convert_bitcast_fusion, bf16[2048,128]{1,0:T(8,128)(2,1)S(1)} %get-tuple-element.50, bf16[2048,128]{1,0:T(8,128)(2,1)S(1)} %get-tuple-element.61), kind=kLoop, calls=%fused_computation.3 | loop fusion | flops 2377728 | bytes 2105348 | tf_op jit(solution)/shard_map/concatenate | solution.py:311
  9.7 1.9 %collective-permute-start.3 = (bf16[2064,128]{1,0:T(8,128)(2,1)}, bf16[2064,128]{1,0:T(8,128)(2,1)}, u32[]{:S(2)}, u32[]{:S(2)}) collective-permute-start(bf16[2064,128]{1,0:T(8,128)(2,1)} %get-tuple-element.59), channel_id=1, source_target_pairs={{0,8},{8,0},{16,24},{24,16},{1,9},{9,1},{17,25},{25,17},{2,10},{10... | collective-permute-start | bytes 1585160 | tf_op jit(solution)/shard_map/ppermute | solution.py:261
  11.7 1.5 %collective-permute-start.4 = (bf16[2064,128]{1,0:T(8,128)(2,1)}, bf16[2064,128]{1,0:T(8,128)(2,1)}, u32[]{:S(2)}, u32[]{:S(2)}) collective-permute-start(bf16[2064,128]{1,0:T(8,128)(2,1)} %get-tuple-element.60), channel_id=1, source_target_pairs={{0,16},{8,24},{16,0},{24,8},{1,17},{9,25},{17,1},{25,9},{2,18},{10... | collective-permute-start | bytes 1585160 | tf_op jit(solution)/shard_map/ppermute | solution.py:261
  14.0 13.1 %collective-permute-done.1.refs_1_ = bf16[2048,256]{1,0:T(8,128)(2,1)S(1)} collective-permute-done((bf16[2048,256]{1,0:T(8,128)(2,1)}, bf16[2048,256]{1,0:T(8,128)(2,1)S(1)}, u32[]{:S(2)}, u32[]{:S(2)}) %collective-permute-start.1) | collective-permute-done | bytes 1048608 | tf_op jit(solution)/shard_map/ppermute | solution.py:261
  27.1 1.1 %fusion.21 = (bf16[2048,128]{1,0:T(8,128)(2,1)}, bf16[2048,128]{1,0:T(8,128)(2,1)}) fusion(bf16[2048,256]{1,0:T(8,128)(2,1)S(1)} %collective-permute-done.1.refs_1_), kind=kLoop, calls=%fused_computation.58 | loop fusion | bytes 2097152 | tf_op jit(solution)/shard_map/slice | solution.py:307
  28.2 2.1 %collective-permute-start.5 = (bf16[2048,128]{1,0:T(8,128)(2,1)}, bf16[2048,128]{1,0:T(8,128)(2,1)}, u32[]{:S(2)}, u32[]{:S(2)}) collective-permute-start(bf16[2048,128]{1,0:T(8,128)(2,1)} %get-tuple-element.48), channel_id=1, source_target_pairs={{0,16},{8,24},{16,0},{24,8},{1,17},{9,25},{17,1},{25,9},{2,18},{10... | collective-permute-start | bytes 1572872 | tf_op jit(solution)/shard_map/ppermute | solution.py:261
  30.3 1.1 %fusion.20 = (bf16[2048,128]{1,0:T(8,128)(2,1)}, bf16[2048,128]{1,0:T(8,128)(2,1)}) fusion(bf16[2048,256]{1,0:T(8,128)(2,1)S(1)} %collective-permute-done.2.refs_5_), kind=kLoop, calls=%fused_computation.57 | loop fusion | bytes 2097152 | tf_op jit(solution)/shard_map/slice | solution.py:308
  31.3 1.5 %collective-permute-start.6 = (bf16[2048,128]{1,0:T(8,128)(2,1)}, bf16[2048,128]{1,0:T(8,128)(2,1)}, u32[]{:S(2)}, u32[]{:S(2)}) collective-permute-start(bf16[2048,128]{1,0:T(8,128)(2,1)} %get-tuple-element.46), channel_id=1, source_target_pairs={{0,8},{8,0},{16,24},{24,16},{1,9},{9,1},{17,25},{25,17},{2,10},{10... | collective-permute-start | bytes 1572872 | tf_op jit(solution)/shard_map/ppermute | solution.py:261
  33.9 4.7 %collective-permute-done.3.refs_4_ = bf16[2064,128]{1,0:T(8,128)(2,1)} collective-permute-done((bf16[2064,128]{1,0:T(8,128)(2,1)}, bf16[2064,128]{1,0:T(8,128)(2,1)}, u32[]{:S(2)}, u32[]{:S(2)}) %collective-permute-start.3) | collective-permute-done | bytes 528416 | tf_op jit(solution)/shard_map/ppermute | solution.py:261
  38.6 2.1 %collective-permute-start.8 = (bf16[2048,128]{1,0:T(8,128)(2,1)}, bf16[2048,128]{1,0:T(8,128)(2,1)}, u32[]{:S(2)}, u32[]{:S(2)}) collective-permute-start(bf16[2048,128]{1,0:T(8,128)(2,1)} %get-tuple-element.39.refs_3_), channel_id=1, source_target_pairs={{0,8},{8,0},{16,24},{24,16},{1,9},{9,1},{17,25},{25,17},{2,10},{10... | collective-permute-start | bytes 1572872 | tf_op jit(solution)/shard_map/ppermute | solution.py:261
  40.6 0.7 add_bitcast_fusion.1
  41.3 0.7 add_bitcast_fusion
  42.1 1.2 %copy-done.1 = bf16[2048,256]{1,0:T(8,128)(2,1)S(1)} copy-done((bf16[2048,256]{1,0:T(8,128)(2,1)S(1)}, bf16[2048,256]{1,0:T(8,128)(2,1)}, u32[]{:S(2)}) %copy-start.1) | copy-done | bytes 1048600
  43.3 1.2 %copy-done.4 = bf16[2048,256]{1,0:T(8,128)(2,1)S(1)} copy-done((bf16[2048,256]{1,0:T(8,128)(2,1)S(1)}, bf16[2048,256]{1,0:T(8,128)(2,1)}, u32[]{:S(2)}) %copy-start.4) | copy-done | bytes 1048600
  44.5 10.0 %early.2 = (f32[2176,128]{1,0:T(8,128)S(1)}, f32[2176,128]{1,0:T(8,128)S(1)}, bf16[2048,128]{1,0:T(8,128)(2,1)S(1)}, bf16[2048,128]{1,0:T(8,128)(2,1)S(1)}) custom-call(s32[288]{0:T(512)S(1)} %fusion.17.lists_ref, f32[288]{0:T(512)S(1)} %fusion.16.flags_ref, s32[6]{0:T(128)S(1)} %pad_add_fusion.4.glob_ref, s32[2]{0:T(128)S(1)} %broadcast_subtract_fusion.own_ref, ...), custom_call_target="tpu_custom_call" | custom-call | flops 4831838208 | bytes 3145728 | tf_op jit(solution)/shard_map/early/pallas_call | solution.py:241
  54.5 1.6 %collective-permute-start.9 = (bf16[2048,128]{1,0:T(8,128)(2,1)}, bf16[2048,128]{1,0:T(8,128)(2,1)}, u32[]{:S(2)}, u32[]{:S(2)}) collective-permute-start(bf16[2048,128]{1,0:T(8,128)(2,1)} %get-tuple-element.41), channel_id=1, source_target_pairs={{0,16},{8,24},{16,0},{24,8},{1,17},{9,25},{17,1},{25,9},{2,18},{10... | collective-permute-start | bytes 1572872 | tf_op jit(solution)/shard_map/ppermute | solution.py:261
  56.6 5.7 %late.2.refs_4_ = bf16[2048,256]{1,0:T(8,128)(2,1)} custom-call(s32[224]{0:T(256)S(1)} %select_n.64.lists_ref, f32[224]{0:T(256)S(1)} %reshape.77.flags_ref, s32[2]{0:T(128)S(1)} %collective-permute-done.glob_ref, s32[2]{0:T(128)S(1)} %broadcast_subtract_fusion.own_ref, bf16[2048,128]{1,0:T(8,128)(2,1)S(1)} %get-tuple-element.33.q_ref, ...), custom_call_target="tpu_custom_call" | custom-call | flops 2147483648 | bytes 1048576 | tf_op jit(solution)/shard_map/late/pallas_call | solution.py:241
  63.2 1.0 %copy-done.6 = bf16[2048,128]{1,0:T(8,128)(2,1)S(1)} copy-done((bf16[2048,128]{1,0:T(8,128)(2,1)S(1)}, bf16[2048,128]{1,0:T(8,128)(2,1)}, u32[]{:S(2)}) %copy-start.6) | copy-done | bytes 524312
  64.2 9.7 %early.3 = (f32[2176,128]{1,0:T(8,128)S(1)}, f32[2176,128]{1,0:T(8,128)S(1)}, bf16[2048,128]{1,0:T(8,128)(2,1)S(1)}) custom-call(s32[288]{0:T(512)S(1)} %fusion.19.lists_ref, f32[288]{0:T(512)S(1)} %fusion.18.flags_ref, s32[6]{0:T(128)S(1)} %pad_add_fusion.4.glob_ref, s32[2]{0:T(128)S(1)} %broadcast_subtract_fusion.own_ref, bf16[2048,128]{1,0:T(8,128)(2,1)S(1)} %copy-done.6, ...), custom_call_target="tpu_custom_call" | custom-call | flops 4831838208 | bytes 3145728 | tf_op jit(solution)/shard_map/early/pallas_call | solution.py:241
  73.9 5.6 %late.3 = bf16[2048,256]{1,0:T(8,128)(2,1)} custom-call(s32[224]{0:T(256)S(1)} %select_n.62.lists_ref, f32[224]{0:T(256)S(1)} %reshape.76.flags_ref, s32[2]{0:T(128)S(1)} %collective-permute-done.glob_ref, s32[2]{0:T(128)S(1)} %broadcast_subtract_fusion.own_ref, bf16[2048,128]{1,0:T(8,128)(2,1)S(1)} %get-tuple-element.40.q_ref, ...), custom_call_target="tpu_custom_call", output_to_operand_aliasing={{}: (9, {})} | custom-call | flops 2147483648 | bytes 1048576 | tf_op jit(solution)/shard_map/late/pallas_call | solution.py:241
  (58 shorter events, 4.0 us)
Async XLA Ops:
  0.0 27.1 %collective-permute-start.1 = (bf16[2048,256]{1,0:T(8,128)(2,1)}, bf16[2048,256]{1,0:T(8,128)(2,1)S(1)}, u32[]{:S(2)}, u32[]{:S(2)}) collective-permute-start(bf16[2048,256]{1,0:T(8,128)(2,1)} %refs_0_.1), channel_id=1, source_target_pairs={{0,8},{8,0},{16,24},{24,16},{1,9},{9,1},{17,25},{25,17},{2,10},{10... | collective-permute-start | bytes 3145736 | tf_op jit(solution)/shard_map/ppermute | solution.py:261
  2.9 27.3 %collective-permute-start.2 = (bf16[2048,256]{1,0:T(8,128)(2,1)}, bf16[2048,256]{1,0:T(8,128)(2,1)S(1)}, u32[]{:S(2)}, u32[]{:S(2)}) collective-permute-start(bf16[2048,256]{1,0:T(8,128)(2,1)} %refs_3_.1), channel_id=1, source_target_pairs={{0,16},{8,24},{16,0},{24,8},{1,17},{9,25},{17,1},{25,9},{2,18},{10... | collective-permute-start | bytes 3145736 | tf_op jit(solution)/shard_map/ppermute | solution.py:261
  5.9 26.9 %collective-permute-start = (s32[2]{0:T(128)S(1)}, s32[2]{0:T(128)S(1)}, u32[]{:S(2)}, u32[]{:S(2)}) collective-permute-start(s32[2]{0:T(128)S(1)} %broadcast_subtract_fusion.own_ref), channel_id=1, source_target_pairs={{0,24},{8,16},{16,8},{24,0},{1,25},{9,17},{17,9},{25,1},{2,26},{10... | collective-permute-start | bytes 32 | tf_op jit(solution)/shard_map/ppermute | solution.py:261
  9.7 28.8 %collective-permute-start.3 = (bf16[2064,128]{1,0:T(8,128)(2,1)}, bf16[2064,128]{1,0:T(8,128)(2,1)}, u32[]{:S(2)}, u32[]{:S(2)}) collective-permute-start(bf16[2064,128]{1,0:T(8,128)(2,1)} %get-tuple-element.59), channel_id=1, source_target_pairs={{0,8},{8,0},{16,24},{24,16},{1,9},{9,1},{17,25},{25,17},{2,10},{10... | collective-permute-start | bytes 1585160 | tf_op jit(solution)/shard_map/ppermute | solution.py:261
  11.7 29.6 %collective-permute-start.4 = (bf16[2064,128]{1,0:T(8,128)(2,1)}, bf16[2064,128]{1,0:T(8,128)(2,1)}, u32[]{:S(2)}, u32[]{:S(2)}) collective-permute-start(bf16[2064,128]{1,0:T(8,128)(2,1)} %get-tuple-element.60), channel_id=1, source_target_pairs={{0,16},{8,24},{16,0},{24,8},{1,17},{9,25},{17,1},{25,9},{2,18},{10... | collective-permute-start | bytes 1585160 | tf_op jit(solution)/shard_map/ppermute | solution.py:261
  28.2 13.9 %copy-start = (bf16[2048,256]{1,0:T(8,128)(2,1)S(1)}, bf16[2048,256]{1,0:T(8,128)(2,1)}, u32[]{:S(2)}) copy-start(bf16[2048,256]{1,0:T(8,128)(2,1)} %refs_3_.1) | copy-start | bytes 3145732
  28.2 27.9 %collective-permute-start.5 = (bf16[2048,128]{1,0:T(8,128)(2,1)}, bf16[2048,128]{1,0:T(8,128)(2,1)}, u32[]{:S(2)}, u32[]{:S(2)}) collective-permute-start(bf16[2048,128]{1,0:T(8,128)(2,1)} %get-tuple-element.48), channel_id=1, source_target_pairs={{0,16},{8,24},{16,0},{24,8},{1,17},{9,25},{17,1},{25,9},{2,18},{10... | collective-permute-start | bytes 1572872 | tf_op jit(solution)/shard_map/ppermute | solution.py:261
  31.3 25.3 %collective-permute-start.6 = (bf16[2048,128]{1,0:T(8,128)(2,1)}, bf16[2048,128]{1,0:T(8,128)(2,1)}, u32[]{:S(2)}, u32[]{:S(2)}) collective-permute-start(bf16[2048,128]{1,0:T(8,128)(2,1)} %get-tuple-element.46), channel_id=1, source_target_pairs={{0,8},{8,0},{16,24},{24,16},{1,9},{9,1},{17,25},{25,17},{2,10},{10... | collective-permute-start | bytes 1572872 | tf_op jit(solution)/shard_map/ppermute | solution.py:261
  33.3 29.8 %collective-permute-start.7 = (bf16[2048,128]{1,0:T(8,128)(2,1)}, bf16[2048,128]{1,0:T(8,128)(2,1)}, u32[]{:S(2)}, u32[]{:S(2)}) collective-permute-start(bf16[2048,128]{1,0:T(8,128)(2,1)} %get-tuple-element.38.refs_0_), channel_id=1, source_target_pairs={{0,16},{8,24},{16,0},{24,8},{1,17},{9,25},{17,1},{25,9},{2,18},{10... | collective-permute-start | bytes 1572872 | tf_op jit(solution)/shard_map/ppermute | solution.py:261
  38.6 24.6 %collective-permute-start.8 = (bf16[2048,128]{1,0:T(8,128)(2,1)}, bf16[2048,128]{1,0:T(8,128)(2,1)}, u32[]{:S(2)}, u32[]{:S(2)}) collective-permute-start(bf16[2048,128]{1,0:T(8,128)(2,1)} %get-tuple-element.39.refs_3_), channel_id=1, source_target_pairs={{0,8},{8,0},{16,24},{24,16},{1,9},{9,1},{17,25},{25,17},{2,10},{10... | collective-permute-start | bytes 1572872 | tf_op jit(solution)/shard_map/ppermute | solution.py:261
  42.1 1.2 %copy-start.1 = (bf16[2048,256]{1,0:T(8,128)(2,1)S(1)}, bf16[2048,256]{1,0:T(8,128)(2,1)}, u32[]{:S(2)}) copy-start(bf16[2048,256]{1,0:T(8,128)(2,1)} %refs_0_.1) | copy-start | bytes 3145732
  43.3 1.2 %copy-start.4 = (bf16[2048,256]{1,0:T(8,128)(2,1)S(1)}, bf16[2048,256]{1,0:T(8,128)(2,1)}, u32[]{:S(2)}) copy-start(bf16[2048,256]{1,0:T(8,128)(2,1)} %q_ref.1) | copy-start | bytes 3145732
  54.5 7.8 %copy-start.5 = (bf16[2048,128]{1,0:T(8,128)(2,1)}, bf16[2048,128]{1,0:T(8,128)(2,1)S(1)}, u32[]{:S(2)}) copy-start(bf16[2048,128]{1,0:T(8,128)(2,1)S(1)} %get-tuple-element.37.q_ref) | copy-start | bytes 1572868
  54.5 8.6 %copy-start.2 = (bf16[2048,128]{1,0:T(8,128)(2,1)S(1)}, bf16[2048,128]{1,0:T(8,128)(2,1)}, u32[]{:S(2)}) copy-start(bf16[2048,128]{1,0:T(8,128)(2,1)} %get-tuple-element.39.refs_3_) | copy-start | bytes 1572868
  54.5 8.6 %copy-start.3 = (bf16[2048,128]{1,0:T(8,128)(2,1)S(1)}, bf16[2048,128]{1,0:T(8,128)(2,1)}, u32[]{:S(2)}) copy-start(bf16[2048,128]{1,0:T(8,128)(2,1)} %get-tuple-element.38.refs_0_) | copy-start | bytes 1572868
  54.5 19.4 %collective-permute-start.9 = (bf16[2048,128]{1,0:T(8,128)(2,1)}, bf16[2048,128]{1,0:T(8,128)(2,1)}, u32[]{:S(2)}, u32[]{:S(2)}) collective-permute-start(bf16[2048,128]{1,0:T(8,128)(2,1)} %get-tuple-element.41), channel_id=1, source_target_pairs={{0,16},{8,24},{16,0},{24,8},{1,17},{9,25},{17,1},{25,9},{2,18},{10... | collective-permute-start | bytes 1572872 | tf_op jit(solution)/shard_map/ppermute | solution.py:261
  56.1 17.8 %collective-permute-start.10 = (bf16[2048,128]{1,0:T(8,128)(2,1)}, bf16[2048,128]{1,0:T(8,128)(2,1)}, u32[]{:S(2)}, u32[]{:S(2)}) collective-permute-start(bf16[2048,128]{1,0:T(8,128)(2,1)} %get-tuple-element.42), channel_id=1, source_target_pairs={{0,8},{8,0},{16,24},{24,16},{1,9},{9,1},{17,25},{25,17},{2,10},{10... | collective-permute-start | bytes 1572872 | tf_op jit(solution)/shard_map/ppermute | solution.py:261
  63.2 1.0 %copy-start.6 = (bf16[2048,128]{1,0:T(8,128)(2,1)S(1)}, bf16[2048,128]{1,0:T(8,128)(2,1)}, u32[]{:S(2)}) copy-start(bf16[2048,128]{1,0:T(8,128)(2,1)} %copy-done.5) | copy-start | bytes 1572868

commit v11 on v10

--- a/solution.py
+++ b/solution.py
@@ -17,7 +17,7 @@
 TOGETHER = 8
 CHUNK = 2048
 SUBS = 2
-VMEM_BYTES = 16 * 1024 * 1024
+VMEM_BYTES = 8 * 1024 * 1024
 EXP2_SCALE = 0.125 * 1.4426950408889634
 
 

time: 80 us -> 80 us (level)
  no operation moved by 1% of the time
where the time goes in v11:
time: 80 us; the launch traced here: 79.6 us
  Pallas kernels  30.9 us (39%)
  waiting for transfers between devices  18.5 us (23%)
  starting transfers between devices  16.3 us (20%)
  local copies, waits for them, and re-layouts  9.57 us (12%)
  other arithmetic  4.01 us (5%)
    pallas_call x4, Pallas kernels, part_call(): pl.pallas_call(functools.partial(part_kernel, pair, kind, wide, gpd, toke...  30.9 us
    ppermute x11, waiting for transfers between devices, exchange(): return lax.ppermute(array, 'seq', [(i, i ^ step) for i in range(count)])  18.5 us
    ppermute x11, starting transfers between devices, exchange(): return lax.ppermute(array, 'seq', [(i, i ^ step) for i in range(count)])  16.3 us
    slice x2, local copies, waits for them, and re-layouts, shards(): v_parts = {0: v_held[:, lanes], back[0]: v_first[:, lanes]}  3.73 us
    unnamed x14, local copies, waits for them, and re-layouts  3.5 us
  transfers between devices with their start and end apart: 11, of which 3 were waited for; matrix products, arithmetic and copies ran while one was open for 13% of the time, Pallas kernels for 32%

profile of v11, /device:TPU:0, one launch (start us, length us, event | category | flops | bytes accessed | tf_op | source)
XLA Modules:
  0.0 79.6 jit_solution(15849927350538471015)
XLA Ops:
  0.0 2.9 %collective-permute-start.1 = (bf16[2048,256]{1,0:T(8,128)(2,1)}, bf16[2048,256]{1,0:T(8,128)(2,1)S(1)}, u32[]{:S(2)}, u32[]{:S(2)}) collective-permute-start(bf16[2048,256]{1,0:T(8,128)(2,1)} %refs_0_.1), channel_id=1, source_target_pairs={{0,8},{8,0},{16,24},{24,16},{1,9},{9,1},{17,25},{25,17},{2,10},{10... | collective-permute-start | bytes 3145736 | tf_op jit(solution)/shard_map/ppermute | solution.py:261
  2.9 1.5 %collective-permute-start.2 = (bf16[2048,256]{1,0:T(8,128)(2,1)}, bf16[2048,256]{1,0:T(8,128)(2,1)S(1)}, u32[]{:S(2)}, u32[]{:S(2)}) collective-permute-start(bf16[2048,256]{1,0:T(8,128)(2,1)} %refs_3_.1), channel_id=1, source_target_pairs={{0,16},{8,24},{16,0},{24,8},{1,17},{9,25},{17,1},{25,9},{2,18},{10... | collective-permute-start | bytes 3145736 | tf_op jit(solution)/shard_map/ppermute | solution.py:261
  5.1 0.7 fusion.5
  6.0 2.7 %fusion.22 = (bf16[2048,128]{1,0:T(8,128)(2,1)}, bf16[2048,128]{1,0:T(8,128)(2,1)S(1)}, bf16[2048,128]{1,0:T(8,128)(2,1)S(1)}, bf16[2048,128]{1,0:T(8,128)(2,1)}) fusion(bf16[2048,256]{1,0:T(8,128)(2,1)} %refs_3_.1, bf16[2048,256]{1,0:T(8,128)(2,1)} %refs_0_.1), kind=kLoop, calls=%fused_computation.59 | loop fusion | bytes 4194304 | tf_op jit(solution)/shard_map/slice | solution.py:308
  8.7 1.0 %fusion.2 = (bf16[2064,128]{1,0:T(8,128)(2,1)}, bf16[2064,128]{1,0:T(8,128)(2,1)}) fusion(bf16[1,2]{1,0:T(2,128)(2,1)S(1)} %convert_bitcast_fusion, bf16[2048,128]{1,0:T(8,128)(2,1)S(1)} %get-tuple-element.50, bf16[2048,128]{1,0:T(8,128)(2,1)S(1)} %get-tuple-element.61), kind=kLoop, calls=%fused_computation.3 | loop fusion | flops 2377728 | bytes 2105348 | tf_op jit(solution)/shard_map/concatenate | solution.py:311
  9.7 1.9 %collective-permute-start.3 = (bf16[2064,128]{1,0:T(8,128)(2,1)}, bf16[2064,128]{1,0:T(8,128)(2,1)}, u32[]{:S(2)}, u32[]{:S(2)}) collective-permute-start(bf16[2064,128]{1,0:T(8,128)(2,1)} %get-tuple-element.59), channel_id=1, source_target_pairs={{0,8},{8,0},{16,24},{24,16},{1,9},{9,1},{17,25},{25,17},{2,10},{10... | collective-permute-start | bytes 1585160 | tf_op jit(solution)/shard_map/ppermute | solution.py:261
  11.7 1.5 %collective-permute-start.4 = (bf16[2064,128]{1,0:T(8,128)(2,1)}, bf16[2064,128]{1,0:T(8,128)(2,1)}, u32[]{:S(2)}, u32[]{:S(2)}) collective-permute-start(bf16[2064,128]{1,0:T(8,128)(2,1)} %get-tuple-element.60), channel_id=1, source_target_pairs={{0,16},{8,24},{16,0},{24,8},{1,17},{9,25},{17,1},{25,9},{2,18},{10... | collective-permute-start | bytes 1585160 | tf_op jit(solution)/shard_map/ppermute | solution.py:261
  14.0 13.1 %collective-permute-done.1.refs_1_ = bf16[2048,256]{1,0:T(8,128)(2,1)S(1)} collective-permute-done((bf16[2048,256]{1,0:T(8,128)(2,1)}, bf16[2048,256]{1,0:T(8,128)(2,1)S(1)}, u32[]{:S(2)}, u32[]{:S(2)}) %collective-permute-start.1) | collective-permute-done | bytes 1048608 | tf_op jit(solution)/shard_map/ppermute | solution.py:261
  27.1 1.1 %fusion.21 = (bf16[2048,128]{1,0:T(8,128)(2,1)}, bf16[2048,128]{1,0:T(8,128)(2,1)}) fusion(bf16[2048,256]{1,0:T(8,128)(2,1)S(1)} %collective-permute-done.1.refs_1_), kind=kLoop, calls=%fused_computation.58 | loop fusion | bytes 2097152 | tf_op jit(solution)/shard_map/slice | solution.py:307
  28.2 2.1 %collective-permute-start.5 = (bf16[2048,128]{1,0:T(8,128)(2,1)}, bf16[2048,128]{1,0:T(8,128)(2,1)}, u32[]{:S(2)}, u32[]{:S(2)}) collective-permute-start(bf16[2048,128]{1,0:T(8,128)(2,1)} %get-tuple-element.48), channel_id=1, source_target_pairs={{0,16},{8,24},{16,0},{24,8},{1,17},{9,25},{17,1},{25,9},{2,18},{10... | collective-permute-start | bytes 1572872 | tf_op jit(solution)/shard_map/ppermute | solution.py:261
  30.3 1.1 %fusion.20 = (bf16[2048,128]{1,0:T(8,128)(2,1)}, bf16[2048,128]{1,0:T(8,128)(2,1)}) fusion(bf16[2048,256]{1,0:T(8,128)(2,1)S(1)} %collective-permute-done.2.refs_5_), kind=kLoop, calls=%fused_computation.57 | loop fusion | bytes 2097152 | tf_op jit(solution)/shard_map/slice | solution.py:308
  31.3 1.5 %collective-permute-start.6 = (bf16[2048,128]{1,0:T(8,128)(2,1)}, bf16[2048,128]{1,0:T(8,128)(2,1)}, u32[]{:S(2)}, u32[]{:S(2)}) collective-permute-start(bf16[2048,128]{1,0:T(8,128)(2,1)} %get-tuple-element.46), channel_id=1, source_target_pairs={{0,8},{8,0},{16,24},{24,16},{1,9},{9,1},{17,25},{25,17},{2,10},{10... | collective-permute-start | bytes 1572872 | tf_op jit(solution)/shard_map/ppermute | solution.py:261
  33.9 4.7 %collective-permute-done.3.refs_4_ = bf16[2064,128]{1,0:T(8,128)(2,1)} collective-permute-done((bf16[2064,128]{1,0:T(8,128)(2,1)}, bf16[2064,128]{1,0:T(8,128)(2,1)}, u32[]{:S(2)}, u32[]{:S(2)}) %collective-permute-start.3) | collective-permute-done | bytes 528416 | tf_op jit(solution)/shard_map/ppermute | solution.py:261
  38.6 2.1 %collective-permute-start.8 = (bf16[2048,128]{1,0:T(8,128)(2,1)}, bf16[2048,128]{1,0:T(8,128)(2,1)}, u32[]{:S(2)}, u32[]{:S(2)}) collective-permute-start(bf16[2048,128]{1,0:T(8,128)(2,1)} %get-tuple-element.39.refs_3_), channel_id=1, source_target_pairs={{0,8},{8,0},{16,24},{24,16},{1,9},{9,1},{17,25},{25,17},{2,10},{10... | collective-permute-start | bytes 1572872 | tf_op jit(solution)/shard_map/ppermute | solution.py:261
  40.6 0.7 add_bitcast_fusion.1
  41.3 0.7 add_bitcast_fusion
  42.1 1.2 %copy-done.1 = bf16[2048,256]{1,0:T(8,128)(2,1)S(1)} copy-done((bf16[2048,256]{1,0:T(8,128)(2,1)S(1)}, bf16[2048,256]{1,0:T(8,128)(2,1)}, u32[]{:S(2)}) %copy-start.1) | copy-done | bytes 1048600
  43.3 1.2 %copy-done.4 = bf16[2048,256]{1,0:T(8,128)(2,1)S(1)} copy-done((bf16[2048,256]{1,0:T(8,128)(2,1)S(1)}, bf16[2048,256]{1,0:T(8,128)(2,1)}, u32[]{:S(2)}) %copy-start.4) | copy-done | bytes 1048600
  44.5 10.0 %early.2 = (f32[2176,128]{1,0:T(8,128)S(1)}, f32[2176,128]{1,0:T(8,128)S(1)}, bf16[2048,128]{1,0:T(8,128)(2,1)S(1)}, bf16[2048,128]{1,0:T(8,128)(2,1)S(1)}) custom-call(s32[288]{0:T(512)S(1)} %fusion.17.lists_ref, f32[288]{0:T(512)S(1)} %fusion.16.flags_ref, s32[6]{0:T(128)S(1)} %pad_add_fusion.4.glob_ref, s32[2]{0:T(128)S(1)} %broadcast_subtract_fusion.own_ref, ...), custom_call_target="tpu_custom_call" | custom-call | flops 4831838208 | bytes 3145728 | tf_op jit(solution)/shard_map/early/pallas_call | solution.py:241
  54.5 1.6 %collective-permute-start.9 = (bf16[2048,128]{1,0:T(8,128)(2,1)}, bf16[2048,128]{1,0:T(8,128)(2,1)}, u32[]{:S(2)}, u32[]{:S(2)}) collective-permute-start(bf16[2048,128]{1,0:T(8,128)(2,1)} %get-tuple-element.41), channel_id=1, source_target_pairs={{0,16},{8,24},{16,0},{24,8},{1,17},{9,25},{17,1},{25,9},{2,18},{10... | collective-permute-start | bytes 1572872 | tf_op jit(solution)/shard_map/ppermute | solution.py:261
  56.6 5.7 %late.2.refs_4_ = bf16[2048,256]{1,0:T(8,128)(2,1)} custom-call(s32[224]{0:T(256)S(1)} %select_n.64.lists_ref, f32[224]{0:T(256)S(1)} %reshape.77.flags_ref, s32[2]{0:T(128)S(1)} %collective-permute-done.glob_ref, s32[2]{0:T(128)S(1)} %broadcast_subtract_fusion.own_ref, bf16[2048,128]{1,0:T(8,128)(2,1)S(1)} %get-tuple-element.33.q_ref, ...), custom_call_target="tpu_custom_call" | custom-call | flops 2147483648 | bytes 1048576 | tf_op jit(solution)/shard_map/late/pallas_call | solution.py:241
  63.2 1.0 %copy-done.6 = bf16[2048,128]{1,0:T(8,128)(2,1)S(1)} copy-done((bf16[2048,128]{1,0:T(8,128)(2,1)S(1)}, bf16[2048,128]{1,0:T(8,128)(2,1)}, u32[]{:S(2)}) %copy-start.6) | copy-done | bytes 524312
  64.2 9.7 %early.3 = (f32[2176,128]{1,0:T(8,128)S(1)}, f32[2176,128]{1,0:T(8,128)S(1)}, bf16[2048,128]{1,0:T(8,128)(2,1)S(1)}) custom-call(s32[288]{0:T(512)S(1)} %fusion.19.lists_ref, f32[288]{0:T(512)S(1)} %fusion.18.flags_ref, s32[6]{0:T(128)S(1)} %pad_add_fusion.4.glob_ref, s32[2]{0:T(128)S(1)} %broadcast_subtract_fusion.own_ref, bf16[2048,128]{1,0:T(8,128)(2,1)S(1)} %copy-done.6, ...), custom_call_target="tpu_custom_call" | custom-call | flops 4831838208 | bytes 3145728 | tf_op jit(solution)/shard_map/early/pallas_call | solution.py:241
  73.9 5.6 %late.3 = bf16[2048,256]{1,0:T(8,128)(2,1)} custom-call(s32[224]{0:T(256)S(1)} %select_n.62.lists_ref, f32[224]{0:T(256)S(1)} %reshape.76.flags_ref, s32[2]{0:T(128)S(1)} %collective-permute-done.glob_ref, s32[2]{0:T(128)S(1)} %broadcast_subtract_fusion.own_ref, bf16[2048,128]{1,0:T(8,128)(2,1)S(1)} %get-tuple-element.40.q_ref, ...), custom_call_target="tpu_custom_call", output_to_operand_aliasing={{}: (9, {})} | custom-call | flops 2147483648 | bytes 1048576 | tf_op jit(solution)/shard_map/late/pallas_call | solution.py:241
  (58 shorter events, 4.0 us)
Async XLA Ops:
  0.0 27.1 %collective-permute-start.1 = (bf16[2048,256]{1,0:T(8,128)(2,1)}, bf16[2048,256]{1,0:T(8,128)(2,1)S(1)}, u32[]{:S(2)}, u32[]{:S(2)}) collective-permute-start(bf16[2048,256]{1,0:T(8,128)(2,1)} %refs_0_.1), channel_id=1, source_target_pairs={{0,8},{8,0},{16,24},{24,16},{1,9},{9,1},{17,25},{25,17},{2,10},{10... | collective-permute-start | bytes 3145736 | tf_op jit(solution)/shard_map/ppermute | solution.py:261
  2.9 27.3 %collective-permute-start.2 = (bf16[2048,256]{1,0:T(8,128)(2,1)}, bf16[2048,256]{1,0:T(8,128)(2,1)S(1)}, u32[]{:S(2)}, u32[]{:S(2)}) collective-permute-start(bf16[2048,256]{1,0:T(8,128)(2,1)} %refs_3_.1), channel_id=1, source_target_pairs={{0,16},{8,24},{16,0},{24,8},{1,17},{9,25},{17,1},{25,9},{2,18},{10... | collective-permute-start | bytes 3145736 | tf_op jit(solution)/shard_map/ppermute | solution.py:261
  5.9 26.9 %collective-permute-start = (s32[2]{0:T(128)S(1)}, s32[2]{0:T(128)S(1)}, u32[]{:S(2)}, u32[]{:S(2)}) collective-permute-start(s32[2]{0:T(128)S(1)} %broadcast_subtract_fusion.own_ref), channel_id=1, source_target_pairs={{0,24},{8,16},{16,8},{24,0},{1,25},{9,17},{17,9},{25,1},{2,26},{10... | collective-permute-start | bytes 32 | tf_op jit(solution)/shard_map/ppermute | solution.py:261
  9.7 28.8 %collective-permute-start.3 = (bf16[2064,128]{1,0:T(8,128)(2,1)}, bf16[2064,128]{1,0:T(8,128)(2,1)}, u32[]{:S(2)}, u32[]{:S(2)}) collective-permute-start(bf16[2064,128]{1,0:T(8,128)(2,1)} %get-tuple-element.59), channel_id=1, source_target_pairs={{0,8},{8,0},{16,24},{24,16},{1,9},{9,1},{17,25},{25,17},{2,10},{10... | collective-permute-start | bytes 1585160 | tf_op jit(solution)/shard_map/ppermute | solution.py:261
  11.7 29.6 %collective-permute-start.4 = (bf16[2064,128]{1,0:T(8,128)(2,1)}, bf16[2064,128]{1,0:T(8,128)(2,1)}, u32[]{:S(2)}, u32[]{:S(2)}) collective-permute-start(bf16[2064,128]{1,0:T(8,128)(2,1)} %get-tuple-element.60), channel_id=1, source_target_pairs={{0,16},{8,24},{16,0},{24,8},{1,17},{9,25},{17,1},{25,9},{2,18},{10... | collective-permute-start | bytes 1585160 | tf_op jit(solution)/shard_map/ppermute | solution.py:261
  28.2 13.9 %copy-start = (bf16[2048,256]{1,0:T(8,128)(2,1)S(1)}, bf16[2048,256]{1,0:T(8,128)(2,1)}, u32[]{:S(2)}) copy-start(bf16[2048,256]{1,0:T(8,128)(2,1)} %refs_3_.1) | copy-start | bytes 3145732
  28.2 27.9 %collective-permute-start.5 = (bf16[2048,128]{1,0:T(8,128)(2,1)}, bf16[2048,128]{1,0:T(8,128)(2,1)}, u32[]{:S(2)}, u32[]{:S(2)}) collective-permute-start(bf16[2048,128]{1,0:T(8,128)(2,1)} %get-tuple-element.48), channel_id=1, source_target_pairs={{0,16},{8,24},{16,0},{24,8},{1,17},{9,25},{17,1},{25,9},{2,18},{10... | collective-permute-start | bytes 1572872 | tf_op jit(solution)/shard_map/ppermute | solution.py:261
  31.3 25.3 %collective-permute-start.6 = (bf16[2048,128]{1,0:T(8,128)(2,1)}, bf16[2048,128]{1,0:T(8,128)(2,1)}, u32[]{:S(2)}, u32[]{:S(2)}) collective-permute-start(bf16[2048,128]{1,0:T(8,128)(2,1)} %get-tuple-element.46), channel_id=1, source_target_pairs={{0,8},{8,0},{16,24},{24,16},{1,9},{9,1},{17,25},{25,17},{2,10},{10... | collective-permute-start | bytes 1572872 | tf_op jit(solution)/shard_map/ppermute | solution.py:261
  33.3 29.8 %collective-permute-start.7 = (bf16[2048,128]{1,0:T(8,128)(2,1)}, bf16[2048,128]{1,0:T(8,128)(2,1)}, u32[]{:S(2)}, u32[]{:S(2)}) collective-permute-start(bf16[2048,128]{1,0:T(8,128)(2,1)} %get-tuple-element.38.refs_0_), channel_id=1, source_target_pairs={{0,16},{8,24},{16,0},{24,8},{1,17},{9,25},{17,1},{25,9},{2,18},{10... | collective-permute-start | bytes 1572872 | tf_op jit(solution)/shard_map/ppermute | solution.py:261
  38.6 24.6 %collective-permute-start.8 = (bf16[2048,128]{1,0:T(8,128)(2,1)}, bf16[2048,128]{1,0:T(8,128)(2,1)}, u32[]{:S(2)}, u32[]{:S(2)}) collective-permute-start(bf16[2048,128]{1,0:T(8,128)(2,1)} %get-tuple-element.39.refs_3_), channel_id=1, source_target_pairs={{0,8},{8,0},{16,24},{24,16},{1,9},{9,1},{17,25},{25,17},{2,10},{10... | collective-permute-start | bytes 1572872 | tf_op jit(solution)/shard_map/ppermute | solution.py:261
  42.1 1.2 %copy-start.1 = (bf16[2048,256]{1,0:T(8,128)(2,1)S(1)}, bf16[2048,256]{1,0:T(8,128)(2,1)}, u32[]{:S(2)}) copy-start(bf16[2048,256]{1,0:T(8,128)(2,1)} %refs_0_.1) | copy-start | bytes 3145732
  43.3 1.2 %copy-start.4 = (bf16[2048,256]{1,0:T(8,128)(2,1)S(1)}, bf16[2048,256]{1,0:T(8,128)(2,1)}, u32[]{:S(2)}) copy-start(bf16[2048,256]{1,0:T(8,128)(2,1)} %q_ref.1) | copy-start | bytes 3145732
  54.5 7.8 %copy-start.5 = (bf16[2048,128]{1,0:T(8,128)(2,1)}, bf16[2048,128]{1,0:T(8,128)(2,1)S(1)}, u32[]{:S(2)}) copy-start(bf16[2048,128]{1,0:T(8,128)(2,1)S(1)} %get-tuple-element.37.q_ref) | copy-start | bytes 1572868
  54.5 8.6 %copy-start.2 = (bf16[2048,128]{1,0:T(8,128)(2,1)S(1)}, bf16[2048,128]{1,0:T(8,128)(2,1)}, u32[]{:S(2)}) copy-start(bf16[2048,128]{1,0:T(8,128)(2,1)} %get-tuple-element.39.refs_3_) | copy-start | bytes 1572868
  54.5 8.6 %copy-start.3 = (bf16[2048,128]{1,0:T(8,128)(2,1)S(1)}, bf16[2048,128]{1,0:T(8,128)(2,1)}, u32[]{:S(2)}) copy-start(bf16[2048,128]{1,0:T(8,128)(2,1)} %get-tuple-element.38.refs_0_) | copy-start | bytes 1572868
  54.5 19.4 %collective-permute-start.9 = (bf16[2048,128]{1,0:T(8,128)(2,1)}, bf16[2048,128]{1,0:T(8,128)(2,1)}, u32[]{:S(2)}, u32[]{:S(2)}) collective-permute-start(bf16[2048,128]{1,0:T(8,128)(2,1)} %get-tuple-element.41), channel_id=1, source_target_pairs={{0,16},{8,24},{16,0},{24,8},{1,17},{9,25},{17,1},{25,9},{2,18},{10... | collective-permute-start | bytes 1572872 | tf_op jit(solution)/shard_map/ppermute | solution.py:261
  56.1 17.8 %collective-permute-start.10 = (bf16[2048,128]{1,0:T(8,128)(2,1)}, bf16[2048,128]{1,0:T(8,128)(2,1)}, u32[]{:S(2)}, u32[]{:S(2)}) collective-permute-start(bf16[2048,128]{1,0:T(8,128)(2,1)} %get-tuple-element.42), channel_id=1, source_target_pairs={{0,8},{8,0},{16,24},{24,16},{1,9},{9,1},{17,25},{25,17},{2,10},{10... | collective-permute-start | bytes 1572872 | tf_op jit(solution)/shard_map/ppermute | solution.py:261
  63.2 1.0 %copy-start.6 = (bf16[2048,128]{1,0:T(8,128)(2,1)S(1)}, bf16[2048,128]{1,0:T(8,128)(2,1)}, u32[]{:S(2)}) copy-start(bf16[2048,128]{1,0:T(8,128)(2,1)} %copy-done.5) | copy-start | bytes 1572868
